TPU v7x, 32 devices: a whole 2x2x4 slice. The times are simulated.
32 devices in a mesh: seq: 4 (over y, core), users: 8 (over z, x).
Axes of the slice: x: 2, y: 2, z: 4, core: 2. Of those that a mesh axis runs over, the one named last changes fastest.
Arguments:
- hidden: float32 [8, 4096, 512], P('users', 'seq'), may hold values from -256 to 256
- target: bfloat16 [8, 4096, 512], P('users', 'seq'), may hold values from -0.25 to 0.25
- pool_table: bfloat16 [8192, 512], P('users'), may hold values from -1 to 1
- pool_items: int32 [8192], P('users'), may hold values from 1 to 16383
- labels: int32 [8, 4096], P('users', 'seq'), may hold values from 1 to 16383
- chosen: int32 [8, 32, 8], P('users', 'seq'), may hold values from 0 to 31, all different within a row
- offsets: int32 [8, 5], P('users'), may hold values from 0 to 4096, as said below
Outputs:
- loss: float32 [], replicated
- grad_hidden: float32 [8, 4096, 512], P('users', 'seq')
- grad_table: float32 [8192, 512], P('users')
Inputs may be any that keep to these rules, and one draw needn't show every extreme that they name: Each row offsets[u] starts at 0 and rises strictly; its last entry is the number of live positions of group u, and equals 4096 in some group; positions from it on are padding. `chosen`: each position block names 8 different negative blocks.
All inputs are finite; a program needn't handle non-finite values.
Results may differ from a plain program's by a relative error of at most 0.003.
Values may be sent and summed in bfloat16 or wider, within the bound.
No kernel may reach another device: no remote copies, remote signals or barrier semaphores. Data moves between devices by JAX's collectives and lax.ppermute only.
A program may use at most 192 MiB of HBM per device.

v0:
```python
import jax
import jax.numpy as jnp
from jax import lax
from jax.sharding import PartitionSpec as P

NB = 256
PB = 128


def history_weights(bounds, positions):
    starts = bounds[:-1]
    finish = bounds[1:]
    lengths = (finish - starts).astype(jnp.float32)
    inside = (positions[..., None] >= starts) & (positions[..., None] < finish)
    return jnp.sum(jnp.where(inside, 1.0 / lengths, 0.0), axis=-1)


def block_terms(states, target, labels, weights, chosen, pool_rows, pool_ids, factor):
    narrow = states.astype(jnp.bfloat16)
    negatives = jnp.take(pool_rows, chosen, axis=0).reshape(-1, pool_rows.shape[2])
    neg_items = jnp.take(pool_ids, chosen, axis=0).reshape(-1)
    scores = jnp.dot(narrow, negatives.T, preferred_element_type=jnp.float32)
    target_wide = target.astype(jnp.float32)
    positive = jnp.sum(narrow.astype(jnp.float32) * target_wide, axis=1)
    masked = jnp.where(neg_items[None, :] == labels[:, None], -1e30, scores)
    peak = jnp.maximum(positive, jnp.max(masked, axis=1))
    neg_exp = jnp.exp(masked - peak[:, None])
    pos_exp = jnp.exp(positive - peak)
    totals = pos_exp + jnp.sum(neg_exp, axis=1)
    cross = peak + jnp.log(totals) - positive
    coeff = weights * factor
    neg_grad = (coeff[:, None] * neg_exp / totals[:, None]).astype(jnp.bfloat16)
    pos_grad = coeff * (pos_exp / totals - 1.0)
    state_grad = (
        jnp.dot(neg_grad, negatives, preferred_element_type=jnp.float32)
        + pos_grad[:, None] * target_wide
    )
    pool_grad = jnp.dot(neg_grad.T, narrow, preferred_element_type=jnp.float32)
    pool_grad = pool_grad.reshape(chosen.shape[0], pool_rows.shape[1], pool_rows.shape[2])
    return (jnp.sum(weights * cross), state_grad, pool_grad)


def run_blocks(
    states,
    targets,
    label_rows,
    weights,
    picked,
    visit_order,
    live_count,
    pool_rows,
    pool_ids,
    factor,
):
    batched = jax.vmap(block_terms, in_axes=(0, 0, 0, 0, 0, None, None, None))
    rounds = (live_count + 3) // 4

    def advance(turn_index, carried):
        loss_acc, grad_acc, state_acc = carried
        slot_picks = lax.dynamic_slice_in_dim(visit_order, turn_index * 4, 4)
        picked_now = jnp.take(picked, slot_picks, axis=0)
        part_loss, state_grad, pool_grad = batched(
            jnp.take(states, slot_picks, axis=0),
            jnp.take(targets, slot_picks, axis=0),
            jnp.take(label_rows, slot_picks, axis=0),
            jnp.take(weights, slot_picks, axis=0),
            picked_now,
            pool_rows,
            pool_ids,
            factor,
        )
        grad_acc = grad_acc.at[picked_now.reshape(-1)].add(
            pool_grad.reshape((-1,) + pool_grad.shape[2:])
        )
        state_acc = state_acc.at[slot_picks].set(state_grad)
        return (loss_acc + jnp.sum(part_loss), grad_acc, state_acc)

    initial = (
        jnp.zeros((), jnp.float32),
        jnp.zeros(pool_rows.shape, jnp.float32),
        jnp.zeros(states.shape, jnp.float32),
    )
    return lax.fori_loop(0, rounds, advance, initial)


def per_device(hidden, target, pool_table, pool_items, labels, chosen, offsets):
    user_count = lax.axis_size("users")
    length = hidden.shape[1]
    features = hidden.shape[2]
    block_count = length // PB
    shard_rows, shard_items = (
        lax.all_gather(pool_table, "users", axis=0, tiled=True),
        lax.all_gather(pool_items, "users", axis=0, tiled=True),
    )
    pool_rows = shard_rows.reshape(-1, NB, features)
    pool_ids = shard_items.reshape(-1, NB)
    factor = 1.0 / (user_count * (offsets.shape[1] - 1))
    seq_place = lax.axis_index("seq")
    live_blocks = (offsets[0, -1] + PB - 1) // PB
    states = hidden.reshape(block_count, PB, features)
    targets = target.reshape(block_count, PB, features)
    label_rows = labels.reshape(block_count, PB)
    picked = chosen.reshape(block_count, chosen.shape[2])
    within = jnp.arange(PB, dtype=jnp.int32)
    slot_index = jnp.arange(block_count, dtype=jnp.int32)
    positions = seq_place * length + slot_index[:, None] * PB + within[None, :]
    weights = history_weights(offsets[0], positions)
    live_count = jnp.clip(live_blocks - seq_place * block_count, 0, block_count)
    loss_part, grad_pool, state_grad = run_blocks(
        states,
        targets,
        label_rows,
        weights,
        picked,
        slot_index,
        live_count,
        pool_rows,
        pool_ids,
        factor,
    )
    grad_hidden = state_grad.reshape(hidden.shape)
    loss_total = lax.psum(loss_part, ("seq", "users")) * factor
    grad_full = grad_pool.reshape(-1, features)
    owned_rows = lax.psum_scatter(grad_full, "users", scatter_dimension=0, tiled=True)
    grad_table = lax.psum(owned_rows, "seq")
    return (loss_total, grad_hidden, grad_table)


def solution(mesh):
    return jax.shard_map(
        per_device,
        mesh=mesh,
        in_specs=(
            P("users", "seq", None),
            P("users", "seq", None),
            P("users", None),
            P("users"),
            P("users", "seq"),
            P("users", "seq", None),
            P("users", None),
        ),
        out_specs=(P(), P("users", "seq", None), P("users", None)),
        check_vma=False,
    )
```

profile of v0, /device:TPU:0, one launch (start us, length us, event | category | flops | bytes accessed | tf_op | source)
XLA Modules:
  0.0 656.4 jit_solution(10172165664551695535)
XLA Ops:
  7.2 0.7 all-gather.2.cloned.1.call-update
  8.0 1.2 slice.11
  9.9 32.7 %all_gather.6 = s32[8192]{0:T(1024)S(1)} all-gather(s32[1024]{0:T(1024)} %param.12), channel_id=1, replica_groups=mesh['seq'=4,'users'=8] {'users'}, dimensions={0}, use_global_device_ids=true | all-gather | bytes 36864 | tf_op jit(solution)/shard_map/all_gather | solution.py:93
  42.6 1.7 convert.11
  44.4 0.1 convert_divide_fusion
  44.6 0.1 select_reduce_fusion
  44.7 93.3 %all-gather.2.cloned.1.call-done = bf16[8192,512]{1,0:T(8,128)(2,1)} async-done(((bf16[1024,512]{1,0:T(8,128)(2,1)}), bf16[8192,512]{1,0:T(8,128)(2,1)}) %all-gather.2.cloned.1.call-update) | async-done | bytes 8388624 | tf_op jit(solution)/shard_map/all_gather | solution.py:92
  138.0 1.6 broadcast_in_dim.127
  139.6 7.9 %broadcast_in_dim.126 = f32[32,256,512]{2,1,0:T(8,128)} broadcast(f32[]{:T(128)} %copy.33), dimensions={} | broadcast | bytes 16777220 | tf_op jit(solution)/shard_map/broadcast_in_dim | solution.py:80
  147.4 163.9 %while.16 = (s32[]{:T(128)}, f32[]{:T(128)}, f32[32,256,512]{2,1,0:T(8,128)}, f32[8,128,512]{2,1,0:T(8,128)}, s32[]{:T(128)}, /*index=5*/s32[8]{0:T(128)S(1)}, f...) while((s32[]{:T(128)}, f32[]{:T(128)}, ...), condition=%wide.region_8.9_spmd, body=%wide.region_1.8_spmd.sunk | while | flops 3252174336 | bytes 194429456 | solution.py:83
  147.4 0.1 compare_and_fusion.4
  147.5 0.6 gather_fusion.3
  148.1 0.1 compare_select_fusion.7
  148.1 0.1 reshape.401
  148.2 0.1 compare_and_fusion.5
  148.3 0.1 select_n.249
  148.4 0.6 gather_fusion.6
  149.0 0.6 gather_fusion.2
  149.5 0.1 broadcast_select_fusion.7
  149.6 0.1 broadcast_bitcast_fusion.2
  149.7 0.6 gather_fusion.4
  150.3 1.8 gather_fusion
  152.2 0.6 gather_fusion.1
  152.8 0.4 fusion.23
  153.1 8.4 %gather_fusion.5 = bf16[32,256,512]{2,1,0:T(8,128)(2,1)} fusion(bf16[32,256,512]{2,1,0:T(8,128)(2,1)} %get-tuple-element.362, s32[1024]{0:T(1024)S(1)} %pad_clamp_fusion.5), kind=kCustom, calls=%fused_computation.6.clone.1 | custom fusion | bytes 16777344 | tf_op jit(solution)/shard_map/while/body/vmap(jit(_take))/gather | solution.py:20
  161.5 4.7 bitcast_select_fusion.3
  166.2 2.9 fusion.24
  169.0 0.4 copy-done.1
  169.4 1.9 copy-done
  171.3 1.0 fusion.25
  172.3 0.7 add_multiply_fusion.2
  173.5 6.5 convolution_add_fusion.2
  180.0 2.8 scatter_fusion.1
  182.7 10.4 %fusion.27 = f32[4,2048,512]{2,1,0:T(8,128)} fusion(bf16[4,128,512]{2,1,0:T(8,128)(2,1)S(1)} %get-tuple-element.308, f32[4,128,2048]{2,1,0:T(8,128)} %copy-done, f32[4,128]{1,0:T(4,128)S(1)} %get-tuple-element.313, f32[4,128]{1,0:T(4,128)S(1)} %get-tuple-element.314, f32[4,128]{1,0:T(4,128)S(1)} %max.31, s32[4,128]{1,0:T(4,128)S(1)} %broadcast_select_fusion.7, ...), kind=kOutput, calls=%fused_computation.40.clone.1 | convolution fusion | flops 1080033280 | bytes 21536768 | tf_op jit(solution)/shard_map/while/body/vmap()/dot_general | solution.py:38
  193.2 36.4 %scatter_fusion = f32[32,256,512]{2,1,0:T(8,128)} fusion(f32[32,256,512]{2,1,0:T(8,128)} %get-tuple-element.335, s32[32]{0:T(128)S(1)} %fusion.26, f32[32,256,512]{2,1,0:T(8,128)} %bitcast.56), kind=kCustom, calls=%fused_computation.7.clone.1 | custom fusion | flops 4194304 | bytes 50331776 | tf_op jit(solution)/shard_map/while/body/scatter-add | solution.py:72
  229.6 0.1 compare_and_fusion.4
  229.6 0.6 gather_fusion.3
  230.2 0.1 compare_select_fusion.7
  230.3 0.1 reshape.401
  230.4 0.1 compare_and_fusion.5
  230.4 0.1 select_n.249
  230.5 0.6 gather_fusion.6
  231.1 0.6 gather_fusion.2
  231.7 0.1 broadcast_select_fusion.7
  231.7 0.1 broadcast_bitcast_fusion.2
  231.8 0.6 gather_fusion.4
  232.5 1.8 gather_fusion
  234.3 0.6 gather_fusion.1
  234.9 0.4 fusion.23
  235.2 8.4 %gather_fusion.5 = bf16[32,256,512]{2,1,0:T(8,128)(2,1)} fusion(bf16[32,256,512]{2,1,0:T(8,128)(2,1)} %get-tuple-element.362, s32[1024]{0:T(1024)S(1)} %pad_clamp_fusion.5), kind=kCustom, calls=%fused_computation.6.clone.1 | custom fusion | bytes 16777344 | tf_op jit(solution)/shard_map/while/body/vmap(jit(_take))/gather | solution.py:20
  243.6 4.7 bitcast_select_fusion.3
  248.3 2.9 fusion.24
  251.2 0.4 copy-done.1
  251.5 1.9 copy-done
  253.4 1.0 fusion.25
  254.4 0.7 add_multiply_fusion.2
  255.6 6.5 convolution_add_fusion.2
  262.1 2.8 scatter_fusion.1
  264.9 10.4 %fusion.27 = f32[4,2048,512]{2,1,0:T(8,128)} fusion(bf16[4,128,512]{2,1,0:T(8,128)(2,1)S(1)} %get-tuple-element.308, f32[4,128,2048]{2,1,0:T(8,128)} %copy-done, f32[4,128]{1,0:T(4,128)S(1)} %get-tuple-element.313, f32[4,128]{1,0:T(4,128)S(1)} %get-tuple-element.314, f32[4,128]{1,0:T(4,128)S(1)} %max.31, s32[4,128]{1,0:T(4,128)S(1)} %broadcast_select_fusion.7, ...), kind=kOutput, calls=%fused_computation.40.clone.1 | convolution fusion | flops 1080033280 | bytes 21536768 | tf_op jit(solution)/shard_map/while/body/vmap()/dot_general | solution.py:38
  275.3 36.1 %scatter_fusion = f32[32,256,512]{2,1,0:T(8,128)} fusion(f32[32,256,512]{2,1,0:T(8,128)} %get-tuple-element.335, s32[32]{0:T(128)S(1)} %fusion.26, f32[32,256,512]{2,1,0:T(8,128)} %bitcast.56), kind=kCustom, calls=%fused_computation.7.clone.1 | custom fusion | flops 4194304 | bytes 50331776 | tf_op jit(solution)/shard_map/while/body/scatter-add | solution.py:72
  311.4 280.5 %reduce-scatter.2.cloned.1.call-done = f32[1024,512]{1,0:T(8,128)} async-done(((f32[8192,512]{1,0:T(8,128)}), f32[1024,512]{1,0:T(8,128)}) %reduce-scatter.2.cloned.1.call-update) | async-done | bytes 2097168 | tf_op jit(solution)/shard_map/reduce_scatter | solution.py:124
  592.0 40.1 %psum.14 = f32[]{:T(128)} all-reduce(f32[]{:T(128)} %get-tuple-element.169), channel_id=1, replica_groups=mesh['seq'=4,'users'=8] {'seq','users'}, use_global_device_ids=true, to_apply=%region_9.10 | all-reduce | flops 1 | bytes 8 | tf_op jit(solution)/shard_map/psum | solution.py:122
  632.8 12.9 %all-reduce.2.cloned.1.call-done = f32[1024,512]{1,0:T(8,128)} async-done(((f32[1024,512]{1,0:T(8,128)}), f32[1024,512]{1,0:T(8,128)}) %all-reduce.2.cloned.1.call-update) | async-done | bytes 2097168 | tf_op jit(solution)/shard_map/psum | solution.py:125
  645.7 3.1 copy.34
  (34 shorter events, 0.5 us)
Async XLA Ops:
  7.2 37.2 %copy-start.4 = (s32[1,5]{1,0:T(1,128)S(1)}, s32[1,5]{1,0:T(1,128)}, u32[]{:S(2)}) copy-start(s32[1,5]{1,0:T(1,128)} %param.15) | copy-start | bytes 64
  7.2 130.8 %all-gather.2.cloned.1.call-start = ((), (), s32[]{:S(2)}) async-start(), calls=%async_computation.1 | async-start | bytes 9437184 | tf_op jit(solution)/shard_map/all_gather | solution.py:92
  7.9 584.0 %reduce-scatter.2.cloned.1.call-start = ((), (), s32[]{:S(2)}) async-start(), calls=%async_computation.2 | async-start | bytes 18874368 | tf_op jit(solution)/shard_map/reduce_scatter | solution.py:124
  139.5 7.9 %copy-start.2 = (s32[1,8,8]{2,1,0:T(8,128)S(1)}, s32[1,8,8]{2,1,0:T(8,128)}, u32[]{:S(2)}) copy-start(s32[1,8,8]{2,1,0:T(8,128)} %param.14) | copy-start | bytes 772
  139.5 7.9 %copy-start.3 = (s32[1,1024]{1,0:T(1,128)S(1)}, s32[1,1024]{1,0:T(1,128)}, u32[]{:S(2)}) copy-start(s32[1,1024]{1,0:T(1,128)} %param.13) | copy-start | bytes 12292
  166.2 3.2 copy-start.1
  169.4 1.9 copy-start
  248.3 3.2 copy-start.1
  251.5 1.9 copy-start
  311.4 334.3 %all-reduce.2.cloned.1.call-start = ((), (), s32[]{:S(2)}) async-start(), calls=%async_computation.3 | async-start | bytes 4194304 | tf_op jit(solution)/shard_map/psum | solution.py:125
Sparse Core Ops, SparseCore 0:
  10.1 127.7 all-gather.1
  311.5 280.4 reduce-scatter.1
  594.4 51.1 all-reduce.1
where the time goes:
time: 657 us; the launch traced here: 656 us
  waiting for transfers between devices  387 us (59%)
  other arithmetic  88.4 us (13%)
  blocking collectives  72.9 us (11%)
  local copies, waits for them, and re-layouts  50.6 us (8%)
  matrix products  39.5 us (6%)
  between operations  16.3 us (2%)
    reduce_scatter x1, waiting for transfers between devices, per_device(): lax.psum_scatter(grad_full, 'users', scatter_dimension=0, tiled=True)  281 us
    all_gather x1, waiting for transfers between devices, per_device(): lax.all_gather(pool_table, 'users', axis=0, tiled=True)  93.3 us
    scatter-add x2, other arithmetic, advance(): grad_acc.at[picked_now.reshape(-1)]  72.5 us
    psum x1, blocking collectives, per_device(): loss_total = lax.psum(loss_part, ('seq', 'users')) * factor  40.1 us
    all_gather x1, blocking collectives, per_device(): lax.all_gather(pool_items, 'users', axis=0, tiled=True)  32.7 us
    dot_general x2, matrix products, block_terms(): pool_grad = jnp.dot(neg_grad.T, narrow, preferred_element_type=jnp.float32)  20.9 us
    gather x2, local copies, waits for them, and re-layouts, block_terms(): jnp.take(pool_rows, chosen, axis=0).reshape(-1, pool_rows.shape[2])  16.8 us
  transfers between devices with their start and end apart: 3, of which 3 were waited for; matrix products, arithmetic and copies ran while one was open for 0% of the time, Pallas kernels for 0%

commit v1 on v0

v1 whole, which is shorter than its diff:
```python
import functools
import jax
import jax.numpy as jnp
from jax import lax
from jax.experimental import pallas as pl
from jax.experimental.pallas import tpu as pltpu
from jax.sharding import PartitionSpec as P

NB = 256
PB = 128
HEAD = 16
ID_BASE = 128
VMEM = 48 * 1024 * 1024
NT = (((1,), (1,)), ((), ()))
TN = (((0,), (0,)), ((), ()))


def swap(array, axis, mask):
    count = lax.axis_size(axis)
    return lax.ppermute(array, axis, [(i, i ^ mask) for i in range(count)])


def history_weights(bounds, positions):
    starts = bounds[:-1]
    finish = bounds[1:]
    lengths = (finish - starts).astype(jnp.float32)
    inside = (positions[..., None] >= starts) & (positions[..., None] < finish)
    return jnp.sum(jnp.where(inside, 1.0 / lengths, 0.0), axis=-1)


def gather_slabs(table, index, first, count, per_piece, stride, slab):
    rows = []
    for k in range(count):
        base = index[first + k]
        row = (base // per_piece) * stride + (base % per_piece) * slab
        rows.append(table[pl.ds(pl.multiple_of(row, 16), slab), :])
    return rows


def lane_row(columns):
    folded = columns[:, :PB]
    for k in range(1, columns.shape[1] // PB):
        folded = folded + columns[:, k * PB:(k + 1) * PB]
    return jnp.sum(folded.T, axis=0, keepdims=True)


def load_pieces(pieces, table, sems, stride):
    copies = [
        pltpu.make_async_copy(piece, table.at[pl.ds(k * stride, stride)], sems.at[k])
        for k, piece in enumerate(pieces)
    ]
    for copy in copies:
        copy.start()
    for copy in copies:
        copy.wait()


def score_kernel(dims, index, *refs):
    peers, blocks, picks, users, per_piece, slab = dims
    labels, narrows, target = refs[0], refs[1:1 + peers], refs[1 + peers]
    pieces = refs[2 + peers:2 + peers + users]
    scores, stats, positives, table, items, sems = refs[2 + peers + users:]
    rows = per_piece * slab
    stride = rows + HEAD
    step = pl.program_id(0)

    @pl.when(step == 0)
    def _():
        load_pieces(pieces, table, sems, stride)
        place = lax.broadcasted_iota(jnp.int32, (HEAD, PB), 0)
        units = jnp.where(place == 0, float(ID_BASE), jnp.where(place == 1, 1.0, 0.0)).astype(jnp.bfloat16)
        top = jnp.zeros((1, PB), jnp.float32)
        for k in range(users):
            head = table[pl.ds(k * stride + rows, HEAD), :]
            items[pl.ds(k * stride, rows), :] = lax.dot_general(
                head[:, :rows], units, TN, preferred_element_type=jnp.float32
            )
            top = jnp.maximum(top, head.astype(jnp.float32)[2:3, :PB])
        stats[pl.ds(2 * peers * blocks, 8), :] = jnp.broadcast_to(top, (8, PB))

    for r in range(peers):
        first = (r * blocks + step) * picks
        narrow = narrows[r][...]
        candidates = jnp.concatenate(gather_slabs(table, index, first, picks, per_piece, stride, slab), axis=0)
        ids = jnp.concatenate(gather_slabs(items, index, first, picks, per_piece, stride, slab), axis=0)
        score = lax.dot_general(candidates, narrow, NT, preferred_element_type=jnp.float32)
        masked = jnp.where(ids == labels[0, pl.ds(r, 1), :], -1e30, score)
        scores[0, r] = masked
        peak = jnp.max(masked, axis=0, keepdims=True)
        total = jnp.sum(jnp.exp(masked - peak), axis=0, keepdims=True)
        if r == 0:
            positive = lane_row(narrow.astype(jnp.float32) * target[...].astype(jnp.float32))
            positives[pl.ds(step, 1), :] = positive
            higher = jnp.maximum(peak, positive)
            total = total * jnp.exp(peak - higher) + jnp.exp(positive - higher)
            peak = higher
        stats[pl.ds(r * blocks + step, 1), :] = peak
        stats[pl.ds((peers + r) * blocks + step, 1), :] = total


def table_kernel(dims, index, *refs):
    peers, blocks, picks, users, per_piece, slab, factor = dims
    scores, weights, positives = refs[:3]
    stats = refs[3:3 + peers]
    narrows = refs[3 + peers:3 + 2 * peers]
    grads, partial, pos_grad, losses, bound, peaks, ratios = refs[3 + 2 * peers:]
    step = pl.program_id(0)

    @pl.when(step == 0)
    def _():
        partial[...] = jnp.zeros_like(partial)
        for r in range(peers):
            tops = [stats[q][pl.ds((q ^ r) * blocks, blocks), :] for q in range(peers)]
            sums = [stats[q][pl.ds((peers + (q ^ r)) * blocks, blocks), :] for q in range(peers)]
            peak = functools.reduce(jnp.maximum, tops)
            total = functools.reduce(jnp.add, [s * jnp.exp(t - peak) for t, s in zip(tops, sums)])
            weight = weights[r]
            peaks[pl.ds(r * blocks, blocks), :] = peak
            ratios[pl.ds(r * blocks, blocks), :] = weight * factor / total
            if r == 0:
                positive = positives[...]
                pos_grad[...] = weight * factor * (jnp.exp(positive - peak) / total - 1.0)
                losses[...] = weight * (peak + jnp.log(total) - positive)
        bound[...] = functools.reduce(jnp.maximum, [s[pl.ds(2 * peers * blocks, 8), :] for s in stats])

    for r in range(peers):
        first = (r * blocks + step) * picks
        peak = peaks[pl.ds(r * blocks + step, 1), :]
        ratio = ratios[pl.ds(r * blocks + step, 1), :]
        grad = (jnp.exp(scores[0, r] - peak) * ratio).astype(jnp.bfloat16)
        grads[0, r] = grad
        rows = jnp.dot(grad, narrows[r][...], preferred_element_type=jnp.float32)
        for k in range(picks):
            place = pl.ds(pl.multiple_of(index[first + k] * slab, 16), slab)
            partial[place, :] += rows[k * slab:(k + 1) * slab]


def hidden_kernel(dims, index, *refs):
    peers, blocks, picks, users, per_piece, slab = dims
    grads, pos_grad, target = refs[:3]
    pieces = refs[3:3 + users]
    outs = refs[3 + users:3 + users + peers]
    table, sems = refs[3 + users + peers:]
    stride = per_piece * slab + HEAD
    step = pl.program_id(0)

    @pl.when(step == 0)
    def _():
        load_pieces(pieces, table, sems, stride)

    for r in range(peers):
        first = (r * blocks + step) * picks
        candidates = jnp.concatenate(gather_slabs(table, index, first, picks, per_piece, stride, slab), axis=0)
        result = lax.dot_general(grads[0, r], candidates, TN, preferred_element_type=jnp.float32)
        if r == 0:
            row = jnp.broadcast_to(pos_grad[pl.ds(step, 1), :], (PB, PB)).T
            wide = target[...].astype(jnp.float32)
            for k in range(wide.shape[1] // PB):
                lanes = slice(k * PB, (k + 1) * PB)
                outs[0][:, lanes] = result[:, lanes] + row * wide[:, lanes]
        else:
            outs[r][...] = result


def per_device(hidden, target, pool_table, pool_items, labels, chosen, offsets):
    users, peers = lax.axis_size("users"), lax.axis_size("seq")
    user, peer = lax.axis_index("users"), lax.axis_index("seq")
    length, features = hidden.shape[1], hidden.shape[2]
    blocks, picks = length // PB, chosen.shape[2]
    per_piece = pool_table.shape[0] // NB
    slab = NB // peers
    rows = per_piece * slab
    stride = rows + HEAD
    wide = picks * slab
    factor = 1.0 / (users * (offsets.shape[1] - 1))
    f32, bf16 = jnp.float32, jnp.bfloat16
    params = pltpu.CompilerParams(vmem_limit_bytes=VMEM, dimension_semantics=("arbitrary",))

    narrow = hidden[0].astype(bf16)
    largest = jnp.max(jnp.abs(narrow))

    own_rows = lax.dynamic_slice_in_dim(pool_table.reshape(per_piece, NB, features), peer * slab, slab, axis=1)
    own_ids = lax.dynamic_slice_in_dim(pool_items.reshape(per_piece, NB), peer * slab, slab, axis=1).reshape(1, rows)
    own_ids = jnp.pad(own_ids, ((0, 0), (0, features - rows)))
    head = jnp.concatenate([
        (own_ids // ID_BASE).astype(bf16),
        (own_ids % ID_BASE).astype(bf16),
        jnp.broadcast_to(largest, (1, features)),
        jnp.zeros((HEAD - 3, features), bf16),
    ])
    piece = jnp.concatenate([own_rows.reshape(rows, features), head])

    pieces = {0: piece}
    for q in range(2, users, 2):
        pieces[q] = swap(piece, "users", q)
    for q in range(0, users, 2):
        pieces[q + 1] = swap(pieces[q], "users", 1)
    pieces = [pieces[q] for q in range(users)]

    narrows = {0: narrow, 1: swap(narrow, "seq", 1)}
    for q in range(2, peers, 2):
        narrows[q] = swap(narrow, "seq", q)
        narrows[q + 1] = swap(narrows[q], "seq", 1)
    narrows = [narrows[q] for q in range(peers)]

    spare = -(blocks * picks) % PB
    notes = jnp.concatenate([labels.reshape(-1), jnp.pad(chosen.reshape(-1), (0, spare))]).reshape(-1, PB)
    notes = jnp.stack([notes] + [swap(notes, "seq", q) for q in range(1, peers)])
    label_rows = notes[:, :blocks].astype(f32).transpose(1, 0, 2)
    picked = notes[:, blocks:].reshape(peers, -1)[:, :blocks * picks]
    index = (((picked // per_piece) ^ user) * per_piece + picked % per_piece).reshape(-1)

    owners = peer ^ jnp.arange(peers, dtype=jnp.int32)
    positions = owners[:, None] * length + jnp.arange(length, dtype=jnp.int32)[None, :]
    weights = history_weights(offsets[0], positions).reshape(peers, blocks, PB)

    dims = (peers, blocks, picks, users, per_piece, slab)
    by_block = pl.BlockSpec((PB, features), lambda i, _: (i, 0))
    whole = lambda *shape: pl.BlockSpec(shape, lambda i, _: (0,) * len(shape))
    score_block = pl.BlockSpec((1, peers, wide, PB), lambda i, _: (i, 0, 0, 0))
    anywhere = pl.BlockSpec(memory_space=pl.ANY)
    stat_rows = 2 * peers * blocks + 8
    work = 2 * peers * length * wide * features

    scores, stats, positives = pl.pallas_call(
        functools.partial(score_kernel, dims),
        grid_spec=pltpu.PrefetchScalarGridSpec(
            num_scalar_prefetch=1,
            grid=(blocks,),
            in_specs=[pl.BlockSpec((1, peers, PB), lambda i, _: (i, 0, 0))] + [by_block] * (peers + 1) + [anywhere] * users,
            out_specs=[score_block, whole(stat_rows, PB), whole(blocks, PB)],
            scratch_shapes=[
                pltpu.VMEM((users * stride, features), bf16),
                pltpu.VMEM((users * stride, PB), f32),
                pltpu.SemaphoreType.DMA((users,)),
            ],
        ),
        out_shape=[
            jax.ShapeDtypeStruct((blocks, peers, wide, PB), f32),
            jax.ShapeDtypeStruct((stat_rows, PB), f32),
            jax.ShapeDtypeStruct((blocks, PB), f32),
        ],
        compiler_params=params,
        cost_estimate=pl.CostEstimate(flops=work, bytes_accessed=16 << 20, transcendentals=0),
        name="scores",
    )(index, label_rows, *narrows, target[0], *pieces)

    all_stats = [stats] + [swap(stats, "seq", q) for q in range(1, peers)]

    grads, partial, pos_grad, losses, bound = pl.pallas_call(
        functools.partial(table_kernel, dims + (factor,)),
        grid_spec=pltpu.PrefetchScalarGridSpec(
            num_scalar_prefetch=1,
            grid=(blocks,),
            in_specs=[score_block, whole(peers, blocks, PB), whole(blocks, PB)]
            + [whole(stat_rows, PB)] * peers + [by_block] * peers,
            out_specs=[score_block, whole(users * rows, features), whole(blocks, PB), whole(blocks, PB), whole(8, PB)],
            scratch_shapes=[pltpu.VMEM((peers * blocks, PB), f32), pltpu.VMEM((peers * blocks, PB), f32)],
        ),
        out_shape=[
            jax.ShapeDtypeStruct((blocks, peers, wide, PB), bf16),
            jax.ShapeDtypeStruct((users * rows, features), f32),
            jax.ShapeDtypeStruct((blocks, PB), f32),
            jax.ShapeDtypeStruct((blocks, PB), f32),
            jax.ShapeDtypeStruct((8, PB), f32),
        ],
        compiler_params=params,
        cost_estimate=pl.CostEstimate(flops=work, bytes_accessed=20 << 20, transcendentals=0),
        name="table_grads",
    )(index, scores, weights, positives, *all_stats, *narrows)

    ceiling = jnp.maximum(bound[0, 0], 1e-30)
    scale, back = 16384.0 / ceiling, ceiling / 16384.0
    parts = partial.reshape(users, rows, features)
    sums = {}
    for q in reversed(range(0, users, 2)):
        arrived = swap((parts[q + 1] * scale).astype(jnp.float16), "users", 1)
        sums[q] = parts[q] * scale + arrived.astype(f32)
    owned = sums[0]
    for q in reversed(range(2, users, 2)):
        owned = owned + swap(sums[q].astype(jnp.float16), "users", q).astype(f32)

    hiddens = pl.pallas_call(
        functools.partial(hidden_kernel, dims),
        grid_spec=pltpu.PrefetchScalarGridSpec(
            num_scalar_prefetch=1,
            grid=(blocks,),
            in_specs=[score_block, whole(blocks, PB), by_block] + [anywhere] * users,
            out_specs=[by_block] * peers,
            scratch_shapes=[pltpu.VMEM((users * stride, features), bf16), pltpu.SemaphoreType.DMA((users,))],
        ),
        out_shape=[jax.ShapeDtypeStruct((length, features), f32)] * peers,
        compiler_params=params,
        cost_estimate=pl.CostEstimate(flops=work, bytes_accessed=16 << 20, transcendentals=0),
        name="hidden_grads",
    )(index, grads, pos_grad, target[0], *pieces)

    hidden_scale = 16384.0 / factor
    grad_hidden = hiddens[0] + swap(hiddens[1], "seq", 1)
    for q in range(2, peers, 2):
        both = hiddens[q] + swap(hiddens[q + 1], "seq", 1)
        arrived = swap((both * hidden_scale).astype(jnp.float16), "seq", q)
        grad_hidden = grad_hidden + arrived.astype(f32) * (1.0 / hidden_scale)

    total = jnp.broadcast_to(jnp.sum(losses) * factor, (8, PB))
    for axis, size in (("seq", peers), ("users", users)):
        mask = 1
        while mask < size:
            total = total + swap(total, axis, mask)
            mask *= 2
    loss = total[0, 0]

    quarters = {0: owned, 1: swap(owned, "seq", 1)}
    for q in range(2, peers, 2):
        coded = swap(owned.astype(jnp.float16), "seq", q)
        quarters[q], quarters[q + 1] = coded.astype(f32), swap(coded, "seq", 1).astype(f32)
    quarters = jnp.stack([quarters[q] for q in range(peers)]) * back
    ordered = jnp.take(quarters, owners, axis=0).reshape(peers, per_piece, slab, features)
    grad_table = ordered.transpose(1, 0, 2, 3).reshape(pool_table.shape)
    return loss, grad_hidden[None], grad_table


def solution(mesh):
    return jax.shard_map(
        per_device,
        mesh=mesh,
        in_specs=(
            P("users", "seq", None),
            P("users", "seq", None),
            P("users", None),
            P("users"),
            P("users", "seq"),
            P("users", "seq", None),
            P("users", None),
        ),
        out_specs=(P(), P("users", "seq", None), P("users", None)),
        check_vma=False,
    )
```

time: 657 us -> 200 us (0.30)
  waiting for transfers between devices: 387 us -> 95.3 us
  blocking collectives: 72.9 us -> 0 us
  other arithmetic: 88.4 us -> 18.3 us
  local copies, waits for them, and re-layouts: 50.6 us -> 10.9 us
  matrix products: 39.5 us -> 0 us
  starting transfers between devices: 0.12 us -> 37.2 us
  Pallas kernels: 0 us -> 35.5 us
  between operations: 16.3 us -> 2.26 us
    reduce_scatter x1 -> x0, waiting for transfers between devices: 281 us -> none  [per_device(): lax.psum_scatter(grad_full, 'users', scatter_dimension=0, tiled=True)]
    ppermute x0 -> x34, waiting for transfers between devices: none -> 95.3 us  [swap(): return lax.ppermute(array, axis, [(i, i ^ mask) for i in range(count)])]
    all_gather x1 -> x0, waiting for transfers between devices: 93.3 us -> none  [per_device(): lax.all_gather(pool_table, 'users', axis=0, tiled=True)]
    scatter-add x2 -> x0, other arithmetic: 72.5 us -> none  [advance(): grad_acc.at[picked_now.reshape(-1)]]
    psum x1 -> x0, blocking collectives: 40.1 us -> none  [per_device(): loss_total = lax.psum(loss_part, ('seq', 'users')) * factor]
    dot_general x6 -> x0, matrix products: 39.5 us -> none  [the longest x2 20.9 us: block_terms(): pool_grad = jnp.dot(neg_grad.T, narrow, preferred_element_type=jnp.float32)]
    ppermute x0 -> x34, starting transfers between devices: none -> 37.2 us  [swap(): return lax.ppermute(array, axis, [(i, i ^ mask) for i in range(count)])]
    pallas_call x0 -> x3, Pallas kernels: none -> 35.5 us  [the longest x1 12.6 us: per_device(): pl.pallas_call(functools.partial(score_kernel, dims), grid_spec=pltpu.Pre...]
  transfers between devices with their start and end apart: 3 -> 34, of which waited for: 3 -> 14; matrix products, arithmetic and copies ran while one was open for 0% -> 11% of each run, Pallas kernels for 0% -> 0%
where the time goes in v1:
time: 200 us; the launch traced here: 199 us
  waiting for transfers between devices  95.3 us (48%)
  starting transfers between devices  37.2 us (19%)
  Pallas kernels  35.5 us (18%)
  other arithmetic  18.3 us (9%)
  local copies, waits for them, and re-layouts  10.9 us (5%)
  between operations  2.26 us (1%)
    ppermute x34, waiting for transfers between devices, swap(): return lax.ppermute(array, axis, [(i, i ^ mask) for i in range(count)])  95.3 us
    ppermute x34, starting transfers between devices, swap(): return lax.ppermute(array, axis, [(i, i ^ mask) for i in range(count)])  37.2 us
    pallas_call x1, Pallas kernels, per_device(): pl.pallas_call(functools.partial(score_kernel, dims), grid_spec=pltpu.Pre...  12.6 us
    pallas_call x1, Pallas kernels, per_device(): pl.pallas_call(functools.partial(table_kernel, dims + (factor,)), grid_sp...  12.3 us
    pallas_call x1, Pallas kernels, per_device(): pl.pallas_call(functools.partial(hidden_kernel, dims), grid_spec=pltpu.Pr...  10.6 us
  transfers between devices with their start and end apart: 34, of which 14 were waited for; matrix products, arithmetic and copies ran while one was open for 11% of the time, Pallas kernels for 0%

profile of v1, /device:TPU:0, one launch (start us, length us, event | category | flops | bytes accessed | tf_op | source)
XLA Modules:
  0.0 199.4 jit_solution(12841152488662507523)
XLA Ops:
  0.7 2.5 %abs_reduce_fusion = (bf16[]{:T(256)}, bf16[1024,512]{1,0:T(8,128)(2,1)S(1)}) fusion(f32[1,1024,512]{2,1,0:T(8,128)} %param.7), kind=kLoop, calls=%fused_computation.5 | loop fusion | flops 1572863 | bytes 3145730 | tf_op jit(solution)/shard_map/reduce_max | solution.py:180
  3.2 3.0 %collective-permute-start.4 = (bf16[1024,512]{1,0:T(8,128)(2,1)S(1)}, bf16[1024,512]{1,0:T(8,128)(2,1)S(1)}, u32[]{:S(2)}, u32[]{:S(2)}) collective-permute-start(bf16[1024,512]{1,0:T(8,128)(2,1)S(1)} %get-tuple-element.30.refs_1_.refs_7_), channel_id=1, source_target_pairs={{0,16},{8,24},{16,0},{24,8},{1,17},{9,25},{17,1},{25,9},{2,18},{10... | collective-permute-start | bytes 3145736 | tf_op jit(solution)/shard_map/ppermute | solution.py:20
  6.4 0.4 collective-permute-start.3
  6.9 0.1 reshape.124
  7.0 0.7 constant_dynamic-slice_fusion.1
  7.8 0.7 broadcast_in_dim.36
  8.4 1.2 concatenate.7.refs_6_.refs_3_
  9.6 2.9 %collective-permute-start.9 = (bf16[272,512]{1,0:T(8,128)(2,1)S(1)}, bf16[272,512]{1,0:T(8,128)(2,1)}, u32[]{:S(2)}, u32[]{:S(2)}) collective-permute-start(bf16[272,512]{1,0:T(8,128)(2,1)S(1)} %concatenate.7.refs_6_.refs_3_), channel_id=1, source_target_pairs={{0,4},{1,5},{2,6},{3,7},{4,0},{5,1},{6,2},{7,3},{8,12},{9,13},{10,... | collective-permute-start | bytes 835592 | tf_op jit(solution)/shard_map/ppermute | solution.py:20
  12.5 16.9 %collective-permute-done.4.refs_3_.refs_9_ = bf16[1024,512]{1,0:T(8,128)(2,1)S(1)} collective-permute-done((bf16[1024,512]{1,0:T(8,128)(2,1)S(1)}, bf16[1024,512]{1,0:T(8,128)(2,1)S(1)}, u32[]{:S(2)}, u32[]{:S(2)}) %collective-permute-start.4) | collective-permute-done | bytes 1048608 | tf_op jit(solution)/shard_map/ppermute | solution.py:20
  29.5 1.9 collective-permute-start.2
  31.4 3.7 %collective-permute-start.11 = (bf16[272,512]{1,0:T(8,128)(2,1)S(1)}, bf16[272,512]{1,0:T(8,128)(2,1)}, u32[]{:S(2)}, u32[]{:S(2)}) collective-permute-start(bf16[272,512]{1,0:T(8,128)(2,1)S(1)} %concatenate.7.refs_6_.refs_3_), channel_id=1, source_target_pairs={{0,6},{1,7},{2,4},{3,5},{4,2},{5,3},{6,0},{7,1},{8,14},{9,15},{10,... | collective-permute-start | bytes 835592 | tf_op jit(solution)/shard_map/ppermute | solution.py:20
  35.1 1.6 collective-permute-start.6
  36.8 6.2 %collective-permute-done.11.refs_12_.refs_9_ = bf16[272,512]{1,0:T(8,128)(2,1)} collective-permute-done((bf16[272,512]{1,0:T(8,128)(2,1)S(1)}, bf16[272,512]{1,0:T(8,128)(2,1)}, u32[]{:S(2)}, u32[]{:S(2)}) %collective-permute-start.11) | collective-permute-done | bytes 278560 | tf_op jit(solution)/shard_map/ppermute | solution.py:20
  43.0 1.5 collective-permute-start.10
  44.5 3.6 %collective-permute-done.7.refs_8_.refs_5_ = bf16[272,512]{1,0:T(8,128)(2,1)} collective-permute-done((bf16[272,512]{1,0:T(8,128)(2,1)S(1)}, bf16[272,512]{1,0:T(8,128)(2,1)}, u32[]{:S(2)}, u32[]{:S(2)}) %collective-permute-start.7) | collective-permute-done | bytes 278560 | tf_op jit(solution)/shard_map/ppermute | solution.py:20
  48.1 1.5 collective-permute-start.12
  49.6 0.7 copy-done.2
  50.3 0.5 collective-permute-start.8
  50.8 0.1 reshape.120.index
  51.0 7.0 %collective-permute-done.12.refs_13_.refs_10_ = bf16[272,512]{1,0:T(8,128)(2,1)} collective-permute-done((bf16[272,512]{1,0:T(8,128)(2,1)}, bf16[272,512]{1,0:T(8,128)(2,1)}, u32[]{:S(2)}, u32[]{:S(2)}) %collective-permute-start.12) | collective-permute-done | bytes 278560 | tf_op jit(solution)/shard_map/ppermute | solution.py:20
  57.9 5.0 %collective-permute-done.8.refs_9_.refs_6_ = bf16[272,512]{1,0:T(8,128)(2,1)} collective-permute-done((bf16[272,512]{1,0:T(8,128)(2,1)}, bf16[272,512]{1,0:T(8,128)(2,1)}, u32[]{:S(2)}, u32[]{:S(2)}) %collective-permute-start.8) | collective-permute-done | bytes 278560 | tf_op jit(solution)/shard_map/ppermute | solution.py:20
  63.0 1.0 copy-done.3
  63.9 12.6 %scores.1 = (f32[8,4,512,128]{3,2,1,0:T(8,128)}, f32[72,128]{1,0:T(8,128)S(1)}, f32[8,128]{1,0:T(8,128)S(1)}) custom-call(s32[256]{0:T(256)S(1)} %reshape.120.index, f32[8,4,128]{2,1,0:T(4,128)S(1)} %fusion.1.refs_0_, bf16[1024,512]{1,0:T(8,128)(2,1)S(1)} %get-tuple-element.30.refs_1_.refs_7_, bf16[1024,512]{1,0:T(8,128)(2,1)} %collective-permute-done.3.refs_2_.refs_8_, ...), custom_call_target="tpu_custom_call" | custom-call | flops 2147483648 | bytes 16777216 | tf_op jit(solution)/shard_map/scores/pallas_call | solution.py:225
  76.6 0.6 collective-permute-start.14
  77.2 1.3 collective-permute-start.15
  78.4 0.1 select_reduce_fusion
  78.6 2.4 %collective-permute-done.14.refs_5_ = f32[72,128]{1,0:T(8,128)S(1)} collective-permute-done((f32[72,128]{1,0:T(8,128)S(1)}, f32[72,128]{1,0:T(8,128)S(1)}, u32[]{:S(2)}, u32[]{:S(2)}) %collective-permute-start.14) | collective-permute-done | bytes 36896 | tf_op jit(solution)/shard_map/ppermute | solution.py:20
  81.0 12.3 %table_grads.1 = (bf16[8,4,512,128]{3,2,1,0:T(8,128)(2,1)}, f32[2048,512]{1,0:T(8,128)}, f32[8,128]{1,0:T(8,128)S(1)}, f32[8,128]{1,0:T(8,128)S(1)}, f32[8,128]{1,0:T(8,128)S(1)}) custom-call(s32[256]{0:T(256)S(1)} %reshape.120.index, f32[8,4,512,128]{3,2,1,0:T(8,128)} %get-tuple-element.15.refs_0_, f32[4,8,128]{2,1,0:T(8,128)S(1)} %bitcast.47, ...), custom_call_target="tpu_custom_call" | custom-call | flops 2147483648 | bytes 20971520 | tf_op jit(solution)/shard_map/table_grads/pallas_call | solution.py:250
  93.3 10.6 %hidden_grads.1 = (f32[1024,512]{1,0:T(8,128)S(1)}, f32[1024,512]{1,0:T(8,128)}, f32[1024,512]{1,0:T(8,128)}, f32[1024,512]{1,0:T(8,128)}) custom-call(s32[256]{0:T(256)S(1)} %reshape.120.index, bf16[8,4,512,128]{3,2,1,0:T(8,128)(2,1)} %get-tuple-element.19.refs_0_, f32[8,128]{1,0:T(8,128)S(1)} %get-tuple-element.20.refs_1_, bf16[1024,512]{1,0:T(8,128)(2,1)S(1)} %bitcast.49, ...), custom_call_target="tpu_custom_call" | custom-call | flops 2147483648 | bytes 16777216 | tf_op jit(solution)/shard_map/hidden_grads/pallas_call | solution.py:283
  103.9 0.3 collective-permute-start.22
  104.2 0.5 slice.62
  105.4 1.2 multiply_convert_fusion.4
  106.6 1.5 collective-permute-start.25
  108.1 0.5 collective-permute-start.27
  108.6 1.5 collective-permute-start.29
  110.1 0.5 collective-permute-start.24
  110.6 0.6 reduce_sum.19
  111.9 4.1 %collective-permute-done.25 = f16[256,512]{1,0:T(8,128)(2,1)} collective-permute-done((f16[256,512]{1,0:T(8,128)(2,1)}, f16[256,512]{1,0:T(8,128)(2,1)}, u32[]{:S(2)}, u32[]{:S(2)}) %collective-permute-start.25) | collective-permute-done | bytes 262176 | tf_op jit(solution)/shard_map/ppermute | solution.py:20
  116.0 5.6 %collective-permute-done.27 = f16[256,512]{1,0:T(8,128)(2,1)} collective-permute-done((f16[256,512]{1,0:T(8,128)(2,1)}, f16[256,512]{1,0:T(8,128)(2,1)}, u32[]{:S(2)}, u32[]{:S(2)}) %collective-permute-start.27) | collective-permute-done | bytes 262176 | tf_op jit(solution)/shard_map/ppermute | solution.py:20
  121.6 5.6 %collective-permute-done.29 = f16[256,512]{1,0:T(8,128)(2,1)} collective-permute-done((f16[256,512]{1,0:T(8,128)(2,1)}, f16[256,512]{1,0:T(8,128)(2,1)}, u32[]{:S(2)}, u32[]{:S(2)}) %collective-permute-start.29) | collective-permute-done | bytes 262176 | tf_op jit(solution)/shard_map/ppermute | solution.py:20
  127.2 1.9 add_convert_fusion.2
  129.1 3.5 %collective-permute-start.26 = (f16[256,512]{1,0:T(8,128)(2,1)S(1)}, f16[256,512]{1,0:T(8,128)(2,1)S(1)}, u32[]{:S(2)}, u32[]{:S(2)}) collective-permute-start(f16[256,512]{1,0:T(8,128)(2,1)S(1)} %get-tuple-element.37), channel_id=1, source_target_pairs={{0,6},{1,7},{2,4},{3,5},{4,2},{5,3},{6,0},{7,1},{8,14},{9,15},{10,... | collective-permute-start | bytes 786440 | tf_op jit(solution)/shard_map/ppermute | solution.py:20
  132.6 2.7 %collective-permute-start.28 = (f16[256,512]{1,0:T(8,128)(2,1)S(1)}, f16[256,512]{1,0:T(8,128)(2,1)S(1)}, u32[]{:S(2)}, u32[]{:S(2)}) collective-permute-start(f16[256,512]{1,0:T(8,128)(2,1)S(1)} %get-tuple-element.39), channel_id=1, source_target_pairs={{0,4},{1,5},{2,6},{3,7},{4,0},{5,1},{6,2},{7,3},{8,12},{9,13},{10,... | collective-permute-start | bytes 786440 | tf_op jit(solution)/shard_map/ppermute | solution.py:20
  135.4 0.1 collective-permute-start.30
  135.5 4.1 %collective-permute-done.26 = f16[256,512]{1,0:T(8,128)(2,1)S(1)} collective-permute-done((f16[256,512]{1,0:T(8,128)(2,1)S(1)}, f16[256,512]{1,0:T(8,128)(2,1)S(1)}, u32[]{:S(2)}, u32[]{:S(2)}) %collective-permute-start.26) | collective-permute-done | bytes 262176 | tf_op jit(solution)/shard_map/ppermute | solution.py:20
  139.6 0.8 collective-permute-start.17
  140.5 14.7 %collective-permute-done.28 = f16[256,512]{1,0:T(8,128)(2,1)S(1)} collective-permute-done((f16[256,512]{1,0:T(8,128)(2,1)S(1)}, f16[256,512]{1,0:T(8,128)(2,1)S(1)}, u32[]{:S(2)}, u32[]{:S(2)}) %collective-permute-start.28) | collective-permute-done | bytes 262176 | tf_op jit(solution)/shard_map/ppermute | solution.py:20
  155.1 1.2 fusion.12
  156.4 1.1 collective-permute-start.32
  157.4 1.5 collective-permute-start.18
  158.9 2.1 %collective-permute-done.18 = f32[8,128]{1,0:T(8,128)S(1)} collective-permute-done((f32[8,128]{1,0:T(8,128)S(1)}, f32[8,128]{1,0:T(8,128)S(1)}, u32[]{:S(2)}, u32[]{:S(2)}) %collective-permute-start.18) | collective-permute-done | bytes 4128 | tf_op jit(solution)/shard_map/ppermute | solution.py:20
  161.0 0.6 collective-permute-start.19
  161.6 3.0 %collective-permute-done.19 = f32[8,128]{1,0:T(8,128)S(1)} collective-permute-done((f32[8,128]{1,0:T(8,128)S(1)}, f32[8,128]{1,0:T(8,128)S(1)}, u32[]{:S(2)}, u32[]{:S(2)}) %collective-permute-start.19) | collective-permute-done | bytes 4128 | tf_op jit(solution)/shard_map/ppermute | solution.py:20
  164.7 1.9 collective-permute-start.20
  166.6 0.5 collective-permute-start.33
  167.1 3.1 %multiply_convert_fusion = f16[1024,512]{1,0:T(8,128)(2,1)} fusion(f32[1024,512]{1,0:T(8,128)S(1)} %copy-done.5, f32[1024,512]{1,0:T(8,128)} %collective-permute-done.22), kind=kLoop, calls=%fused_computation.4 | loop fusion | flops 1572864 | bytes 5242880 | tf_op jit(solution)/shard_map/convert_element_type | solution.py:302
  170.2 1.2 collective-permute-start.23
  171.4 0.5 slice.60
  172.1 1.6 maximum_multiply_fusion
  173.7 3.6 %gather_fusion = f32[4,256,512]{2,1,0:T(8,128)} fusion(f32[4,256,512]{2,1,0:T(8,128)} %maximum_multiply_fusion, s32[1024]{0:T(1024)S(1)} %pad_clamp_fusion), kind=kCustom, calls=%fused_computation | custom fusion | bytes 4194320 | tf_op jit(solution)/shard_map/jit(_take)/gather | solution.py:318
  177.3 1.9 select_bitcast_fusion
  179.2 1.5 copy.15
  180.8 14.9 %collective-permute-done.23 = f16[1024,512]{1,0:T(8,128)(2,1)} collective-permute-done((f16[1024,512]{1,0:T(8,128)(2,1)}, f16[1024,512]{1,0:T(8,128)(2,1)}, u32[]{:S(2)}, u32[]{:S(2)}) %collective-permute-start.23) | collective-permute-done | bytes 1048608 | tf_op jit(solution)/shard_map/ppermute | solution.py:20
  195.6 3.8 %add_bitcast_fusion = f32[1,1024,512]{2,1,0:T(8,128)} fusion(f16[1024,512]{1,0:T(8,128)(2,1)} %collective-permute-done.23, f32[1024,512]{1,0:T(8,128)S(1)} %get-tuple-element.21, f32[1024,512]{1,0:T(8,128)} %collective-permute-done.21), kind=kLoop, calls=%fused_computation.3 | loop fusion | flops 2097152 | bytes 7340032 | tf_op jit(solution)/shard_map/broadcast_in_dim | solution.py:320
  (76 shorter events, 1.0 us)
Async XLA Ops:
  0.6 6.4 %copy-start = (bf16[1024,512]{1,0:T(8,128)(2,1)S(1)}, bf16[1024,512]{1,0:T(8,128)(2,1)}, u32[]{:S(2)}) copy-start(bf16[1024,512]{1,0:T(8,128)(2,1)} %param.9) | copy-start | bytes 3145732
  0.6 5.5 %copy-start.6 = (s32[1,8,8]{2,1,0:T(8,128)S(1)}, s32[1,8,8]{2,1,0:T(8,128)}, u32[]{:S(2)}) copy-start(s32[1,8,8]{2,1,0:T(8,128)} %param.12) | copy-start | bytes 772
  0.7 5.6 %copy-start.8 = (s32[1,1024]{1,0:T(1,128)S(1)}, s32[1,1024]{1,0:T(1,128)}, u32[]{:S(2)}) copy-start(s32[1,1024]{1,0:T(1,128)} %param.11) | copy-start | bytes 12292
  0.7 6.2 %copy-start.7 = (s32[1024]{0:T(1024)S(1)}, s32[1024]{0:T(1024)}, u32[]{:S(2)}) copy-start(s32[1024]{0:T(1024)} %param.10) | copy-start | bytes 12292
  0.7 30.7 %copy-start.9 = (s32[1,5]{1,0:T(1,128)S(1)}, s32[1,5]{1,0:T(1,128)}, u32[]{:S(2)}) copy-start(s32[1,5]{1,0:T(1,128)} %param.13) | copy-start | bytes 64
  3.2 26.2 %collective-permute-start.4 = (bf16[1024,512]{1,0:T(8,128)(2,1)S(1)}, bf16[1024,512]{1,0:T(8,128)(2,1)S(1)}, u32[]{:S(2)}, u32[]{:S(2)}) collective-permute-start(bf16[1024,512]{1,0:T(8,128)(2,1)S(1)} %get-tuple-element.30.refs_1_.refs_7_), channel_id=1, source_target_pairs={{0,16},{8,24},{16,0},{24,8},{1,17},{9,25},{17,1},{25,9},{2,18},{10... | collective-permute-start | bytes 3145736 | tf_op jit(solution)/shard_map/ppermute | solution.py:20
  6.2 23.2 %collective-permute-start = (s32[9,128]{1,0:T(8,128)S(1)}, s32[9,128]{1,0:T(8,128)S(1)}, u32[]{:S(2)}, u32[]{:S(2)}) collective-permute-start(s32[9,128]{1,0:T(8,128)S(1)} %get-tuple-element.41), channel_id=1, source_target_pairs={{0,8},{8,0},{16,24},{24,16},{1,9},{9,1},{17,25},{25,17},{2,10},{10... | collective-permute-start | bytes 13832 | tf_op jit(solution)/shard_map/ppermute | solution.py:20
  6.3 25.1 %collective-permute-start.1 = (s32[9,128]{1,0:T(8,128)S(1)}, s32[9,128]{1,0:T(8,128)S(1)}, u32[]{:S(2)}, u32[]{:S(2)}) collective-permute-start(s32[9,128]{1,0:T(8,128)S(1)} %get-tuple-element.41), channel_id=1, source_target_pairs={{0,16},{8,24},{16,0},{24,8},{1,17},{9,25},{17,1},{25,9},{2,18},{10... | collective-permute-start | bytes 13832 | tf_op jit(solution)/shard_map/ppermute | solution.py:20
  6.4 56.6 %collective-permute-start.3 = (bf16[1024,512]{1,0:T(8,128)(2,1)S(1)}, bf16[1024,512]{1,0:T(8,128)(2,1)}, u32[]{:S(2)}, u32[]{:S(2)}) collective-permute-start(bf16[1024,512]{1,0:T(8,128)(2,1)S(1)} %get-tuple-element.30.refs_1_.refs_7_), channel_id=1, source_target_pairs={{0,8},{8,0},{16,24},{24,16},{1,9},{9,1},{17,25},{25,17},{2,10},{10... | collective-permute-start | bytes 3145736 | tf_op jit(solution)/shard_map/ppermute | solution.py:20
  9.6 25.5 %collective-permute-start.9 = (bf16[272,512]{1,0:T(8,128)(2,1)S(1)}, bf16[272,512]{1,0:T(8,128)(2,1)}, u32[]{:S(2)}, u32[]{:S(2)}) collective-permute-start(bf16[272,512]{1,0:T(8,128)(2,1)S(1)} %concatenate.7.refs_6_.refs_3_), channel_id=1, source_target_pairs={{0,4},{1,5},{2,6},{3,7},{4,0},{5,1},{6,2},{7,3},{8,12},{9,13},{10,... | collective-permute-start | bytes 835592 | tf_op jit(solution)/shard_map/ppermute | solution.py:20
  29.4 33.6 %collective-permute-start.5 = (bf16[1024,512]{1,0:T(8,128)(2,1)S(1)}, bf16[1024,512]{1,0:T(8,128)(2,1)}, u32[]{:S(2)}, u32[]{:S(2)}) collective-permute-start(bf16[1024,512]{1,0:T(8,128)(2,1)S(1)} %collective-permute-done.4.refs_3_.refs_9_), channel_id=1, source_target_pairs={{0,8},{8,0},{16,24},{24,16},{1,9},{9,1},{17,25},{25,17},{2,10},{10... | collective-permute-start | bytes 3145736 | tf_op jit(solution)/shard_map/ppermute | solution.py:20
  29.5 5.6 %collective-permute-start.2 = (s32[9,128]{1,0:T(8,128)S(1)}, s32[9,128]{1,0:T(8,128)S(1)}, u32[]{:S(2)}, u32[]{:S(2)}) collective-permute-start(s32[9,128]{1,0:T(8,128)S(1)} %get-tuple-element.41), channel_id=1, source_target_pairs={{0,24},{8,16},{16,8},{24,0},{1,25},{9,17},{17,9},{25,1},{2,26},{10... | collective-permute-start | bytes 13832 | tf_op jit(solution)/shard_map/ppermute | solution.py:20
  31.4 11.6 %collective-permute-start.11 = (bf16[272,512]{1,0:T(8,128)(2,1)S(1)}, bf16[272,512]{1,0:T(8,128)(2,1)}, u32[]{:S(2)}, u32[]{:S(2)}) collective-permute-start(bf16[272,512]{1,0:T(8,128)(2,1)S(1)} %concatenate.7.refs_6_.refs_3_), channel_id=1, source_target_pairs={{0,6},{1,7},{2,4},{3,5},{4,2},{5,3},{6,0},{7,1},{8,14},{9,15},{10,... | collective-permute-start | bytes 835592 | tf_op jit(solution)/shard_map/ppermute | solution.py:20
  35.1 13.0 %collective-permute-start.7 = (bf16[272,512]{1,0:T(8,128)(2,1)S(1)}, bf16[272,512]{1,0:T(8,128)(2,1)}, u32[]{:S(2)}, u32[]{:S(2)}) collective-permute-start(bf16[272,512]{1,0:T(8,128)(2,1)S(1)} %concatenate.7.refs_6_.refs_3_), channel_id=1, source_target_pairs={{0,2},{1,3},{2,0},{3,1},{4,6},{5,7},{6,4},{7,5},{8,10},{9,11},{10,... | collective-permute-start | bytes 835592 | tf_op jit(solution)/shard_map/ppermute | solution.py:20
  35.1 14.5 %collective-permute-start.6 = (bf16[272,512]{1,0:T(8,128)(2,1)S(1)}, bf16[272,512]{1,0:T(8,128)(2,1)S(1)}, u32[]{:S(2)}, u32[]{:S(2)}) collective-permute-start(bf16[272,512]{1,0:T(8,128)(2,1)S(1)} %concatenate.7.refs_6_.refs_3_), channel_id=1, source_target_pairs={{0,1},{1,0},{2,3},{3,2},{4,5},{5,4},{6,7},{7,6},{8,9},{9,8},{10,11... | collective-permute-start | bytes 835592 | tf_op jit(solution)/shard_map/ppermute | solution.py:20
  43.0 8.0 %collective-permute-start.10 = (bf16[272,512]{1,0:T(8,128)(2,1)}, bf16[272,512]{1,0:T(8,128)(2,1)}, u32[]{:S(2)}, u32[]{:S(2)}) collective-permute-start(bf16[272,512]{1,0:T(8,128)(2,1)} %collective-permute-done.9.refs_10_.refs_7_), channel_id=1, source_target_pairs={{0,1},{1,0},{2,3},{3,2},{4,5},{5,4},{6,7},{7,6},{8,9},{9,8},{10,11... | collective-permute-start | bytes 835592 | tf_op jit(solution)/shard_map/ppermute | solution.py:20
  48.1 9.8 %collective-permute-start.12 = (bf16[272,512]{1,0:T(8,128)(2,1)}, bf16[272,512]{1,0:T(8,128)(2,1)}, u32[]{:S(2)}, u32[]{:S(2)}) collective-permute-start(bf16[272,512]{1,0:T(8,128)(2,1)} %collective-permute-done.11.refs_12_.refs_9_), channel_id=1, source_target_pairs={{0,1},{1,0},{2,3},{3,2},{4,5},{5,4},{6,7},{7,6},{8,9},{9,8},{10,11... | collective-permute-start | bytes 835592 | tf_op jit(solution)/shard_map/ppermute | solution.py:20
  49.6 0.7 copy-start.2
  50.3 12.7 %collective-permute-start.8 = (bf16[272,512]{1,0:T(8,128)(2,1)}, bf16[272,512]{1,0:T(8,128)(2,1)}, u32[]{:S(2)}, u32[]{:S(2)}) collective-permute-start(bf16[272,512]{1,0:T(8,128)(2,1)} %collective-permute-done.7.refs_8_.refs_5_), channel_id=1, source_target_pairs={{0,1},{1,0},{2,3},{3,2},{4,5},{5,4},{6,7},{7,6},{8,9},{9,8},{10,11... | collective-permute-start | bytes 835592 | tf_op jit(solution)/shard_map/ppermute | solution.py:20
  63.0 1.0 copy-start.3
  76.5 2.1 %collective-permute-start.13 = (f32[72,128]{1,0:T(8,128)S(1)}, f32[72,128]{1,0:T(8,128)S(1)}, u32[]{:S(2)}, u32[]{:S(2)}) collective-permute-start(f32[72,128]{1,0:T(8,128)S(1)} %get-tuple-element.17.refs_3_), channel_id=1, source_target_pairs={{0,8},{8,0},{16,24},{24,16},{1,9},{9,1},{17,25},{25,17},{2,10},{10... | collective-permute-start | bytes 110600 | tf_op jit(solution)/shard_map/ppermute | solution.py:20
  76.6 4.4 %collective-permute-start.14 = (f32[72,128]{1,0:T(8,128)S(1)}, f32[72,128]{1,0:T(8,128)S(1)}, u32[]{:S(2)}, u32[]{:S(2)}) collective-permute-start(f32[72,128]{1,0:T(8,128)S(1)} %get-tuple-element.17.refs_3_), channel_id=1, source_target_pairs={{0,16},{8,24},{16,0},{24,8},{1,17},{9,25},{17,1},{25,9},{2,18},{10... | collective-permute-start | bytes 110600 | tf_op jit(solution)/shard_map/ppermute | solution.py:20
  77.2 3.8 %collective-permute-start.15 = (f32[72,128]{1,0:T(8,128)S(1)}, f32[72,128]{1,0:T(8,128)S(1)}, u32[]{:S(2)}, u32[]{:S(2)}) collective-permute-start(f32[72,128]{1,0:T(8,128)S(1)} %get-tuple-element.17.refs_3_), channel_id=1, source_target_pairs={{0,24},{8,16},{16,8},{24,0},{1,25},{9,17},{17,9},{25,1},{2,26},{10... | collective-permute-start | bytes 110600 | tf_op jit(solution)/shard_map/ppermute | solution.py:20
  81.0 12.3 %copy-start.1 = (bf16[1,1024,512]{2,1,0:T(8,128)(2,1)S(1)}, bf16[1,1024,512]{2,1,0:T(8,128)(2,1)}, u32[]{:S(2)}) copy-start(bf16[1,1024,512]{2,1,0:T(8,128)(2,1)} %param.8) | copy-start | bytes 3145732
  93.3 12.1 %copy-start.4 = (f32[2048,512]{1,0:T(8,128)S(1)}, f32[2048,512]{1,0:T(8,128)}, u32[]{:S(2)}) copy-start(f32[2048,512]{1,0:T(8,128)} %get-tuple-element.25) | copy-start | bytes 12582916
  103.9 63.2 %collective-permute-start.22 = (f32[1024,512]{1,0:T(8,128)}, f32[1024,512]{1,0:T(8,128)}, u32[]{:S(2)}, u32[]{:S(2)}) collective-permute-start(f32[1024,512]{1,0:T(8,128)} %get-tuple-element.24), channel_id=1, source_target_pairs={{0,8},{8,0},{16,24},{24,16},{1,9},{9,1},{17,25},{25,17},{2,10},{10... | collective-permute-start | bytes 6291464 | tf_op jit(solution)/shard_map/ppermute | solution.py:20
  106.6 9.4 %collective-permute-start.25 = (f16[256,512]{1,0:T(8,128)(2,1)}, f16[256,512]{1,0:T(8,128)(2,1)}, u32[]{:S(2)}, u32[]{:S(2)}) collective-permute-start(f16[256,512]{1,0:T(8,128)(2,1)} %get-tuple-element.36), channel_id=1, source_target_pairs={{0,1},{1,0},{2,3},{3,2},{4,5},{5,4},{6,7},{7,6},{8,9},{9,8},{10,11... | collective-permute-start | bytes 786440 | tf_op jit(solution)/shard_map/ppermute | solution.py:20
  108.1 13.6 %collective-permute-start.27 = (f16[256,512]{1,0:T(8,128)(2,1)}, f16[256,512]{1,0:T(8,128)(2,1)}, u32[]{:S(2)}, u32[]{:S(2)}) collective-permute-start(f16[256,512]{1,0:T(8,128)(2,1)} %get-tuple-element.35), channel_id=1, source_target_pairs={{0,1},{1,0},{2,3},{3,2},{4,5},{5,4},{6,7},{7,6},{8,9},{9,8},{10,11... | collective-permute-start | bytes 786440 | tf_op jit(solution)/shard_map/ppermute | solution.py:20
  108.6 18.7 %collective-permute-start.29 = (f16[256,512]{1,0:T(8,128)(2,1)}, f16[256,512]{1,0:T(8,128)(2,1)}, u32[]{:S(2)}, u32[]{:S(2)}) collective-permute-start(f16[256,512]{1,0:T(8,128)(2,1)} %get-tuple-element.34), channel_id=1, source_target_pairs={{0,1},{1,0},{2,3},{3,2},{4,5},{5,4},{6,7},{7,6},{8,9},{9,8},{10,11... | collective-permute-start | bytes 786440 | tf_op jit(solution)/shard_map/ppermute | solution.py:20
  110.1 25.4 %collective-permute-start.24 = (f16[256,512]{1,0:T(8,128)(2,1)}, f16[256,512]{1,0:T(8,128)(2,1)S(1)}, u32[]{:S(2)}, u32[]{:S(2)}) collective-permute-start(f16[256,512]{1,0:T(8,128)(2,1)} %get-tuple-element.33), channel_id=1, source_target_pairs={{0,1},{1,0},{2,3},{3,2},{4,5},{5,4},{6,7},{7,6},{8,9},{9,8},{10,11... | collective-permute-start | bytes 786440 | tf_op jit(solution)/shard_map/ppermute | solution.py:20
  116.0 51.1 %copy-start.5 = (f32[1024,512]{1,0:T(8,128)S(1)}, f32[1024,512]{1,0:T(8,128)}, u32[]{:S(2)}) copy-start(f32[1024,512]{1,0:T(8,128)} %get-tuple-element.23) | copy-start | bytes 6291460
  116.0 19.4 %collective-permute-start.16 = (f32[8,128]{1,0:T(8,128)S(1)}, f32[8,128]{1,0:T(8,128)S(1)}, u32[]{:S(2)}, u32[]{:S(2)}) collective-permute-start(f32[8,128]{1,0:T(8,128)S(1)} %broadcast_in_dim.40), channel_id=1, source_target_pairs={{0,8},{8,0},{16,24},{24,16},{1,9},{9,1},{17,25},{25,17},{2,10},{10... | collective-permute-start | bytes 12296 | tf_op jit(solution)/shard_map/ppermute | solution.py:20
  129.1 10.5 %collective-permute-start.26 = (f16[256,512]{1,0:T(8,128)(2,1)S(1)}, f16[256,512]{1,0:T(8,128)(2,1)S(1)}, u32[]{:S(2)}, u32[]{:S(2)}) collective-permute-start(f16[256,512]{1,0:T(8,128)(2,1)S(1)} %get-tuple-element.37), channel_id=1, source_target_pairs={{0,6},{1,7},{2,4},{3,5},{4,2},{5,3},{6,0},{7,1},{8,14},{9,15},{10,... | collective-permute-start | bytes 786440 | tf_op jit(solution)/shard_map/ppermute | solution.py:20
  132.6 22.5 %collective-permute-start.28 = (f16[256,512]{1,0:T(8,128)(2,1)S(1)}, f16[256,512]{1,0:T(8,128)(2,1)S(1)}, u32[]{:S(2)}, u32[]{:S(2)}) collective-permute-start(f16[256,512]{1,0:T(8,128)(2,1)S(1)} %get-tuple-element.39), channel_id=1, source_target_pairs={{0,4},{1,5},{2,6},{3,7},{4,0},{5,1},{6,2},{7,3},{8,12},{9,13},{10,... | collective-permute-start | bytes 786440 | tf_op jit(solution)/shard_map/ppermute | solution.py:20
  135.4 19.8 %collective-permute-start.30 = (f16[256,512]{1,0:T(8,128)(2,1)S(1)}, f16[256,512]{1,0:T(8,128)(2,1)S(1)}, u32[]{:S(2)}, u32[]{:S(2)}) collective-permute-start(f16[256,512]{1,0:T(8,128)(2,1)S(1)} %get-tuple-element.38), channel_id=1, source_target_pairs={{0,2},{1,3},{2,0},{3,1},{4,6},{5,7},{6,4},{7,5},{8,10},{9,11},{10,... | collective-permute-start | bytes 786440 | tf_op jit(solution)/shard_map/ppermute | solution.py:20
  135.5 45.3 %collective-permute-start.21 = (f32[1024,512]{1,0:T(8,128)}, f32[1024,512]{1,0:T(8,128)}, u32[]{:S(2)}, u32[]{:S(2)}) collective-permute-start(f32[1024,512]{1,0:T(8,128)} %get-tuple-element.22), channel_id=1, source_target_pairs={{0,8},{8,0},{16,24},{24,16},{1,9},{9,1},{17,25},{25,17},{2,10},{10... | collective-permute-start | bytes 6291464 | tf_op jit(solution)/shard_map/ppermute | solution.py:20
  139.6 17.8 %collective-permute-start.17 = (f32[8,128]{1,0:T(8,128)S(1)}, f32[8,128]{1,0:T(8,128)S(1)}, u32[]{:S(2)}, u32[]{:S(2)}) collective-permute-start(f32[8,128]{1,0:T(8,128)S(1)} %broadcast_add_fusion), channel_id=1, source_target_pairs={{0,16},{8,24},{16,0},{24,8},{1,17},{9,25},{17,1},{25,9},{2,18},{10... | collective-permute-start | bytes 12296 | tf_op jit(solution)/shard_map/ppermute | solution.py:20
  156.4 10.2 %collective-permute-start.32 = (f16[256,512]{1,0:T(8,128)(2,1)S(1)}, f16[256,512]{1,0:T(8,128)(2,1)S(1)}, u32[]{:S(2)}, u32[]{:S(2)}) collective-permute-start(f16[256,512]{1,0:T(8,128)(2,1)S(1)} %get-tuple-element.27), channel_id=1, source_target_pairs={{0,16},{8,24},{16,0},{24,8},{1,17},{9,25},{17,1},{25,9},{2,18},{10... | collective-permute-start | bytes 786440 | tf_op jit(solution)/shard_map/ppermute | solution.py:20
  157.4 3.6 %collective-permute-start.18 = (f32[8,128]{1,0:T(8,128)S(1)}, f32[8,128]{1,0:T(8,128)S(1)}, u32[]{:S(2)}, u32[]{:S(2)}) collective-permute-start(f32[8,128]{1,0:T(8,128)S(1)} %fusion.13), channel_id=1, source_target_pairs={{0,1},{1,0},{2,3},{3,2},{4,5},{5,4},{6,7},{7,6},{8,9},{9,8},{10,11... | collective-permute-start | bytes 12296 | tf_op jit(solution)/shard_map/ppermute | solution.py:20
  161.0 3.6 %collective-permute-start.19 = (f32[8,128]{1,0:T(8,128)S(1)}, f32[8,128]{1,0:T(8,128)S(1)}, u32[]{:S(2)}, u32[]{:S(2)}) collective-permute-start(f32[8,128]{1,0:T(8,128)S(1)} %add.111), channel_id=1, source_target_pairs={{0,2},{1,3},{2,0},{3,1},{4,6},{5,7},{6,4},{7,5},{8,10},{9,11},{10,... | collective-permute-start | bytes 12296 | tf_op jit(solution)/shard_map/ppermute | solution.py:20
  164.7 6.8 %collective-permute-start.20 = (f32[8,128]{1,0:T(8,128)S(1)}, f32[8,128]{1,0:T(8,128)S(1)}, u32[]{:S(2)}, u32[]{:S(2)}) collective-permute-start(f32[8,128]{1,0:T(8,128)S(1)} %add.112), channel_id=1, source_target_pairs={{0,4},{1,5},{2,6},{3,7},{4,0},{5,1},{6,2},{7,3},{8,12},{9,13},{10,... | collective-permute-start | bytes 12296 | tf_op jit(solution)/shard_map/ppermute | solution.py:20
  166.6 5.5 %collective-permute-start.31 = (f32[256,512]{1,0:T(8,128)S(1)}, f32[256,512]{1,0:T(8,128)S(1)}, u32[]{:S(2)}, u32[]{:S(2)}) collective-permute-start(f32[256,512]{1,0:T(8,128)S(1)} %get-tuple-element.28), channel_id=1, source_target_pairs={{0,8},{8,0},{16,24},{24,16},{1,9},{9,1},{17,25},{25,17},{2,10},{10... | collective-permute-start | bytes 1572872 | tf_op jit(solution)/shard_map/ppermute | solution.py:20
  166.6 5.4 %collective-permute-start.33 = (f16[256,512]{1,0:T(8,128)(2,1)S(1)}, f16[256,512]{1,0:T(8,128)(2,1)S(1)}, u32[]{:S(2)}, u32[]{:S(2)}) collective-permute-start(f16[256,512]{1,0:T(8,128)(2,1)S(1)} %collective-permute-done.32), channel_id=1, source_target_pairs={{0,8},{8,0},{16,24},{24,16},{1,9},{9,1},{17,25},{25,17},{2,10},{10... | collective-permute-start | bytes 786440 | tf_op jit(solution)/shard_map/ppermute | solution.py:20
  170.2 25.4 %collective-permute-start.23 = (f16[1024,512]{1,0:T(8,128)(2,1)}, f16[1024,512]{1,0:T(8,128)(2,1)}, u32[]{:S(2)}, u32[]{:S(2)}) collective-permute-start(f16[1024,512]{1,0:T(8,128)(2,1)} %multiply_convert_fusion), channel_id=1, source_target_pairs={{0,16},{8,24},{16,0},{24,8},{1,17},{9,25},{17,1},{25,9},{2,18},{10... | collective-permute-start | bytes 3145736 | tf_op jit(solution)/shard_map/ppermute | solution.py:20

commit v2 on v0

v2 whole, which is shorter than its diff:
```python
import functools
import jax
import jax.numpy as jnp
from jax import lax
from jax.experimental import pallas as pl
from jax.experimental.pallas import tpu as pltpu
from jax.sharding import PartitionSpec as P

NB = 256
PB = 128
HEAD = 16
ID_BASE = 128
VMEM = 8 * 1024 * 1024
NT = (((1,), (1,)), ((), ()))
TN = (((0,), (0,)), ((), ()))


def swap(array, axis, mask):
    count = lax.axis_size(axis)
    return lax.ppermute(array, axis, [(i, i ^ mask) for i in range(count)])


def history_weights(bounds, positions):
    starts = bounds[:-1]
    finish = bounds[1:]
    lengths = (finish - starts).astype(jnp.float32)
    inside = (positions[..., None] >= starts) & (positions[..., None] < finish)
    return jnp.sum(jnp.where(inside, 1.0 / lengths, 0.0), axis=-1)


def gather_slabs(table, index, first, count, per_piece, stride, slab):
    rows = []
    for k in range(count):
        base = index[first + k]
        row = (base // per_piece) * stride + (base % per_piece) * slab
        rows.append(table[pl.ds(pl.multiple_of(row, 16), slab), :])
    return jnp.concatenate(rows, axis=0)


def block_of(ref, step):
    return ref[pl.ds(pl.multiple_of(step * PB, PB), PB), :]


def lane_row(columns):
    folded = columns[:, :PB]
    for k in range(1, columns.shape[1] // PB):
        folded = folded + columns[:, k * PB:(k + 1) * PB]
    return jnp.sum(folded.T, axis=0, keepdims=True)


def score_kernel(dims, index, *refs):
    peers, blocks, picks, users, per_piece, slab = dims
    labels, top, narrows = refs[0], refs[1], refs[2:2 + peers]
    target_from, pieces = refs[2 + peers], refs[3 + peers:-7]
    scores, stats, table, items, target, sems, target_sem = refs[-7:]
    rows = per_piece * slab
    stride = rows + HEAD
    kept = 2 * peers * blocks

    copies = [pltpu.make_async_copy(target_from, target, target_sem)]
    for k, piece in enumerate(pieces):
        copies.append(pltpu.make_async_copy(piece, table.at[pl.ds(k * stride, stride)], sems.at[k]))
    for copy in copies:
        copy.start()
    place = lax.broadcasted_iota(jnp.int32, (HEAD, PB), 0)
    units = jnp.where(place == 0, float(ID_BASE), jnp.where(place == 1, 1.0, 0.0)).astype(jnp.bfloat16)
    stats[pl.ds(kept + blocks, 8), :] = top[...]
    for copy in copies:
        copy.wait()
    for k in range(users):
        items[k * stride:k * stride + rows, :] = lax.dot_general(
            table[k * stride + rows:(k + 1) * stride, :rows], units, TN, preferred_element_type=jnp.float32
        )

    def advance(step, _):
        for r in range(peers):
            first = (r * blocks + step) * picks
            narrow = block_of(narrows[r], step)
            candidates = gather_slabs(table, index, first, picks, per_piece, stride, slab)
            ids = gather_slabs(items, index, first, picks, per_piece, stride, slab)
            score = lax.dot_general(candidates, narrow, NT, preferred_element_type=jnp.float32)
            masked = jnp.where(ids == labels[pl.ds(r * blocks + step, 1), :], -1e30, score)
            scores[step, r] = masked
            peak = jnp.max(masked, axis=0, keepdims=True)
            total = jnp.sum(jnp.exp(masked - peak), axis=0, keepdims=True)
            if r == 0:
                positive = lane_row(narrow.astype(jnp.float32) * block_of(target, step).astype(jnp.float32))
                stats[pl.ds(kept + step, 1), :] = positive
                higher = jnp.maximum(peak, positive)
                total = total * jnp.exp(peak - higher) + jnp.exp(positive - higher)
                peak = higher
            stats[pl.ds(r * blocks + step, 1), :] = peak
            stats[pl.ds((peers + r) * blocks + step, 1), :] = total
        return 0

    lax.fori_loop(0, blocks, advance, 0)


def tree_sum(terms):
    while len(terms) > 1:
        terms = [terms[k] + terms[k + 1] for k in range(0, len(terms), 2)]
    return terms[0]


def grad_kernel(dims, index, *refs):
    peers, blocks, picks, users, per_piece, slab, factor = dims
    scores, weights, table = refs[:3]
    stats = refs[3:3 + peers]
    outs = refs[3 + peers:]
    near, far, pos_grad, loss, bound = outs[:5]
    hiddens, (peaks, ratios) = outs[5:4 + peers], outs[4 + peers:]
    kept = 2 * peers * blocks
    stride = per_piece * slab + HEAD

    terms = []
    for r in range(peers):
        tops = [stats[q][pl.ds((q ^ r) * blocks, blocks), :] for q in range(peers)]
        sums = [stats[q][pl.ds((peers + (q ^ r)) * blocks, blocks), :] for q in range(peers)]
        peak = functools.reduce(jnp.maximum, tops)
        total = tree_sum([s * jnp.exp(t - peak) for t, s in zip(tops, sums)])
        weight = weights[r * blocks:(r + 1) * blocks, :]
        peaks[r * blocks:(r + 1) * blocks, :] = peak
        ratios[r * blocks:(r + 1) * blocks, :] = weight * factor / total
        positive = stats[r][pl.ds(kept, blocks), :]
        terms.append(weight * (peak + jnp.log(total) - positive))
        if r == 0:
            pos_grad[...] = weight * factor * (jnp.exp(positive - peak) / total - 1.0)
    loss[...] = jnp.broadcast_to(jnp.sum(tree_sum(terms), keepdims=True) * factor, loss.shape)
    bound[...] = functools.reduce(jnp.maximum, [s[pl.ds(kept + blocks, 8), :] for s in stats])

    def advance(step, _):
        span = pl.ds(pl.multiple_of(step * PB, PB), PB)
        for r in range(peers):
            peak = peaks[pl.ds(r * blocks + step, 1), :]
            ratio = ratios[pl.ds(r * blocks + step, 1), :]
            grad = (jnp.exp(scores[step, r] - peak) * ratio).astype(jnp.bfloat16)
            if r == 0:
                near[step] = grad
            else:
                far[step, r - 1] = grad
                first = (r * blocks + step) * picks
                candidates = gather_slabs(table, index, first, picks, per_piece, stride, slab)
                hiddens[r - 1][span, :] = lax.dot_general(grad, candidates, TN, preferred_element_type=jnp.float32)
        return 0

    lax.fori_loop(0, blocks, advance, 0)


def table_kernel(dims, index, *refs):
    peers, blocks, picks, users, per_piece, slab = dims
    near, far = refs[:2]
    narrows = refs[2:2 + peers]
    partial = refs[2 + peers]
    partial[...] = jnp.zeros_like(partial)

    def advance(step, _):
        for r in range(peers):
            grad = near[step] if r == 0 else far[step, r - 1]
            rows = jnp.dot(grad, block_of(narrows[r], step), preferred_element_type=jnp.float32)
            first = (r * blocks + step) * picks
            for k in range(picks):
                place = pl.ds(pl.multiple_of(index[first + k] * slab, 16), slab)
                partial[place, :] += rows[k * slab:(k + 1) * slab]
        return 0

    lax.fori_loop(0, blocks, advance, 0)


def hidden_kernel(dims, index, near, table, pos_grad, target, out):
    peers, blocks, picks, users, per_piece, slab = dims
    stride = per_piece * slab + HEAD

    def advance(step, _):
        span = pl.ds(pl.multiple_of(step * PB, PB), PB)
        candidates = gather_slabs(table, index, step * picks, picks, per_piece, stride, slab)
        result = lax.dot_general(near[step], candidates, TN, preferred_element_type=jnp.float32)
        row = jnp.broadcast_to(pos_grad[pl.ds(step, 1), :], (PB, PB)).T
        wide = block_of(target, step).astype(jnp.float32)
        for k in range(0, wide.shape[1], PB):
            out[span, k:k + PB] = result[:, k:k + PB] + row * wide[:, k:k + PB]
        return 0

    lax.fori_loop(0, blocks, advance, 0)


def per_device(hidden, target, pool_table, pool_items, labels, chosen, offsets):
    users, peers = lax.axis_size("users"), lax.axis_size("seq")
    user, peer = lax.axis_index("users"), lax.axis_index("seq")
    length, features = hidden.shape[1], hidden.shape[2]
    blocks, picks = length // PB, chosen.shape[2]
    per_piece = pool_table.shape[0] // NB
    slab = NB // peers
    rows = per_piece * slab
    stride = rows + HEAD
    wide = picks * slab
    factor = 1.0 / (users * (offsets.shape[1] - 1))
    f32, bf16 = jnp.float32, jnp.bfloat16

    narrow = hidden[0].astype(bf16)
    largest = jnp.max(jnp.abs(narrow))

    def halves(whole_numbers):
        numbers = whole_numbers.reshape(-1)
        numbers = jnp.pad(numbers, (0, -numbers.shape[0] % features)).reshape(-1, features)
        return [(numbers // ID_BASE).astype(bf16), (numbers % ID_BASE).astype(bf16)]

    def whole_again(array, row, count):
        lines = -(-count // features)
        high, low = array[row:row + lines], array[row + lines:row + 2 * lines]
        return (high.astype(f32) * ID_BASE + low.astype(f32)).reshape(-1)[:count], row + 2 * lines

    own_rows = lax.dynamic_slice_in_dim(pool_table.reshape(per_piece, NB, features), peer * slab, slab, axis=1)
    own_ids = lax.dynamic_slice_in_dim(pool_items.reshape(per_piece, NB), peer * slab, slab, axis=1)
    spare = jnp.zeros((HEAD - 2, features), bf16)
    piece = jnp.concatenate([own_rows.reshape(rows, features)] + halves(own_ids) + [spare])

    notes = jnp.concatenate(halves(labels) + halves(chosen))
    notes = jnp.pad(notes, ((0, -notes.shape[0] % 16), (0, 0)))
    packed = jnp.concatenate([narrow, notes])
    top = jnp.broadcast_to(largest.astype(f32), (8, PB))

    pairs = users // 2
    batches = [[pairs - 1] + list(range(1, pairs // 2)), list(range(pairs // 2, pairs - 1))]
    pieces = {0: piece, 1: swap(piece, "users", 1)}
    states = {0: packed}
    for q in range(2, peers, 2):
        states[q] = swap(packed, "seq", q)
    top = jnp.maximum(top, swap(top, "users", 1))
    held = piece
    for turn, batch in enumerate(batches):
        came = [swap(held, "users", 2 * k) for k in batch]
        came, top, pieces, held = lax.optimization_barrier((came, top, pieces, piece))
        for k, part in zip(batch, came):
            pieces[2 * k] = part
            pieces[2 * k + 1] = swap(part, "users", 1)
        top = jnp.maximum(top, swap(top, "users", 2 << turn))
    mask = 2 << len(batches)
    while mask < users:
        top = jnp.maximum(top, swap(top, "users", mask))
        mask *= 2
    own, _ = lax.optimization_barrier((packed, came))
    states[1] = swap(own, "seq", 1)
    for q in range(2, peers, 2):
        states[q + 1] = swap(states[q], "seq", 1)
    narrows = [states[q] for q in range(peers)]
    pieces = [pieces[q] for q in range(users)]

    label_rows, picked = [], []
    for state in narrows:
        line, row = whole_again(state, length, length)
        label_rows.append(line.reshape(blocks, PB))
        line, row = whole_again(state, row, blocks * picks)
        picked.append(line.astype(jnp.int32))
    label_rows, picked = jnp.concatenate(label_rows), jnp.concatenate(picked)
    owner = picked // per_piece
    index = (owner ^ user) * per_piece + picked % per_piece

    owners = peer ^ jnp.arange(peers, dtype=jnp.int32)
    positions = owners[:, None] * length + jnp.arange(length, dtype=jnp.int32)[None, :]
    weights = history_weights(offsets[0], positions).reshape(peers * blocks, PB)
    weights, label_rows, index, top = lax.optimization_barrier((weights, label_rows, index, top))

    dims = (peers, blocks, picks, users, per_piece, slab)
    half = features // 2
    stat_rows = (2 * peers + 1) * blocks + 8
    in_vmem, in_smem = pl.BlockSpec(memory_space=pltpu.VMEM), pl.BlockSpec(memory_space=pltpu.SMEM)
    in_hbm = pl.BlockSpec(memory_space=pltpu.HBM)
    cost = pl.CostEstimate(flops=1 << 20, bytes_accessed=1 << 20, transcendentals=0)
    params = pltpu.CompilerParams(vmem_limit_bytes=VMEM)

    def call(kernel, name, outs, scratch, rows_of, *operands, unplaced=0):
        placed = len(operands) - unplaced
        return pl.pallas_call(
            kernel,
            in_specs=[in_smem] + [in_vmem] * placed + [in_hbm] * unplaced,
            out_specs=[in_vmem] * len(outs),
            out_shape=[jax.ShapeDtypeStruct(shape, dtype) for shape, dtype in outs],
            scratch_shapes=scratch,
            compiler_params=params, cost_estimate=cost, name=name,
        )(rows_of, *operands[:placed], *[pltpu.with_memory_space_constraint(x, pltpu.HBM) for x in operands[placed:]])

    scores, stats, table = call(
        functools.partial(score_kernel, dims), "scores",
        [((blocks, peers, wide, PB), f32), ((stat_rows, PB), f32), ((users * stride, features), bf16)],
        [
            pltpu.VMEM((users * stride, PB), f32),
            pltpu.VMEM((length, features), bf16),
            pltpu.SemaphoreType.DMA((users,)),
            pltpu.SemaphoreType.DMA,
        ],
        index, label_rows, top, *narrows, target[0], *pieces, unplaced=1 + users,
    )
    all_stats = [stats] + [swap(stats, "seq", q) for q in range(1, peers)]

    state_out = ((length, features), f32)
    near, far, pos_grad, loss, bound, *hiddens = call(
        functools.partial(grad_kernel, dims + (factor,)), "grads",
        [
            ((blocks, wide, PB), bf16),
            ((blocks, peers - 1, wide, PB), bf16),
            ((blocks, PB), f32),
            ((8, PB), f32),
            ((8, PB), f32),
        ] + [state_out] * (peers - 1),
        [pltpu.VMEM((peers * blocks, PB), f32)] * 2,
        index, scores, weights, table, *all_stats,
    )
    from_core = [swap(hiddens[q], "seq", 1) for q in range(2, peers, 2)]
    loss_arrived = swap(loss, "users", 1)
    (partial,) = call(
        functools.partial(table_kernel, dims), "table_grads", [((users * rows, features), f32)], [],
        index, near, far, *narrows,
    )
    partial, from_core, loss_arrived = lax.optimization_barrier((partial, from_core, loss_arrived))

    ceiling = jnp.maximum(bound[0, 0], 1e-30)
    scale, back = 16384.0 / ceiling, ceiling / 16384.0

    parts = partial.reshape(pairs, 2, rows, features)
    halved = [slice(0, half), slice(half, features)]

    def with_partner(lanes, arrived):
        sums = parts[:, 0, :, lanes] * scale + arrived.astype(f32)
        return sums[0], sums.astype(jnp.float16)

    def with_owners(owned, sent):
        for k in reversed(range(1, pairs)):
            owned = owned + swap(sent[k], "users", 2 * k).astype(f32)
        return owned

    hidden_scale = 16384.0 / factor
    hidden_coded = [
        [((hiddens[2 * k + 1][:, lanes] + part[:, lanes]) * hidden_scale).astype(jnp.float16) for lanes in halved]
        for k, part in enumerate(from_core)
    ]
    first_coded, second_coded = [(parts[:, 1, :, lanes] * scale).astype(jnp.float16) for lanes in halved]
    first_coded, hidden_coded = lax.optimization_barrier((first_coded, hidden_coded))
    hidden_arrived = [[swap(two[0], "seq", 2 * k + 2)] for k, two in enumerate(hidden_coded)]
    first_arrived = swap(first_coded, "users", 1)
    own_core = swap(hiddens[0], "seq", 1)
    loss = loss + loss_arrived
    mask = 2
    while mask < users:
        loss = loss + swap(loss, "users", mask)
        mask *= 2
    first_arrived, loss, second_coded, hidden_arrived, own_core, hidden_coded = lax.optimization_barrier(
        (first_arrived, loss, second_coded, hidden_arrived, own_core, hidden_coded)
    )
    second_arrived = swap(second_coded, "users", 1)
    for k, two in enumerate(hidden_coded):
        hidden_arrived[k].append(swap(two[1], "seq", 2 * k + 2))
    owned_first, sent_first = with_partner(halved[0], first_arrived)
    owned_first = with_owners(owned_first, sent_first)
    owned_first, second_arrived, near, hidden_arrived = lax.optimization_barrier(
        (owned_first, second_arrived, near, hidden_arrived)
    )
    owned_second, sent_second = with_partner(halved[1], second_arrived)
    owned_second = with_owners(owned_second, sent_second)
    (own_hidden,) = call(
        functools.partial(hidden_kernel, dims), "own_hidden_grads", [state_out], [],
        index, near, table, pos_grad, target[0],
    )
    grad_hidden = own_hidden + own_core
    for two in hidden_arrived:
        grad_hidden = grad_hidden + jnp.concatenate(two, axis=1).astype(f32) * (1.0 / hidden_scale)
    owned = jnp.concatenate([owned_first, owned_second], axis=1)
    loss = loss[0, 0]

    quarters = {0: owned, 1: swap(owned, "seq", 1)}
    for q in range(2, peers, 2):
        coded = swap(owned.astype(jnp.float16), "seq", q)
        quarters[q], quarters[q + 1] = coded.astype(f32), swap(coded, "seq", 1).astype(f32)
    grad_table = jnp.zeros((per_piece, peers, slab, features), f32)
    for q in range(peers):
        quarter = (quarters[q] * back).reshape(per_piece, 1, slab, features)
        grad_table = lax.dynamic_update_slice_in_dim(grad_table, quarter, peer ^ q, axis=1)
    return loss, grad_hidden[None], grad_table.reshape(pool_table.shape)


def solution(mesh):
    return jax.shard_map(
        per_device,
        mesh=mesh,
        in_specs=(
            P("users", "seq", None),
            P("users", "seq", None),
            P("users", None),
            P("users"),
            P("users", "seq"),
            P("users", "seq", None),
            P("users", None),
        ),
        out_specs=(P(), P("users", "seq", None), P("users", None)),
        check_vma=False,
    )
```

time: 657 us -> 137 us (0.21)
  waiting for transfers between devices: 387 us -> 48.8 us
  other arithmetic: 88.4 us -> 10.9 us
  blocking collectives: 72.9 us -> 0 us
  matrix products: 39.5 us -> 0 us
  local copies, waits for them, and re-layouts: 50.6 us -> 12.6 us
  starting transfers between devices: 0.12 us -> 36.2 us
  Pallas kernels: 0 us -> 25 us
  between operations: 16.3 us -> 2.49 us
    reduce_scatter x1 -> x0, waiting for transfers between devices: 281 us -> none  [per_device(): lax.psum_scatter(grad_full, 'users', scatter_dimension=0, tiled=True)]
    all_gather x1 -> x0, waiting for transfers between devices: 93.3 us -> none  [per_device(): lax.all_gather(pool_table, 'users', axis=0, tiled=True)]
    scatter-add x2 -> x0, other arithmetic: 72.5 us -> none  [advance(): grad_acc.at[picked_now.reshape(-1)]]
    ppermute x0 -> x34, waiting for transfers between devices: none -> 48.8 us  [swap(): return lax.ppermute(array, axis, [(i, i ^ mask) for i in range(count)])]
    psum x1 -> x0, blocking collectives: 40.1 us -> none  [per_device(): loss_total = lax.psum(loss_part, ('seq', 'users')) * factor]
    dot_general x6 -> x0, matrix products: 39.5 us -> none  [the longest x2 20.9 us: block_terms(): pool_grad = jnp.dot(neg_grad.T, narrow, preferred_element_type=jnp.float32)]
    ppermute x0 -> x34, starting transfers between devices: none -> 36.2 us  [swap(): return lax.ppermute(array, axis, [(i, i ^ mask) for i in range(count)])]
    all_gather x1 -> x0, blocking collectives: 32.7 us -> none  [per_device(): lax.all_gather(pool_items, 'users', axis=0, tiled=True)]
  transfers between devices with their start and end apart: 3 -> 34, of which waited for: 3 -> 17; matrix products, arithmetic and copies ran while one was open for 0% -> 9% of each run, Pallas kernels for 0% -> 7%
where the time goes in v2:
time: 137 us; the launch traced here: 136 us
  waiting for transfers between devices  48.8 us (36%)
  starting transfers between devices  36.2 us (26%)
  Pallas kernels  25 us (18%)
  local copies, waits for them, and re-layouts  12.6 us (9%)
  other arithmetic  10.9 us (8%)
  between operations  2.49 us (2%)
    ppermute x34, waiting for transfers between devices, swap(): return lax.ppermute(array, axis, [(i, i ^ mask) for i in range(count)])  48.8 us
    ppermute x34, starting transfers between devices, swap(): return lax.ppermute(array, axis, [(i, i ^ mask) for i in range(count)])  36.2 us
    pallas_call x4, Pallas kernels, call(): pl.pallas_call(kernel, in_specs=[in_smem] + [in_vmem] * placed + [in_hbm]...  25 us
    unnamed x39, local copies, waits for them, and re-layouts  6.84 us
  transfers between devices with their start and end apart: 34, of which 17 were waited for; matrix products, arithmetic and copies ran while one was open for 9% of the time, Pallas kernels for 7%

profile of v2, /device:TPU:0, one launch (start us, length us, event | category | flops | bytes accessed | tf_op | source)
XLA Modules:
  0.0 136.0 jit_solution(10692693585455416838)
XLA Ops:
  0.7 0.8 reshape.202
  2.1 5.1 %collective-permute-start = (bf16[272,512]{1,0:T(8,128)(2,1)S(1)}, bf16[272,512]{1,0:T(8,128)(2,1)}, u32[]{:S(2)}, u32[]{:S(2)}) collective-permute-start(bf16[272,512]{1,0:T(8,128)(2,1)S(1)} %maximum_maximum_fusion.refs_7_), channel_id=1, source_target_pairs={{0,6},{1,7},{2,4},{3,5},{4,2},{5,3},{6,0},{7,1},{8,14},{9,15},{10,... | collective-permute-start | bytes 835592 | tf_op jit(solution)/shard_map/ppermute | solution.py:20
  7.3 1.5 %collective-permute-start.3 = (bf16[272,512]{1,0:T(8,128)(2,1)S(1)}, bf16[272,512]{1,0:T(8,128)(2,1)}, u32[]{:S(2)}, u32[]{:S(2)}) collective-permute-start(bf16[272,512]{1,0:T(8,128)(2,1)S(1)} %maximum_maximum_fusion.refs_7_), channel_id=1, source_target_pairs={{0,1},{1,0},{2,3},{3,2},{4,5},{5,4},{6,7},{7,6},{8,9},{9,8},{10,11... | collective-permute-start | bytes 835592 | tf_op jit(solution)/shard_map/ppermute | solution.py:20
  8.7 2.4 %abs_reduce_fusion = (bf16[]{:T(256)}, bf16[1024,512]{1,0:T(8,128)(2,1)S(1)}) fusion(f32[1,1024,512]{2,1,0:T(8,128)} %param.7), kind=kLoop, calls=%fused_computation.17 | loop fusion | flops 1572863 | bytes 3145730 | tf_op jit(solution)/shard_map/reduce_max | solution.py:200
  11.2 0.6 broadcast_in_dim.29
  11.8 0.6 collective-permute-start.2
  12.5 0.5 broadcast.242
  13.1 0.7 reduce.3
  13.9 1.6 %collective-permute-start.9 = (bf16[1040,512]{1,0:T(8,128)(2,1)S(1)}, bf16[1040,512]{1,0:T(8,128)(2,1)S(1)}, u32[]{:S(2)}, u32[]{:S(2)}) collective-permute-start(bf16[1040,512]{1,0:T(8,128)(2,1)S(1)} %pad_maximum_fusion.refs_2_), channel_id=1, source_target_pairs={{0,16},{8,24},{16,0},{24,8},{1,17},{9,25},{17,1},{25,9},{2,18},{10... | collective-permute-start | bytes 3194888 | tf_op jit(solution)/shard_map/ppermute | solution.py:20
  16.2 3.8 %collective-permute-done.1.refs_9_ = bf16[272,512]{1,0:T(8,128)(2,1)} collective-permute-done((bf16[272,512]{1,0:T(8,128)(2,1)S(1)}, bf16[272,512]{1,0:T(8,128)(2,1)}, u32[]{:S(2)}, u32[]{:S(2)}) %collective-permute-start.1) | collective-permute-done | bytes 278560 | tf_op jit(solution)/shard_map/ppermute | solution.py:20
  20.1 0.7 collective-permute-start.4
  20.8 1.5 %collective-permute-start.6 = (bf16[272,512]{1,0:T(8,128)(2,1)}, bf16[272,512]{1,0:T(8,128)(2,1)S(1)}, u32[]{:S(2)}, u32[]{:S(2)}) collective-permute-start(bf16[272,512]{1,0:T(8,128)(2,1)} %collective-permute-done.1.refs_9_), channel_id=1, source_target_pairs={{0,1},{1,0},{2,3},{3,2},{4,5},{5,4},{6,7},{7,6},{8,9},{9,8},{10,11... | collective-permute-start | bytes 835592 | tf_op jit(solution)/shard_map/ppermute | solution.py:20
  22.3 0.5 collective-permute-start.7
  22.9 1.6 %collective-permute-start.5 = (f32[8,128]{1,0:T(8,128)S(1)}, f32[8,128]{1,0:T(8,128)S(1)}, u32[]{:S(2)}, u32[]{:S(2)}) collective-permute-start(f32[8,128]{1,0:T(8,128)S(1)} %broadcast_maximum_fusion), channel_id=1, source_target_pairs={{0,2},{1,3},{2,0},{3,1},{4,6},{5,7},{6,4},{7,5},{8,10},{9,11},{10,... | collective-permute-start | bytes 12296 | tf_op jit(solution)/shard_map/ppermute | solution.py:20
  24.5 2.1 %collective-permute-done.5 = f32[8,128]{1,0:T(8,128)S(1)} collective-permute-done((f32[8,128]{1,0:T(8,128)S(1)}, f32[8,128]{1,0:T(8,128)S(1)}, u32[]{:S(2)}, u32[]{:S(2)}) %collective-permute-start.5) | collective-permute-done | bytes 4128 | tf_op jit(solution)/shard_map/ppermute | solution.py:20
  26.6 9.0 %collective-permute-done.4.refs_11_ = bf16[272,512]{1,0:T(8,128)(2,1)} collective-permute-done((bf16[272,512]{1,0:T(8,128)(2,1)S(1)}, bf16[272,512]{1,0:T(8,128)(2,1)}, u32[]{:S(2)}, u32[]{:S(2)}) %collective-permute-start.4) | collective-permute-done | bytes 278560 | tf_op jit(solution)/shard_map/ppermute | solution.py:20
  35.7 0.7 copy-done.14
  36.4 0.7 copy-done.15
  37.2 1.1 collective-permute-start.11
  38.5 1.6 %collective-permute-start.12 = (bf16[272,512]{1,0:T(8,128)(2,1)}, bf16[272,512]{1,0:T(8,128)(2,1)}, u32[]{:S(2)}, u32[]{:S(2)}) collective-permute-start(bf16[272,512]{1,0:T(8,128)(2,1)} %collective-permute-done.4.refs_11_), channel_id=1, source_target_pairs={{0,1},{1,0},{2,3},{3,2},{4,5},{5,4},{6,7},{7,6},{8,9},{9,8},{10,11... | collective-permute-start | bytes 835592 | tf_op jit(solution)/shard_map/ppermute | solution.py:20
  40.0 1.7 %collective-permute-done.11 = f32[8,128]{1,0:T(8,128)S(1)} collective-permute-done((f32[8,128]{1,0:T(8,128)S(1)}, f32[8,128]{1,0:T(8,128)S(1)}, u32[]{:S(2)}, u32[]{:S(2)}) %collective-permute-start.11) | collective-permute-done | bytes 4128 | tf_op jit(solution)/shard_map/ppermute | solution.py:20
  41.8 0.8 convert_add_fusion.2
  42.6 0.8 fusion.60
  43.4 1.2 collective-permute-done.10.refs_5_
  44.6 0.8 fusion.62
  45.4 0.8 convert_add_fusion
  46.3 1.4 collective-permute-done.12.refs_12_
  47.6 10.6 %scores.1 = (f32[8,4,512,128]{3,2,1,0:T(8,128)S(1)}, f32[80,128]{1,0:T(8,128)S(1)}, bf16[2176,512]{1,0:T(8,128)(2,1)S(1)}) custom-call(s32[256]{0:T(256)S(1)} %fusion.39.index, f32[32,128]{1,0:T(8,128)S(1)} %pad_maximum_fusion.2.refs_0_, f32[8,128]{1,0:T(8,128)S(1)} %max.15.refs_1_, bf16[1040,512]{1,0:T(8,128)(2,1)S(1)} %pad_maximum_fusion.refs_2_, ...), custom_call_target="tpu_custom_call" | custom-call | flops 1048576 | bytes 1048576 | tf_op jit(solution)/shard_map/scores/pallas_call | solution.py:273
  58.3 1.6 %collective-permute-start.14 = (f32[80,128]{1,0:T(8,128)S(1)}, f32[80,128]{1,0:T(8,128)S(1)}, u32[]{:S(2)}, u32[]{:S(2)}) collective-permute-start(f32[80,128]{1,0:T(8,128)S(1)} %get-tuple-element.71.refs_3_), channel_id=1, source_target_pairs={{0,16},{8,24},{16,0},{24,8},{1,17},{9,25},{17,1},{25,9},{2,18},{10... | collective-permute-start | bytes 122888 | tf_op jit(solution)/shard_map/ppermute | solution.py:20
  60.2 2.2 %collective-permute-done.14.refs_5_ = f32[80,128]{1,0:T(8,128)S(1)} collective-permute-done((f32[80,128]{1,0:T(8,128)S(1)}, f32[80,128]{1,0:T(8,128)S(1)}, u32[]{:S(2)}, u32[]{:S(2)}) %collective-permute-start.14) | collective-permute-done | bytes 40992 | tf_op jit(solution)/shard_map/ppermute | solution.py:20
  62.4 1.0 collective-permute-done.15.refs_6_
  63.4 4.4 %grads.1 = (bf16[8,512,128]{2,1,0:T(8,128)(2,1)S(1)}, bf16[8,3,512,128]{3,2,1,0:T(8,128)(2,1)S(1)}, f32[8,128]{1,0:T(8,128)S(1)}, f32[8,128]{1,0:T(8,128)S(1)}, ...) custom-call(s32[256]{0:T(256)S(1)} %fusion.39.index, ...), custom_call_target="tpu_custom_call" | custom-call | flops 1048576 | bytes 1048576 | tf_op jit(solution)/shard_map/grads/pallas_call | solution.py:273
  68.5 1.5 %collective-permute-start.17 = (f32[8,128]{1,0:T(8,128)S(1)}, f32[8,128]{1,0:T(8,128)S(1)}, u32[]{:S(2)}, u32[]{:S(2)}) collective-permute-start(f32[8,128]{1,0:T(8,128)S(1)} %get-tuple-element.75), channel_id=1, source_target_pairs={{0,1},{1,0},{2,3},{3,2},{4,5},{5,4},{6,7},{7,6},{8,9},{9,8},{10,11... | collective-permute-start | bytes 12296 | tf_op jit(solution)/shard_map/ppermute | solution.py:20
  69.9 0.5 slice.141
  71.2 7.4 %table_grads.1 = f32[2048,512]{1,0:T(8,128)S(1)} custom-call(s32[256]{0:T(256)S(1)} %fusion.39.index, bf16[8,512,128]{2,1,0:T(8,128)(2,1)S(1)} %get-tuple-element.90.refs_0_.near, bf16[8,3,512,128]{3,2,1,0:T(8,128)(2,1)S(1)} %get-tuple-element.73.refs_1_, bf16[1040,512]{1,0:T(8,128)(2,1)S(1)} %pad_maximum_fusion.refs_2_, ...), custom_call_target="tpu_custom_call" | custom-call | flops 1048576 | bytes 1048576 | tf_op jit(solution)/shard_map/table_grads/pallas_call | solution.py:273
  79.3 0.6 collective-permute-start.18
  79.9 0.9 collective-permute-start.21
  80.8 0.7 collective-permute-start.19
  81.5 2.9 %collective-permute-done.19 = f32[8,128]{1,0:T(8,128)S(1)} collective-permute-done((f32[8,128]{1,0:T(8,128)S(1)}, f32[8,128]{1,0:T(8,128)S(1)}, u32[]{:S(2)}, u32[]{:S(2)}) %collective-permute-start.19) | collective-permute-done | bytes 4128 | tf_op jit(solution)/shard_map/ppermute | solution.py:20
  84.4 1.8 %collective-permute-start.20 = (f32[8,128]{1,0:T(8,128)S(1)}, f32[8,128]{1,0:T(8,128)S(1)}, u32[]{:S(2)}, u32[]{:S(2)}) collective-permute-start(f32[8,128]{1,0:T(8,128)S(1)} %add.171), channel_id=1, source_target_pairs={{0,4},{1,5},{2,6},{3,7},{4,0},{5,1},{6,2},{7,3},{8,12},{9,13},{10,... | collective-permute-start | bytes 12296 | tf_op jit(solution)/shard_map/ppermute | solution.py:20
  86.2 2.7 %collective-permute-done.20 = f32[8,128]{1,0:T(8,128)S(1)} collective-permute-done((f32[8,128]{1,0:T(8,128)S(1)}, f32[8,128]{1,0:T(8,128)S(1)}, u32[]{:S(2)}, u32[]{:S(2)}) %collective-permute-start.20) | collective-permute-done | bytes 4128 | tf_op jit(solution)/shard_map/ppermute | solution.py:20
  88.9 4.2 %collective-permute-done.18 = f16[4,256,256]{2,1,0:T(8,128)(2,1)S(1)} collective-permute-done((f16[4,256,256]{2,1,0:T(8,128)(2,1)S(1)}, f16[4,256,256]{2,1,0:T(8,128)(2,1)S(1)}, u32[]{:S(2)}, u32[]{:S(2)}) %collective-permute-start.18) | collective-permute-done | bytes 524320 | tf_op jit(solution)/shard_map/ppermute | solution.py:20
  93.4 0.8 copy-done.10
  94.4 1.6 %collective-permute-start.26 = (f16[4,256,256]{2,1,0:T(8,128)(2,1)S(1)}, f16[4,256,256]{2,1,0:T(8,128)(2,1)S(1)}, u32[]{:S(2)}, u32[]{:S(2)}) collective-permute-start(f16[4,256,256]{2,1,0:T(8,128)(2,1)S(1)} %get-tuple-element.87), channel_id=1, source_target_pairs={{0,1},{1,0},{2,3},{3,2},{4,5},{5,4},{6,7},{7,6},{8,9},{9,8},{10,11... | collective-permute-start | bytes 1572872 | tf_op jit(solution)/shard_map/ppermute | solution.py:20
  95.9 0.9 collective-permute-start.27
  96.9 0.6 collective-permute-start.23
  97.5 1.6 %collective-permute-start.24 = (f16[256,256]{1,0:T(8,128)(2,1)S(1)}, f16[256,256]{1,0:T(8,128)(2,1)S(1)}, u32[]{:S(2)}, u32[]{:S(2)}) collective-permute-start(f16[256,256]{1,0:T(8,128)(2,1)S(1)} %get-tuple-element.123), channel_id=1, source_target_pairs={{0,4},{1,5},{2,6},{3,7},{4,0},{5,1},{6,2},{7,3},{8,12},{9,13},{10,... | collective-permute-start | bytes 393224 | tf_op jit(solution)/shard_map/ppermute | solution.py:20
  99.2 2.2 %collective-permute-start.25 = (f16[256,256]{1,0:T(8,128)(2,1)S(1)}, f16[256,256]{1,0:T(8,128)(2,1)S(1)}, u32[]{:S(2)}, u32[]{:S(2)}) collective-permute-start(f16[256,256]{1,0:T(8,128)(2,1)S(1)} %get-tuple-element.122), channel_id=1, source_target_pairs={{0,2},{1,3},{2,0},{3,1},{4,6},{5,7},{6,4},{7,5},{8,10},{9,11},{10,... | collective-permute-start | bytes 393224 | tf_op jit(solution)/shard_map/ppermute | solution.py:20
  101.4 3.8 %collective-permute-done.23 = f16[256,256]{1,0:T(8,128)(2,1)S(1)} collective-permute-done((f16[256,256]{1,0:T(8,128)(2,1)S(1)}, f16[256,256]{1,0:T(8,128)(2,1)S(1)}, u32[]{:S(2)}, u32[]{:S(2)}) %collective-permute-start.23) | collective-permute-done | bytes 131104 | tf_op jit(solution)/shard_map/ppermute | solution.py:20
  105.2 4.0 %collective-permute-done.24 = f16[256,256]{1,0:T(8,128)(2,1)S(1)} collective-permute-done((f16[256,256]{1,0:T(8,128)(2,1)S(1)}, f16[256,256]{1,0:T(8,128)(2,1)S(1)}, u32[]{:S(2)}, u32[]{:S(2)}) %collective-permute-start.24) | collective-permute-done | bytes 131104 | tf_op jit(solution)/shard_map/ppermute | solution.py:20
  109.3 1.2 fusion.54
  110.5 0.8 slice_bitcast_fusion.7
  111.3 2.2 %collective-permute-start.28 = (f16[256,256]{1,0:T(8,128)(2,1)}, f16[256,256]{1,0:T(8,128)(2,1)}, u32[]{:S(2)}, u32[]{:S(2)}) collective-permute-start(f16[256,256]{1,0:T(8,128)(2,1)} %get-tuple-element.118), channel_id=1, source_target_pairs={{0,6},{1,7},{2,4},{3,5},{4,2},{5,3},{6,0},{7,1},{8,14},{9,15},{10,... | collective-permute-start | bytes 393224 | tf_op jit(solution)/shard_map/ppermute | solution.py:20
  113.5 2.2 %collective-permute-start.30 = (f16[256,256]{1,0:T(8,128)(2,1)}, f16[256,256]{1,0:T(8,128)(2,1)}, u32[]{:S(2)}, u32[]{:S(2)}) collective-permute-start(f16[256,256]{1,0:T(8,128)(2,1)} %get-tuple-element.119), channel_id=1, source_target_pairs={{0,2},{1,3},{2,0},{3,1},{4,6},{5,7},{6,4},{7,5},{8,10},{9,11},{10,... | collective-permute-start | bytes 393224 | tf_op jit(solution)/shard_map/ppermute | solution.py:20
  116.2 1.2 copy-done.3
  117.4 1.2 copy-done.5
  118.7 2.6 %own_hidden_grads.1 = f32[1024,512]{1,0:T(8,128)S(1)} custom-call(s32[256]{0:T(256)S(1)} %fusion.39.index, bf16[8,512,128]{2,1,0:T(8,128)(2,1)S(1)} %copy-done.5, bf16[2176,512]{1,0:T(8,128)(2,1)S(1)} %copy-done.2, f32[8,128]{1,0:T(8,128)S(1)} %get-tuple-element.91.pos_grad, bf16[1024,512]{1,0:T(8,128)(2,1)S(1)} %bitcast.121), custom_call_target="tpu_custom_call" | custom-call | flops 1048576 | bytes 1048576 | tf_op jit(solution)/shard_map/own_hidden_grads/pallas_call | solution.py:273
  121.3 3.0 %collective-permute-done.29 = f16[256,256]{1,0:T(8,128)(2,1)} collective-permute-done((f16[256,256]{1,0:T(8,128)(2,1)}, f16[256,256]{1,0:T(8,128)(2,1)}, u32[]{:S(2)}, u32[]{:S(2)}) %collective-permute-start.29) | collective-permute-done | bytes 131104 | tf_op jit(solution)/shard_map/ppermute | solution.py:20
  124.3 1.2 fusion.14
  125.5 1.1 collective-permute-start.32
  126.6 1.9 %add_bitcast_fusion = f32[1,1024,512]{2,1,0:T(8,128)} fusion(f32[1024,512]{1,0:T(8,128)S(1)} %own_hidden_grads.1, f32[1024,512]{1,0:T(8,128)S(1)} %copy-done.7, f16[1024,256]{1,0:T(8,128)(2,1)S(1)} %copy-done.13, f16[1024,256]{1,0:T(8,128)(2,1)S(1)} %copy-done.11), kind=kLoop, calls=%fused_computation | loop fusion | flops 2621440 | bytes 7340032 | tf_op jit(solution)/shard_map/broadcast_in_dim | solution.py:377
  128.5 4.3 %collective-permute-done.32 = f16[256,512]{1,0:T(8,128)(2,1)S(1)} collective-permute-done((f16[256,512]{1,0:T(8,128)(2,1)S(1)}, f16[256,512]{1,0:T(8,128)(2,1)S(1)}, u32[]{:S(2)}, u32[]{:S(2)}) %collective-permute-start.32) | collective-permute-done | bytes 262176 | tf_op jit(solution)/shard_map/ppermute | solution.py:20
  133.3 1.1 collective-permute-done.33
  134.7 1.3 copy-done.8
  (115 shorter events, 5.1 us)
Async XLA Ops:
  0.6 1.2 copy-start
  1.9 10.5 %copy-start.17 = (s32[1,8,8]{2,1,0:T(8,128)S(1)}, s32[1,8,8]{2,1,0:T(8,128)}, u32[]{:S(2)}) copy-start(s32[1,8,8]{2,1,0:T(8,128)} %param.12) | copy-start | bytes 772
  1.9 11.2 %copy-start.16 = (s32[1,1024]{1,0:T(1,128)S(1)}, s32[1,1024]{1,0:T(1,128)}, u32[]{:S(2)}) copy-start(s32[1,1024]{1,0:T(1,128)} %param.11) | copy-start | bytes 12292
  2.1 18.0 %copy-start.9 = (bf16[272,512]{1,0:T(8,128)(2,1)}, bf16[272,512]{1,0:T(8,128)(2,1)S(1)}, u32[]{:S(2)}) copy-start(bf16[272,512]{1,0:T(8,128)(2,1)S(1)} %maximum_maximum_fusion.refs_7_) | copy-start | bytes 835588
  2.1 13.4 %copy-start.18 = (s32[1,5]{1,0:T(1,128)S(1)}, s32[1,5]{1,0:T(1,128)}, u32[]{:S(2)}) copy-start(s32[1,5]{1,0:T(1,128)} %param.13) | copy-start | bytes 64
  2.1 14.1 %collective-permute-start = (bf16[272,512]{1,0:T(8,128)(2,1)S(1)}, bf16[272,512]{1,0:T(8,128)(2,1)}, u32[]{:S(2)}, u32[]{:S(2)}) collective-permute-start(bf16[272,512]{1,0:T(8,128)(2,1)S(1)} %maximum_maximum_fusion.refs_7_), channel_id=1, source_target_pairs={{0,6},{1,7},{2,4},{3,5},{4,2},{5,3},{6,0},{7,1},{8,14},{9,15},{10,... | collective-permute-start | bytes 835592 | tf_op jit(solution)/shard_map/ppermute | solution.py:20
  7.3 12.8 %collective-permute-start.1 = (bf16[272,512]{1,0:T(8,128)(2,1)S(1)}, bf16[272,512]{1,0:T(8,128)(2,1)}, u32[]{:S(2)}, u32[]{:S(2)}) collective-permute-start(bf16[272,512]{1,0:T(8,128)(2,1)S(1)} %maximum_maximum_fusion.refs_7_), channel_id=1, source_target_pairs={{0,2},{1,3},{2,0},{3,1},{4,6},{5,7},{6,4},{7,5},{8,10},{9,11},{10,... | collective-permute-start | bytes 835592 | tf_op jit(solution)/shard_map/ppermute | solution.py:20
  7.3 12.8 %collective-permute-start.3 = (bf16[272,512]{1,0:T(8,128)(2,1)S(1)}, bf16[272,512]{1,0:T(8,128)(2,1)}, u32[]{:S(2)}, u32[]{:S(2)}) collective-permute-start(bf16[272,512]{1,0:T(8,128)(2,1)S(1)} %maximum_maximum_fusion.refs_7_), channel_id=1, source_target_pairs={{0,1},{1,0},{2,3},{3,2},{4,5},{5,4},{6,7},{7,6},{8,9},{9,8},{10,11... | collective-permute-start | bytes 835592 | tf_op jit(solution)/shard_map/ppermute | solution.py:20
  11.8 4.4 %collective-permute-start.2 = (f32[8,128]{1,0:T(8,128)S(1)}, f32[8,128]{1,0:T(8,128)S(1)}, u32[]{:S(2)}, u32[]{:S(2)}) collective-permute-start(f32[8,128]{1,0:T(8,128)S(1)} %broadcast_in_dim.29), channel_id=1, source_target_pairs={{0,1},{1,0},{2,3},{3,2},{4,5},{5,4},{6,7},{7,6},{8,9},{9,8},{10,11... | collective-permute-start | bytes 12296 | tf_op jit(solution)/shard_map/ppermute | solution.py:20
  13.9 27.8 %collective-permute-start.9 = (bf16[1040,512]{1,0:T(8,128)(2,1)S(1)}, bf16[1040,512]{1,0:T(8,128)(2,1)S(1)}, u32[]{:S(2)}, u32[]{:S(2)}) collective-permute-start(bf16[1040,512]{1,0:T(8,128)(2,1)S(1)} %pad_maximum_fusion.refs_2_), channel_id=1, source_target_pairs={{0,16},{8,24},{16,0},{24,8},{1,17},{9,25},{17,1},{25,9},{2,18},{10... | collective-permute-start | bytes 3194888 | tf_op jit(solution)/shard_map/ppermute | solution.py:20
  20.1 15.6 %collective-permute-start.4 = (bf16[272,512]{1,0:T(8,128)(2,1)S(1)}, bf16[272,512]{1,0:T(8,128)(2,1)}, u32[]{:S(2)}, u32[]{:S(2)}) collective-permute-start(bf16[272,512]{1,0:T(8,128)(2,1)S(1)} %maximum_maximum_fusion.refs_7_), channel_id=1, source_target_pairs={{0,4},{1,5},{2,6},{3,7},{4,0},{5,1},{6,2},{7,3},{8,12},{9,13},{10,... | collective-permute-start | bytes 835592 | tf_op jit(solution)/shard_map/ppermute | solution.py:20
  20.8 14.9 %collective-permute-start.6 = (bf16[272,512]{1,0:T(8,128)(2,1)}, bf16[272,512]{1,0:T(8,128)(2,1)S(1)}, u32[]{:S(2)}, u32[]{:S(2)}) collective-permute-start(bf16[272,512]{1,0:T(8,128)(2,1)} %collective-permute-done.1.refs_9_), channel_id=1, source_target_pairs={{0,1},{1,0},{2,3},{3,2},{4,5},{5,4},{6,7},{7,6},{8,9},{9,8},{10,11... | collective-permute-start | bytes 835592 | tf_op jit(solution)/shard_map/ppermute | solution.py:20
  22.3 14.1 %collective-permute-start.7 = (bf16[272,512]{1,0:T(8,128)(2,1)}, bf16[272,512]{1,0:T(8,128)(2,1)S(1)}, u32[]{:S(2)}, u32[]{:S(2)}) collective-permute-start(bf16[272,512]{1,0:T(8,128)(2,1)} %collective-permute-done.refs_13_), channel_id=1, source_target_pairs={{0,1},{1,0},{2,3},{3,2},{4,5},{5,4},{6,7},{7,6},{8,9},{9,8},{10,11... | collective-permute-start | bytes 835592 | tf_op jit(solution)/shard_map/ppermute | solution.py:20
  22.9 3.7 %collective-permute-start.5 = (f32[8,128]{1,0:T(8,128)S(1)}, f32[8,128]{1,0:T(8,128)S(1)}, u32[]{:S(2)}, u32[]{:S(2)}) collective-permute-start(f32[8,128]{1,0:T(8,128)S(1)} %broadcast_maximum_fusion), channel_id=1, source_target_pairs={{0,2},{1,3},{2,0},{3,1},{4,6},{5,7},{6,4},{7,5},{8,10},{9,11},{10,... | collective-permute-start | bytes 12296 | tf_op jit(solution)/shard_map/ppermute | solution.py:20
  35.6 0.7 copy-start.14
  36.4 0.7 copy-start.15
  37.1 4.7 %collective-permute-start.8 = (bf16[1040,512]{1,0:T(8,128)(2,1)S(1)}, bf16[1040,512]{1,0:T(8,128)(2,1)}, u32[]{:S(2)}, u32[]{:S(2)}) collective-permute-start(bf16[1040,512]{1,0:T(8,128)(2,1)S(1)} %pad_maximum_fusion.refs_2_), channel_id=1, source_target_pairs={{0,8},{8,0},{16,24},{24,16},{1,9},{9,1},{17,25},{25,17},{2,10},{10... | collective-permute-start | bytes 3194888 | tf_op jit(solution)/shard_map/ppermute | solution.py:20
  37.2 4.5 %collective-permute-start.11 = (f32[8,128]{1,0:T(8,128)S(1)}, f32[8,128]{1,0:T(8,128)S(1)}, u32[]{:S(2)}, u32[]{:S(2)}) collective-permute-start(f32[8,128]{1,0:T(8,128)S(1)} %max.14), channel_id=1, source_target_pairs={{0,4},{1,5},{2,6},{3,7},{4,0},{5,1},{6,2},{7,3},{8,12},{9,13},{10,... | collective-permute-start | bytes 12296 | tf_op jit(solution)/shard_map/ppermute | solution.py:20
  38.5 9.2 %collective-permute-start.12 = (bf16[272,512]{1,0:T(8,128)(2,1)}, bf16[272,512]{1,0:T(8,128)(2,1)}, u32[]{:S(2)}, u32[]{:S(2)}) collective-permute-start(bf16[272,512]{1,0:T(8,128)(2,1)} %collective-permute-done.4.refs_11_), channel_id=1, source_target_pairs={{0,1},{1,0},{2,3},{3,2},{4,5},{5,4},{6,7},{7,6},{8,9},{9,8},{10,11... | collective-permute-start | bytes 835592 | tf_op jit(solution)/shard_map/ppermute | solution.py:20
  41.7 2.9 %collective-permute-start.10 = (bf16[1040,512]{1,0:T(8,128)(2,1)S(1)}, bf16[1040,512]{1,0:T(8,128)(2,1)}, u32[]{:S(2)}, u32[]{:S(2)}) collective-permute-start(bf16[1040,512]{1,0:T(8,128)(2,1)S(1)} %collective-permute-done.9.refs_4_), channel_id=1, source_target_pairs={{0,8},{8,0},{16,24},{24,16},{1,9},{9,1},{17,25},{25,17},{2,10},{10... | collective-permute-start | bytes 3194888 | tf_op jit(solution)/shard_map/ppermute | solution.py:20
  58.2 9.7 %copy-start.1 = (bf16[2176,512]{1,0:T(8,128)(2,1)}, bf16[2176,512]{1,0:T(8,128)(2,1)S(1)}, u32[]{:S(2)}) copy-start(bf16[2176,512]{1,0:T(8,128)(2,1)S(1)} %get-tuple-element.70.refs_2_.table) | copy-start | bytes 6684676
  58.2 1.9 %collective-permute-start.13 = (f32[80,128]{1,0:T(8,128)S(1)}, f32[80,128]{1,0:T(8,128)S(1)}, u32[]{:S(2)}, u32[]{:S(2)}) collective-permute-start(f32[80,128]{1,0:T(8,128)S(1)} %get-tuple-element.71.refs_3_), channel_id=1, source_target_pairs={{0,8},{8,0},{16,24},{24,16},{1,9},{9,1},{17,25},{25,17},{2,10},{10... | collective-permute-start | bytes 122888 | tf_op jit(solution)/shard_map/ppermute | solution.py:20
  58.3 4.1 %collective-permute-start.14 = (f32[80,128]{1,0:T(8,128)S(1)}, f32[80,128]{1,0:T(8,128)S(1)}, u32[]{:S(2)}, u32[]{:S(2)}) collective-permute-start(f32[80,128]{1,0:T(8,128)S(1)} %get-tuple-element.71.refs_3_), channel_id=1, source_target_pairs={{0,16},{8,24},{16,0},{24,8},{1,17},{9,25},{17,1},{25,9},{2,18},{10... | collective-permute-start | bytes 122888 | tf_op jit(solution)/shard_map/ppermute | solution.py:20
  59.9 3.5 %collective-permute-start.15 = (f32[80,128]{1,0:T(8,128)S(1)}, f32[80,128]{1,0:T(8,128)S(1)}, u32[]{:S(2)}, u32[]{:S(2)}) collective-permute-start(f32[80,128]{1,0:T(8,128)S(1)} %get-tuple-element.71.refs_3_), channel_id=1, source_target_pairs={{0,24},{8,16},{16,8},{24,0},{1,25},{9,17},{17,9},{25,1},{2,26},{10... | collective-permute-start | bytes 122888 | tf_op jit(solution)/shard_map/ppermute | solution.py:20
  67.9 10.7 %copy-start.4 = (bf16[8,512,128]{2,1,0:T(8,128)(2,1)}, bf16[8,512,128]{2,1,0:T(8,128)(2,1)S(1)}, u32[]{:S(2)}) copy-start(bf16[8,512,128]{2,1,0:T(8,128)(2,1)S(1)} %get-tuple-element.90.refs_0_.near) | copy-start | bytes 3145732
  67.9 10.7 %collective-permute-start.16 = (f32[1024,512]{1,0:T(8,128)S(1)}, f32[1024,512]{1,0:T(8,128)S(1)}, u32[]{:S(2)}, u32[]{:S(2)}) collective-permute-start(f32[1024,512]{1,0:T(8,128)S(1)} %get-tuple-element.74), channel_id=1, source_target_pairs={{0,8},{8,0},{16,24},{24,16},{1,9},{9,1},{17,25},{25,17},{2,10},{10... | collective-permute-start | bytes 6291464 | tf_op jit(solution)/shard_map/ppermute | solution.py:20
  68.1 20.8 %collective-permute-start.22 = (f32[1024,512]{1,0:T(8,128)S(1)}, f32[1024,512]{1,0:T(8,128)S(1)}, u32[]{:S(2)}, u32[]{:S(2)}) collective-permute-start(f32[1024,512]{1,0:T(8,128)S(1)} %get-tuple-element.83), channel_id=1, source_target_pairs={{0,8},{8,0},{16,24},{24,16},{1,9},{9,1},{17,25},{25,17},{2,10},{10... | collective-permute-start | bytes 6291464 | tf_op jit(solution)/shard_map/ppermute | solution.py:20
  68.5 10.2 %collective-permute-start.17 = (f32[8,128]{1,0:T(8,128)S(1)}, f32[8,128]{1,0:T(8,128)S(1)}, u32[]{:S(2)}, u32[]{:S(2)}) collective-permute-start(f32[8,128]{1,0:T(8,128)S(1)} %get-tuple-element.75), channel_id=1, source_target_pairs={{0,1},{1,0},{2,3},{3,2},{4,5},{5,4},{6,7},{7,6},{8,9},{9,8},{10,11... | collective-permute-start | bytes 12296 | tf_op jit(solution)/shard_map/ppermute | solution.py:20
  79.3 13.8 %collective-permute-start.18 = (f16[4,256,256]{2,1,0:T(8,128)(2,1)S(1)}, f16[4,256,256]{2,1,0:T(8,128)(2,1)S(1)}, u32[]{:S(2)}, u32[]{:S(2)}) collective-permute-start(f16[4,256,256]{2,1,0:T(8,128)(2,1)S(1)} %get-tuple-element.80), channel_id=1, source_target_pairs={{0,1},{1,0},{2,3},{3,2},{4,5},{5,4},{6,7},{7,6},{8,9},{9,8},{10,11... | collective-permute-start | bytes 1572872 | tf_op jit(solution)/shard_map/ppermute | solution.py:20
  79.9 13.4 %collective-permute-start.21 = (f16[1024,256]{1,0:T(8,128)(2,1)S(1)}, f16[1024,256]{1,0:T(8,128)(2,1)S(1)}, u32[]{:S(2)}, u32[]{:S(2)}) collective-permute-start(f16[1024,256]{1,0:T(8,128)(2,1)S(1)} %get-tuple-element.82), channel_id=1, source_target_pairs={{0,16},{8,24},{16,0},{24,8},{1,17},{9,25},{17,1},{25,9},{2,18},{10... | collective-permute-start | bytes 1572872 | tf_op jit(solution)/shard_map/ppermute | solution.py:20
  80.8 3.6 %collective-permute-start.19 = (f32[8,128]{1,0:T(8,128)S(1)}, f32[8,128]{1,0:T(8,128)S(1)}, u32[]{:S(2)}, u32[]{:S(2)}) collective-permute-start(f32[8,128]{1,0:T(8,128)S(1)} %add.170), channel_id=1, source_target_pairs={{0,2},{1,3},{2,0},{3,1},{4,6},{5,7},{6,4},{7,5},{8,10},{9,11},{10,... | collective-permute-start | bytes 12296 | tf_op jit(solution)/shard_map/ppermute | solution.py:20
  84.4 4.5 %collective-permute-start.20 = (f32[8,128]{1,0:T(8,128)S(1)}, f32[8,128]{1,0:T(8,128)S(1)}, u32[]{:S(2)}, u32[]{:S(2)}) collective-permute-start(f32[8,128]{1,0:T(8,128)S(1)} %add.171), channel_id=1, source_target_pairs={{0,4},{1,5},{2,6},{3,7},{4,0},{5,1},{6,2},{7,3},{8,12},{9,13},{10,... | collective-permute-start | bytes 12296 | tf_op jit(solution)/shard_map/ppermute | solution.py:20
  88.9 20.4 %copy-start.6 = (f32[1024,512]{1,0:T(8,128)}, f32[1024,512]{1,0:T(8,128)S(1)}, u32[]{:S(2)}) copy-start(f32[1024,512]{1,0:T(8,128)S(1)} %collective-permute-done.22) | copy-start | bytes 6291460
  93.4 0.8 copy-start.10
  94.4 14.9 %collective-permute-start.26 = (f16[4,256,256]{2,1,0:T(8,128)(2,1)S(1)}, f16[4,256,256]{2,1,0:T(8,128)(2,1)S(1)}, u32[]{:S(2)}, u32[]{:S(2)}) collective-permute-start(f16[4,256,256]{2,1,0:T(8,128)(2,1)S(1)} %get-tuple-element.87), channel_id=1, source_target_pairs={{0,1},{1,0},{2,3},{3,2},{4,5},{5,4},{6,7},{7,6},{8,9},{9,8},{10,11... | collective-permute-start | bytes 1572872 | tf_op jit(solution)/shard_map/ppermute | solution.py:20
  95.9 13.4 %collective-permute-start.27 = (f16[1024,256]{1,0:T(8,128)(2,1)S(1)}, f16[1024,256]{1,0:T(8,128)(2,1)S(1)}, u32[]{:S(2)}, u32[]{:S(2)}) collective-permute-start(f16[1024,256]{1,0:T(8,128)(2,1)S(1)} %get-tuple-element.89), channel_id=1, source_target_pairs={{0,16},{8,24},{16,0},{24,8},{1,17},{9,25},{17,1},{25,9},{2,18},{10... | collective-permute-start | bytes 1572872 | tf_op jit(solution)/shard_map/ppermute | solution.py:20
  96.9 8.3 %collective-permute-start.23 = (f16[256,256]{1,0:T(8,128)(2,1)S(1)}, f16[256,256]{1,0:T(8,128)(2,1)S(1)}, u32[]{:S(2)}, u32[]{:S(2)}) collective-permute-start(f16[256,256]{1,0:T(8,128)(2,1)S(1)} %get-tuple-element.121), channel_id=1, source_target_pairs={{0,6},{1,7},{2,4},{3,5},{4,2},{5,3},{6,0},{7,1},{8,14},{9,15},{10,... | collective-permute-start | bytes 393224 | tf_op jit(solution)/shard_map/ppermute | solution.py:20
  97.5 11.7 %collective-permute-start.24 = (f16[256,256]{1,0:T(8,128)(2,1)S(1)}, f16[256,256]{1,0:T(8,128)(2,1)S(1)}, u32[]{:S(2)}, u32[]{:S(2)}) collective-permute-start(f16[256,256]{1,0:T(8,128)(2,1)S(1)} %get-tuple-element.123), channel_id=1, source_target_pairs={{0,4},{1,5},{2,6},{3,7},{4,0},{5,1},{6,2},{7,3},{8,12},{9,13},{10,... | collective-permute-start | bytes 393224 | tf_op jit(solution)/shard_map/ppermute | solution.py:20
  99.2 10.1 %collective-permute-start.25 = (f16[256,256]{1,0:T(8,128)(2,1)S(1)}, f16[256,256]{1,0:T(8,128)(2,1)S(1)}, u32[]{:S(2)}, u32[]{:S(2)}) collective-permute-start(f16[256,256]{1,0:T(8,128)(2,1)S(1)} %get-tuple-element.122), channel_id=1, source_target_pairs={{0,2},{1,3},{2,0},{3,1},{4,6},{5,7},{6,4},{7,5},{8,10},{9,11},{10,... | collective-permute-start | bytes 393224 | tf_op jit(solution)/shard_map/ppermute | solution.py:20
  109.3 6.9 %copy-start.2 = (bf16[2176,512]{1,0:T(8,128)(2,1)S(1)}, bf16[2176,512]{1,0:T(8,128)(2,1)}, u32[]{:S(2)}) copy-start(bf16[2176,512]{1,0:T(8,128)(2,1)} %copy-done.1) | copy-start | bytes 6684676
  109.3 2.0 %copy-start.12 = (f16[1024,256]{1,0:T(8,128)(2,1)}, f16[1024,256]{1,0:T(8,128)(2,1)S(1)}, u32[]{:S(2)}) copy-start(f16[1024,256]{1,0:T(8,128)(2,1)S(1)} %collective-permute-done.27) | copy-start | bytes 1572868
  111.3 10.0 %collective-permute-start.28 = (f16[256,256]{1,0:T(8,128)(2,1)}, f16[256,256]{1,0:T(8,128)(2,1)}, u32[]{:S(2)}, u32[]{:S(2)}) collective-permute-start(f16[256,256]{1,0:T(8,128)(2,1)} %get-tuple-element.118), channel_id=1, source_target_pairs={{0,6},{1,7},{2,4},{3,5},{4,2},{5,3},{6,0},{7,1},{8,14},{9,15},{10,... | collective-permute-start | bytes 393224 | tf_op jit(solution)/shard_map/ppermute | solution.py:20
  113.5 10.8 %collective-permute-start.29 = (f16[256,256]{1,0:T(8,128)(2,1)}, f16[256,256]{1,0:T(8,128)(2,1)}, u32[]{:S(2)}, u32[]{:S(2)}) collective-permute-start(f16[256,256]{1,0:T(8,128)(2,1)} %get-tuple-element.120), channel_id=1, source_target_pairs={{0,4},{1,5},{2,6},{3,7},{4,0},{5,1},{6,2},{7,3},{8,12},{9,13},{10,... | collective-permute-start | bytes 393224 | tf_op jit(solution)/shard_map/ppermute | solution.py:20
  113.5 10.8 %collective-permute-start.30 = (f16[256,256]{1,0:T(8,128)(2,1)}, f16[256,256]{1,0:T(8,128)(2,1)}, u32[]{:S(2)}, u32[]{:S(2)}) collective-permute-start(f16[256,256]{1,0:T(8,128)(2,1)} %get-tuple-element.119), channel_id=1, source_target_pairs={{0,2},{1,3},{2,0},{3,1},{4,6},{5,7},{6,4},{7,5},{8,10},{9,11},{10,... | collective-permute-start | bytes 393224 | tf_op jit(solution)/shard_map/ppermute | solution.py:20
  116.2 1.2 copy-start.3
  117.4 1.2 copy-start.5
  118.7 7.9 %copy-start.11 = (f16[1024,256]{1,0:T(8,128)(2,1)S(1)}, f16[1024,256]{1,0:T(8,128)(2,1)}, u32[]{:S(2)}) copy-start(f16[1024,256]{1,0:T(8,128)(2,1)} %copy-done.10) | copy-start | bytes 1572868
  118.7 7.9 %copy-start.13 = (f16[1024,256]{1,0:T(8,128)(2,1)S(1)}, f16[1024,256]{1,0:T(8,128)(2,1)}, u32[]{:S(2)}) copy-start(f16[1024,256]{1,0:T(8,128)(2,1)} %copy-done.12) | copy-start | bytes 1572868
  121.3 5.3 %copy-start.7 = (f32[1024,512]{1,0:T(8,128)S(1)}, f32[1024,512]{1,0:T(8,128)}, u32[]{:S(2)}) copy-start(f32[1024,512]{1,0:T(8,128)} %copy-done.6) | copy-start | bytes 6291460
  125.5 7.3 %collective-permute-start.32 = (f16[256,512]{1,0:T(8,128)(2,1)S(1)}, f16[256,512]{1,0:T(8,128)(2,1)S(1)}, u32[]{:S(2)}, u32[]{:S(2)}) collective-permute-start(f16[256,512]{1,0:T(8,128)(2,1)S(1)} %get-tuple-element.116), channel_id=1, source_target_pairs={{0,16},{8,24},{16,0},{24,8},{1,17},{9,25},{17,1},{25,9},{2,18},{10... | collective-permute-start | bytes 786440 | tf_op jit(solution)/shard_map/ppermute | solution.py:20
  126.6 6.7 %collective-permute-start.31 = (f32[256,512]{1,0:T(8,128)S(1)}, f32[256,512]{1,0:T(8,128)S(1)}, u32[]{:S(2)}, u32[]{:S(2)}) collective-permute-start(f32[256,512]{1,0:T(8,128)S(1)} %get-tuple-element.117), channel_id=1, source_target_pairs={{0,8},{8,0},{16,24},{24,16},{1,9},{9,1},{17,25},{25,17},{2,10},{10... | collective-permute-start | bytes 1572872 | tf_op jit(solution)/shard_map/ppermute | solution.py:20
  132.8 1.5 %collective-permute-start.33 = (f16[256,512]{1,0:T(8,128)(2,1)S(1)}, f16[256,512]{1,0:T(8,128)(2,1)S(1)}, u32[]{:S(2)}, u32[]{:S(2)}) collective-permute-start(f16[256,512]{1,0:T(8,128)(2,1)S(1)} %collective-permute-done.32), channel_id=1, source_target_pairs={{0,8},{8,0},{16,24},{24,16},{1,9},{9,1},{17,25},{25,17},{2,10},{10... | collective-permute-start | bytes 786440 | tf_op jit(solution)/shard_map/ppermute | solution.py:20
  134.7 1.3 copy-start.8

commit v3 on v2

--- a/solution.py
+++ b/solution.py
@@ -50,21 +50,26 @@
 
 def score_kernel(dims, index, *refs):
     peers, blocks, picks, users, per_piece, slab = dims
-    labels, top, narrows = refs[0], refs[1], refs[2:2 + peers]
-    target_from, pieces = refs[2 + peers], refs[3 + peers:-7]
+    labels, narrows = refs[0], refs[1:1 + peers]
+    target_from, pieces = refs[1 + peers], refs[2 + peers:-7]
     scores, stats, table, items, target, sems, target_sem = refs[-7:]
     rows = per_piece * slab
     stride = rows + HEAD
     kept = 2 * peers * blocks
 
-    copies = [pltpu.make_async_copy(target_from, target, target_sem)]
-    for k, piece in enumerate(pieces):
-        copies.append(pltpu.make_async_copy(piece, table.at[pl.ds(k * stride, stride)], sems.at[k]))
+    target_copy = pltpu.make_async_copy(target_from, target, target_sem)
+    target_copy.start()
+    copies = [
+        pltpu.make_async_copy(piece, table.at[pl.ds(k * stride, stride)], sems.at[k])
+        for k, piece in enumerate(pieces)
+    ]
     for copy in copies:
         copy.start()
     place = lax.broadcasted_iota(jnp.int32, (HEAD, PB), 0)
     units = jnp.where(place == 0, float(ID_BASE), jnp.where(place == 1, 1.0, 0.0)).astype(jnp.bfloat16)
-    stats[pl.ds(kept + blocks, 8), :] = top[...]
+    top = [narrow[narrow.shape[0] - HEAD:, :PB].astype(jnp.float32)[HEAD - 1:] for narrow in narrows]
+    stats[pl.ds(kept + blocks, 8), :] = jnp.broadcast_to(functools.reduce(jnp.maximum, top), (8, PB))
+    target_copy.wait()
     for copy in copies:
         copy.wait()
     for k in range(users):
@@ -107,8 +112,8 @@
     scores, weights, table = refs[:3]
     stats = refs[3:3 + peers]
     outs = refs[3 + peers:]
-    near, far, pos_grad, loss, bound = outs[:5]
-    hiddens, (peaks, ratios) = outs[5:4 + peers], outs[4 + peers:]
+    near, far, pos_grad, word = outs[:4]
+    hiddens, (peaks, ratios) = outs[4:3 + peers], outs[3 + peers:]
     kept = 2 * peers * blocks
     stride = per_piece * slab + HEAD
 
@@ -125,8 +130,9 @@
         terms.append(weight * (peak + jnp.log(total) - positive))
         if r == 0:
             pos_grad[...] = weight * factor * (jnp.exp(positive - peak) / total - 1.0)
-    loss[...] = jnp.broadcast_to(jnp.sum(tree_sum(terms), keepdims=True) * factor, loss.shape)
-    bound[...] = functools.reduce(jnp.maximum, [s[pl.ds(kept + blocks, 8), :] for s in stats])
+    word[:4, :] = jnp.broadcast_to(jnp.sum(tree_sum(terms), keepdims=True) * factor, (4, word.shape[1]))
+    top = jnp.maximum(stats[0][pl.ds(kept + blocks, 4), :], 1e-30)
+    word[4:, :] = top
 
     def advance(step, _):
         span = pl.ds(pl.multiple_of(step * PB, PB), PB)
@@ -214,31 +220,28 @@
     spare = jnp.zeros((HEAD - 2, features), bf16)
     piece = jnp.concatenate([own_rows.reshape(rows, features)] + halves(own_ids) + [spare])
 
-    notes = jnp.concatenate(halves(labels) + halves(chosen))
-    notes = jnp.pad(notes, ((0, -notes.shape[0] % 16), (0, 0)))
-    packed = jnp.concatenate([narrow, notes])
-    top = jnp.broadcast_to(largest.astype(f32), (8, PB))
-
-    pairs = users // 2
-    batches = [[pairs - 1] + list(range(1, pairs // 2)), list(range(pairs // 2, pairs - 1))]
+    notes = halves(labels) + halves(chosen)
+    spare = -(sum(note.shape[0] for note in notes) + 1) % HEAD
+    notes += [jnp.zeros((spare, features), bf16), jnp.broadcast_to(largest, (1, features))]
+    packed = jnp.concatenate([narrow] + notes)
+
     pieces = {0: piece, 1: swap(piece, "users", 1)}
     states = {0: packed}
     for q in range(2, peers, 2):
         states[q] = swap(packed, "seq", q)
-    top = jnp.maximum(top, swap(top, "users", 1))
-    held = piece
-    for turn, batch in enumerate(batches):
-        came = [swap(held, "users", 2 * k) for k in batch]
-        came, top, pieces, held = lax.optimization_barrier((came, top, pieces, piece))
-        for k, part in zip(batch, came):
-            pieces[2 * k] = part
-            pieces[2 * k + 1] = swap(part, "users", 1)
-        top = jnp.maximum(top, swap(top, "users", 2 << turn))
-    mask = 2 << len(batches)
-    while mask < users:
-        top = jnp.maximum(top, swap(top, "users", mask))
-        mask *= 2
-    own, _ = lax.optimization_barrier((packed, came))
+    pairs = users // 2
+    if pairs == 4:
+        pieces[4], pieces[2] = swap(piece, "users", 4), swap(piece, "users", 2)
+        pieces = lax.optimization_barrier(pieces)
+        pieces[6], pieces[5] = swap(pieces[4], "users", 2), swap(pieces[4], "users", 1)
+        pieces = lax.optimization_barrier(pieces)
+        own, came = lax.optimization_barrier((packed, pieces[6]))
+        pieces[7], pieces[3] = swap(pieces[6], "users", 1), swap(pieces[1], "users", 2)
+    else:
+        for q in range(2, users, 2):
+            pieces[q] = swap(piece, "users", q)
+            pieces[q + 1] = swap(pieces[q], "users", 1)
+        own = packed
     states[1] = swap(own, "seq", 1)
     for q in range(2, peers, 2):
         states[q + 1] = swap(states[q], "seq", 1)
@@ -258,7 +261,7 @@
     owners = peer ^ jnp.arange(peers, dtype=jnp.int32)
     positions = owners[:, None] * length + jnp.arange(length, dtype=jnp.int32)[None, :]
     weights = history_weights(offsets[0], positions).reshape(peers * blocks, PB)
-    weights, label_rows, index, top = lax.optimization_barrier((weights, label_rows, index, top))
+    weights, label_rows, index = lax.optimization_barrier((weights, label_rows, index))
 
     dims = (peers, blocks, picks, users, per_piece, slab)
     half = features // 2
@@ -288,93 +291,126 @@
             pltpu.SemaphoreType.DMA((users,)),
             pltpu.SemaphoreType.DMA,
         ],
-        index, label_rows, top, *narrows, target[0], *pieces, unplaced=1 + users,
+        index, label_rows, *narrows, target[0], *pieces, unplaced=1 + users,
     )
     all_stats = [stats] + [swap(stats, "seq", q) for q in range(1, peers)]
 
     state_out = ((length, features), f32)
-    near, far, pos_grad, loss, bound, *hiddens = call(
+    near, far, pos_grad, word, *hiddens = call(
         functools.partial(grad_kernel, dims + (factor,)), "grads",
         [
             ((blocks, wide, PB), bf16),
             ((blocks, peers - 1, wide, PB), bf16),
             ((blocks, PB), f32),
             ((8, PB), f32),
-            ((8, PB), f32),
         ] + [state_out] * (peers - 1),
         [pltpu.VMEM((peers * blocks, PB), f32)] * 2,
         index, scores, weights, table, *all_stats,
     )
+
+    def meet(ours, theirs):
+        row = lax.broadcasted_iota(jnp.int32, ours.shape, 0)
+        return jnp.where(row < 4, ours + theirs, jnp.maximum(ours, theirs))
+
     from_core = [swap(hiddens[q], "seq", 1) for q in range(2, peers, 2)]
-    loss_arrived = swap(loss, "users", 1)
+    partner_word = swap(word, "users", 1)
     (partial,) = call(
         functools.partial(table_kernel, dims), "table_grads", [((users * rows, features), f32)], [],
         index, near, far, *narrows,
     )
-    partial, from_core, loss_arrived = lax.optimization_barrier((partial, from_core, loss_arrived))
-
-    ceiling = jnp.maximum(bound[0, 0], 1e-30)
-    scale, back = 16384.0 / ceiling, ceiling / 16384.0
-
-    parts = partial.reshape(pairs, 2, rows, features)
+    partial, from_core, partner_word = lax.optimization_barrier((partial, from_core, partner_word))
+
+    hidden_scale = 16384.0 / factor
+
+    parts = partial.reshape(users, rows, features)
     halved = [slice(0, half), slice(half, features)]
 
-    def with_partner(lanes, arrived):
-        sums = parts[:, 0, :, lanes] * scale + arrived.astype(f32)
-        return sums[0], sums.astype(jnp.float16)
-
-    def with_owners(owned, sent):
-        for k in reversed(range(1, pairs)):
-            owned = owned + swap(sent[k], "users", 2 * k).astype(f32)
-        return owned
-
-    hidden_scale = 16384.0 / factor
-    hidden_coded = [
-        [((hiddens[2 * k + 1][:, lanes] + part[:, lanes]) * hidden_scale).astype(jnp.float16) for lanes in halved]
-        for k, part in enumerate(from_core)
-    ]
-    first_coded, second_coded = [(parts[:, 1, :, lanes] * scale).astype(jnp.float16) for lanes in halved]
-    first_coded, hidden_coded = lax.optimization_barrier((first_coded, hidden_coded))
-    hidden_arrived = [[swap(two[0], "seq", 2 * k + 2)] for k, two in enumerate(hidden_coded)]
-    first_arrived = swap(first_coded, "users", 1)
-    own_core = swap(hiddens[0], "seq", 1)
-    loss = loss + loss_arrived
-    mask = 2
-    while mask < users:
-        loss = loss + swap(loss, "users", mask)
-        mask *= 2
-    first_arrived, loss, second_coded, hidden_arrived, own_core, hidden_coded = lax.optimization_barrier(
-        (first_arrived, loss, second_coded, hidden_arrived, own_core, hidden_coded)
-    )
-    second_arrived = swap(second_coded, "users", 1)
-    for k, two in enumerate(hidden_coded):
-        hidden_arrived[k].append(swap(two[1], "seq", 2 * k + 2))
-    owned_first, sent_first = with_partner(halved[0], first_arrived)
-    owned_first = with_owners(owned_first, sent_first)
-    owned_first, second_arrived, near, hidden_arrived = lax.optimization_barrier(
-        (owned_first, second_arrived, near, hidden_arrived)
-    )
-    owned_second, sent_second = with_partner(halved[1], second_arrived)
-    owned_second = with_owners(owned_second, sent_second)
-    (own_hidden,) = call(
-        functools.partial(hidden_kernel, dims), "own_hidden_grads", [state_out], [],
-        index, near, table, pos_grad, target[0],
-    )
-    grad_hidden = own_hidden + own_core
-    for two in hidden_arrived:
-        grad_hidden = grad_hidden + jnp.concatenate(two, axis=1).astype(f32) * (1.0 / hidden_scale)
-    owned = jnp.concatenate([owned_first, owned_second], axis=1)
-    loss = loss[0, 0]
+    def coded(sums, bound):
+        return (sums * (16384.0 / bound)).astype(jnp.float16)
+
+    def added(sums, *arrived):
+        for part, bound in arrived:
+            sums = sums + part.astype(f32) * (bound / 16384.0)
+        return sums
+
+    def bound_of(word):
+        row = jnp.maximum(word[4:5], 1e-30)
+        return jnp.concatenate([row] * (features // PB), axis=1)
+
+    def coded_hiddens(lanes):
+        return [
+            ((hiddens[2 * k + 1][:, lanes] + part[:, lanes]) * hidden_scale).astype(jnp.float16)
+            for k, part in enumerate(from_core)
+        ]
+
+    def with_far(coded):
+        return [swap(part, "seq", 2 * k + 2) for k, part in enumerate(coded)]
+
+    word = meet(word, partner_word)
+    if pairs == 4:
+        pair_bound = bound_of(word)
+        sent, hidden_coded = lax.optimization_barrier(
+            ([coded(parts[7], pair_bound), coded(parts[3], pair_bound)], coded_hiddens(halved[0]))
+        )
+        from_pair, from_line = swap(sent[0], "users", 1), swap(sent[1], "users", 2)
+        hidden_arrived = [with_far(hidden_coded)]
+        line_word = swap(word, "users", 2)
+        own_core = swap(hiddens[0], "seq", 1)
+        from_pair, from_line, line_word = lax.optimization_barrier((from_pair, from_line, line_word))
+        line_bound, word = bound_of(line_word), meet(word, line_word)
+        four_bound = bound_of(word)
+        pair_sum = added(parts[1], (from_line, line_bound))
+        sent = [coded(added(parts[6], (from_pair, pair_bound)), four_bound), coded(parts[5], four_bound)]
+
+        from_line, from_pair = swap(sent[0], "users", 2), swap(sent[1], "users", 1)
+        far_word = swap(word, "users", 4)
+        from_pair, from_line, far_word, hidden_arrived, own_core, hidden_coded, near = lax.optimization_barrier(
+            (from_pair, from_line, far_word, hidden_arrived, own_core, coded_hiddens(halved[1]), near)
+        )
+        word = meet(word, far_word)
+        top = bound_of(word)
+        far_sum = added(parts[4], (from_line, four_bound), (from_pair, four_bound))
+        sent = [coded(far_sum, top), coded(parts[2], top), coded(pair_sum, top)]
+
+        arrived = [swap(sent[0], "users", 4), swap(sent[1], "users", 2), swap(sent[2], "users", 1)]
+        hidden_arrived.append(with_far(hidden_coded))
+        (own_hidden,) = call(
+            functools.partial(hidden_kernel, dims), "own_hidden_grads", [state_out], [],
+            index, near, table, pos_grad, target[0],
+        )
+        arrived, own_hidden, hidden_arrived = lax.optimization_barrier((arrived, own_hidden, hidden_arrived))
+        owned = added(parts[0], *[(part, top) for part in arrived])
+    else:
+        mask = 2
+        while mask < users:
+            word = meet(word, swap(word, "users", mask))
+            mask *= 2
+        top = bound_of(word)
+        owned = parts[0]
+        for q in range(0, users, 2):
+            sums = added(parts[q], (swap(coded(parts[q + 1], top), "users", 1), top))
+            owned = sums if q == 0 else added(owned, (swap(coded(sums, top), "users", q), top))
+        hidden_arrived = [with_far(coded_hiddens(lanes)) for lanes in halved]
+        own_core = swap(hiddens[0], "seq", 1)
+        (own_hidden,) = call(
+            functools.partial(hidden_kernel, dims), "own_hidden_grads", [state_out], [],
+            index, near, table, pos_grad, target[0],
+        )
 
     quarters = {0: owned, 1: swap(owned, "seq", 1)}
     for q in range(2, peers, 2):
-        coded = swap(owned.astype(jnp.float16), "seq", q)
-        quarters[q], quarters[q + 1] = coded.astype(f32), swap(coded, "seq", 1).astype(f32)
+        coded_owned = swap(coded(owned, top), "seq", q)
+        quarters[q] = added(0.0, (coded_owned, top))
+        quarters[q + 1] = added(0.0, (swap(coded_owned, "seq", 1), top))
+    grad_hidden = own_hidden + own_core
+    for k in range(peers // 2 - 1):
+        part = jnp.concatenate([lanes[k] for lanes in hidden_arrived], axis=1)
+        grad_hidden = grad_hidden + part.astype(f32) * (1.0 / hidden_scale)
     grad_table = jnp.zeros((per_piece, peers, slab, features), f32)
     for q in range(peers):
-        quarter = (quarters[q] * back).reshape(per_piece, 1, slab, features)
+        quarter = quarters[q].reshape(per_piece, 1, slab, features)
         grad_table = lax.dynamic_update_slice_in_dim(grad_table, quarter, peer ^ q, axis=1)
-    return loss, grad_hidden[None], grad_table.reshape(pool_table.shape)
+    return word[0, 0], grad_hidden[None], grad_table.reshape(pool_table.shape)
 
 
 def solution(mesh):

time: 137 us -> 124 us (0.905)
  starting transfers between devices: 36.2 us -> 27 us
  local copies, waits for them, and re-layouts: 12.6 us -> 9.76 us
  between operations: 2.49 us -> 1.03 us
    ppermute x34 -> x30, starting transfers between devices: 36.2 us -> 27 us  [swap(): return lax.ppermute(array, axis, [(i, i ^ mask) for i in range(count)])]
    unnamed x39 -> x19, local copies, waits for them, and re-layouts: 6.84 us -> 2.11 us
    dynamic_update_slice x3 -> x4, local copies, waits for them, and re-layouts: 0.14 us -> 2.26 us  [per_device(): lax.dynamic_update_slice_in_dim(grad_table, quarter, peer ^ q, axis=1)]
    broadcast_in_dim x1, other arithmetic: 1.91 us -> 3.73 us  [per_device(): return (word[0, 0], grad_hidden[None], grad_table.reshape(pool_table.shape))]
    ppermute x34 -> x30, waiting for transfers between devices: 48.8 us -> 48.3 us  [swap(): return lax.ppermute(array, axis, [(i, i ^ mask) for i in range(count)])]
  transfers between devices with their start and end apart: 34 -> 30, of which waited for: 17 -> 16; matrix products, arithmetic and copies ran while one was open for 9% -> 14% of each run, Pallas kernels for 7% -> 8%
where the time goes in v3:
time: 124 us; the launch traced here: 123 us
  waiting for transfers between devices  48.3 us (39%)
  starting transfers between devices  27 us (22%)
  Pallas kernels  25.4 us (20%)
  other arithmetic  11.5 us (9%)
  local copies, waits for them, and re-layouts  9.76 us (8%)
    ppermute x30, waiting for transfers between devices, swap(): return lax.ppermute(array, axis, [(i, i ^ mask) for i in range(count)])  48.3 us
    ppermute x30, starting transfers between devices, swap(): return lax.ppermute(array, axis, [(i, i ^ mask) for i in range(count)])  27 us
    pallas_call x4, Pallas kernels, call(): pl.pallas_call(kernel, in_specs=[in_smem] + [in_vmem] * placed + [in_hbm]...  25.4 us
    broadcast_in_dim x1, other arithmetic, per_device(): return (word[0, 0], grad_hidden[None], grad_table.reshape(pool_table.shape))  3.73 us
  transfers between devices with their start and end apart: 30, of which 16 were waited for; matrix products, arithmetic and copies ran while one was open for 14% of the time, Pallas kernels for 8%

profile of v3, /device:TPU:0, one launch (start us, length us, event | category | flops | bytes accessed | tf_op | source)
XLA Modules:
  0.0 122.9 jit_solution(6974399823099584242)
XLA Ops:
  0.7 0.8 reshape.411
  1.6 0.2 copy-done
  2.1 3.0 %collective-permute-start = (bf16[272,512]{1,0:T(8,128)(2,1)S(1)}, bf16[272,512]{1,0:T(8,128)(2,1)}, u32[]{:S(2)}, u32[]{:S(2)}) collective-permute-start(bf16[272,512]{1,0:T(8,128)(2,1)S(1)} %maximum_maximum_fusion.refs_6_), channel_id=1, source_target_pairs={{0,1},{1,0},{2,3},{3,2},{4,5},{5,4},{6,7},{7,6},{8,9},{9,8},{10,11... | collective-permute-start | bytes 835592 | tf_op jit(solution)/shard_map/ppermute | solution.py:20
  5.1 1.6 %collective-permute-start.1 = (bf16[272,512]{1,0:T(8,128)(2,1)S(1)}, bf16[272,512]{1,0:T(8,128)(2,1)}, u32[]{:S(2)}, u32[]{:S(2)}) collective-permute-start(bf16[272,512]{1,0:T(8,128)(2,1)S(1)} %maximum_maximum_fusion.refs_6_), channel_id=1, source_target_pairs={{0,2},{1,3},{2,0},{3,1},{4,6},{5,7},{6,4},{7,5},{8,10},{9,11},{10,... | collective-permute-start | bytes 835592 | tf_op jit(solution)/shard_map/ppermute | solution.py:20
  6.7 2.6 %collective-permute-start.2 = (bf16[272,512]{1,0:T(8,128)(2,1)S(1)}, bf16[272,512]{1,0:T(8,128)(2,1)}, u32[]{:S(2)}, u32[]{:S(2)}) collective-permute-start(bf16[272,512]{1,0:T(8,128)(2,1)S(1)} %maximum_maximum_fusion.refs_6_), channel_id=1, source_target_pairs={{0,4},{1,5},{2,6},{3,7},{4,0},{5,1},{6,2},{7,3},{8,12},{9,13},{10,... | collective-permute-start | bytes 835592 | tf_op jit(solution)/shard_map/ppermute | solution.py:20
  9.3 0.8 reshape.408
  10.1 2.4 %abs_reduce_fusion = (bf16[]{:T(256)}, bf16[1024,512]{1,0:T(8,128)(2,1)S(1)}) fusion(f32[1,1024,512]{2,1,0:T(8,128)} %param.7), kind=kLoop, calls=%fused_computation.3 | loop fusion | flops 1572863 | bytes 3145730 | tf_op jit(solution)/shard_map/reduce_max | solution.py:206
  12.5 0.5 broadcast.288
  13.1 0.7 reduce.3
  13.8 0.7 broadcast_in_dim.32
  14.4 0.5 concatenate.70.refs_1_.refs_2_
  14.9 1.6 %collective-permute-start.6 = (bf16[1040,512]{1,0:T(8,128)(2,1)S(1)}, bf16[1040,512]{1,0:T(8,128)(2,1)S(1)}, u32[]{:S(2)}, u32[]{:S(2)}) collective-permute-start(bf16[1040,512]{1,0:T(8,128)(2,1)S(1)} %concatenate.70.refs_1_.refs_2_), channel_id=1, source_target_pairs={{0,16},{8,24},{16,0},{24,8},{1,17},{9,25},{17,1},{25,9},{2,18},{10... | collective-permute-start | bytes 3194888 | tf_op jit(solution)/shard_map/ppermute | solution.py:20
  16.6 2.6 %collective-permute-done.1.refs_8_ = bf16[272,512]{1,0:T(8,128)(2,1)} collective-permute-done((bf16[272,512]{1,0:T(8,128)(2,1)S(1)}, bf16[272,512]{1,0:T(8,128)(2,1)}, u32[]{:S(2)}, u32[]{:S(2)}) %collective-permute-start.1) | collective-permute-done | bytes 278560 | tf_op jit(solution)/shard_map/ppermute | solution.py:20
  19.2 2.4 %collective-permute-done.2.refs_10_ = bf16[272,512]{1,0:T(8,128)(2,1)} collective-permute-done((bf16[272,512]{1,0:T(8,128)(2,1)S(1)}, bf16[272,512]{1,0:T(8,128)(2,1)}, u32[]{:S(2)}, u32[]{:S(2)}) %collective-permute-start.2) | collective-permute-done | bytes 278560 | tf_op jit(solution)/shard_map/ppermute | solution.py:20
  21.6 0.5 collective-permute-start.3
  22.1 0.4 collective-permute-start.4
  22.8 5.5 %collective-permute-done.3.refs_11_ = bf16[272,512]{1,0:T(8,128)(2,1)S(1)} collective-permute-done((bf16[272,512]{1,0:T(8,128)(2,1)}, bf16[272,512]{1,0:T(8,128)(2,1)S(1)}, u32[]{:S(2)}, u32[]{:S(2)}) %collective-permute-start.3) | collective-permute-done | bytes 278560 | tf_op jit(solution)/shard_map/ppermute | solution.py:20
  28.3 0.6 collective-permute-done.4.refs_12_
  29.0 1.6 %collective-permute-start.9 = (bf16[272,512]{1,0:T(8,128)(2,1)}, bf16[272,512]{1,0:T(8,128)(2,1)}, u32[]{:S(2)}, u32[]{:S(2)}) collective-permute-start(bf16[272,512]{1,0:T(8,128)(2,1)} %collective-permute-done.4.refs_12_), channel_id=1, source_target_pairs={{0,1},{1,0},{2,3},{3,2},{4,5},{5,4},{6,7},{7,6},{8,9},{9,8},{10,11... | collective-permute-start | bytes 835592 | tf_op jit(solution)/shard_map/ppermute | solution.py:20
  30.5 0.8 collective-permute-start.8
  31.3 8.1 %collective-permute-done.6.refs_3_.refs_4_ = bf16[1040,512]{1,0:T(8,128)(2,1)S(1)} collective-permute-done((bf16[1040,512]{1,0:T(8,128)(2,1)S(1)}, bf16[1040,512]{1,0:T(8,128)(2,1)S(1)}, u32[]{:S(2)}, u32[]{:S(2)}) %collective-permute-start.6) | collective-permute-done | bytes 1064992 | tf_op jit(solution)/shard_map/ppermute | solution.py:20
  39.5 0.8 convert_add_fusion.2
  40.3 0.8 fusion.36
  41.1 1.2 collective-permute-done.7.refs_4_.refs_5_
  42.3 0.8 fusion.38
  43.0 0.8 convert_add_fusion
  44.0 10.8 %scores.1 = (f32[8,4,512,128]{3,2,1,0:T(8,128)S(1)}, f32[80,128]{1,0:T(8,128)S(1)}, bf16[2176,512]{1,0:T(8,128)(2,1)S(1)}) custom-call(s32[256]{0:T(256)S(1)} %fusion.20.index, f32[32,128]{1,0:T(8,128)S(1)} %pad_maximum_fusion.refs_0_, bf16[1040,512]{1,0:T(8,128)(2,1)S(1)} %concatenate.70.refs_1_.refs_2_, ...), custom_call_target="tpu_custom_call" | custom-call | flops 1048576 | bytes 1048576 | tf_op jit(solution)/shard_map/scores/pallas_call | solution.py:276
  54.8 0.2 collective-permute-start.10
  55.0 1.5 %collective-permute-start.11 = (f32[80,128]{1,0:T(8,128)S(1)}, f32[80,128]{1,0:T(8,128)S(1)}, u32[]{:S(2)}, u32[]{:S(2)}) collective-permute-start(f32[80,128]{1,0:T(8,128)S(1)} %get-tuple-element.65.refs_3_), channel_id=1, source_target_pairs={{0,16},{8,24},{16,0},{24,8},{1,17},{9,25},{17,1},{25,9},{2,18},{10... | collective-permute-start | bytes 122888 | tf_op jit(solution)/shard_map/ppermute | solution.py:20
  56.7 2.3 %collective-permute-done.11.refs_5_ = f32[80,128]{1,0:T(8,128)S(1)} collective-permute-done((f32[80,128]{1,0:T(8,128)S(1)}, f32[80,128]{1,0:T(8,128)S(1)}, u32[]{:S(2)}, u32[]{:S(2)}) %collective-permute-start.11) | collective-permute-done | bytes 40992 | tf_op jit(solution)/shard_map/ppermute | solution.py:20
  59.0 1.1 collective-permute-done.12.refs_6_
  60.1 4.6 %grads.1 = (bf16[8,512,128]{2,1,0:T(8,128)(2,1)S(1)}, bf16[8,3,512,128]{3,2,1,0:T(8,128)(2,1)S(1)}, f32[8,128]{1,0:T(8,128)S(1)}, f32[8,128]{1,0:T(8,128)S(1)}, ...) custom-call(s32[256]{0:T(256)S(1)} %fusion.20.index, ...), custom_call_target="tpu_custom_call" | custom-call | flops 1048576 | bytes 1048576 | tf_op jit(solution)/shard_map/grads/pallas_call | solution.py:276
  64.9 0.5 collective-permute-start.14
  65.6 7.4 %table_grads.1 = f32[2048,512]{1,0:T(8,128)S(1)} custom-call(s32[256]{0:T(256)S(1)} %fusion.20.index, bf16[8,512,128]{2,1,0:T(8,128)(2,1)S(1)} %get-tuple-element.84.refs_0_.near, bf16[8,3,512,128]{3,2,1,0:T(8,128)(2,1)S(1)} %get-tuple-element.68.refs_1_, bf16[1040,512]{1,0:T(8,128)(2,1)S(1)} %concatenate.70.refs_1_.refs_2_, ...), custom_call_target="tpu_custom_call" | custom-call | flops 1048576 | bytes 1048576 | tf_op jit(solution)/shard_map/table_grads/pallas_call | solution.py:276
  73.2 0.3 multiply_convert_fusion
  73.6 1.6 %collective-permute-start.15 = (f16[256,512]{1,0:T(8,128)(2,1)S(1)}, f16[256,512]{1,0:T(8,128)(2,1)S(1)}, u32[]{:S(2)}, u32[]{:S(2)}) collective-permute-start(f16[256,512]{1,0:T(8,128)(2,1)S(1)} %get-tuple-element.74), channel_id=1, source_target_pairs={{0,1},{1,0},{2,3},{3,2},{4,5},{5,4},{6,7},{7,6},{8,9},{9,8},{10,11... | collective-permute-start | bytes 786440 | tf_op jit(solution)/shard_map/ppermute | solution.py:20
  75.2 0.4 collective-permute-start.16
  75.6 1.6 %collective-permute-start.17 = (f32[8,128]{1,0:T(8,128)S(1)}, f32[8,128]{1,0:T(8,128)S(1)}, u32[]{:S(2)}, u32[]{:S(2)}) collective-permute-start(f32[8,128]{1,0:T(8,128)S(1)} %maximum_select_fusion.2), channel_id=1, source_target_pairs={{0,2},{1,3},{2,0},{3,1},{4,6},{5,7},{6,4},{7,5},{8,10},{9,11},{10,... | collective-permute-start | bytes 12296 | tf_op jit(solution)/shard_map/ppermute | solution.py:20
  77.2 0.7 collective-permute-start.21
  77.9 5.6 %collective-permute-done.17 = f32[8,128]{1,0:T(8,128)S(1)} collective-permute-done((f32[8,128]{1,0:T(8,128)S(1)}, f32[8,128]{1,0:T(8,128)S(1)}, u32[]{:S(2)}, u32[]{:S(2)}) %collective-permute-start.17) | collective-permute-done | bytes 4128 | tf_op jit(solution)/shard_map/ppermute | solution.py:20
  83.6 0.4 collective-permute-start.20
  84.2 0.6 collective-permute-start.18
  84.8 0.4 collective-permute-start.19
  85.3 3.0 %collective-permute-done.20 = f32[8,128]{1,0:T(8,128)S(1)} collective-permute-done((f32[8,128]{1,0:T(8,128)S(1)}, f32[8,128]{1,0:T(8,128)S(1)}, u32[]{:S(2)}, u32[]{:S(2)}) %collective-permute-start.20) | collective-permute-done | bytes 4128 | tf_op jit(solution)/shard_map/ppermute | solution.py:20
  88.2 2.4 %collective-permute-done.21 = f16[1024,256]{1,0:T(8,128)(2,1)} collective-permute-done((f16[1024,256]{1,0:T(8,128)(2,1)S(1)}, f16[1024,256]{1,0:T(8,128)(2,1)}, u32[]{:S(2)}, u32[]{:S(2)}) %collective-permute-start.21) | collective-permute-done | bytes 524320 | tf_op jit(solution)/shard_map/ppermute | solution.py:20
  90.6 1.0 collective-permute-done.18
  91.6 0.3 collective-permute-done.19
  92.0 1.0 collective-permute-start.26
  93.1 0.3 multiply_convert_fusion.3
  93.4 2.5 %collective-permute-start.23 = (f16[256,512]{1,0:T(8,128)(2,1)S(1)}, f16[256,512]{1,0:T(8,128)(2,1)S(1)}, u32[]{:S(2)}, u32[]{:S(2)}) collective-permute-start(f16[256,512]{1,0:T(8,128)(2,1)S(1)} %get-tuple-element.104), channel_id=1, source_target_pairs={{0,4},{1,5},{2,6},{3,7},{4,0},{5,1},{6,2},{7,3},{8,12},{9,13},{10,... | collective-permute-start | bytes 786440 | tf_op jit(solution)/shard_map/ppermute | solution.py:20
  95.9 0.5 collective-permute-start.24
  96.4 1.5 %collective-permute-start.25 = (f16[256,512]{1,0:T(8,128)(2,1)S(1)}, f16[256,512]{1,0:T(8,128)(2,1)S(1)}, u32[]{:S(2)}, u32[]{:S(2)}) collective-permute-start(f16[256,512]{1,0:T(8,128)(2,1)S(1)} %get-tuple-element.102), channel_id=1, source_target_pairs={{0,1},{1,0},{2,3},{3,2},{4,5},{5,4},{6,7},{7,6},{8,9},{9,8},{10,11... | collective-permute-start | bytes 786440 | tf_op jit(solution)/shard_map/ppermute | solution.py:20
  98.0 2.6 %own_hidden_grads.1 = f32[1024,512]{1,0:T(8,128)S(1)} custom-call(s32[256]{0:T(256)S(1)} %fusion.20.index, bf16[8,512,128]{2,1,0:T(8,128)(2,1)S(1)} %get-tuple-element.84.refs_0_.near, bf16[2176,512]{1,0:T(8,128)(2,1)S(1)} %get-tuple-element.64.refs_2_.table, f32[8,128]{1,0:T(8,128)S(1)} %get-tuple-element.85.pos_grad, bf16[1024,512]{1,0:T(8,128)(2,1)S(1)} %bitcast.50), custom_call_target="tpu_custom_call" | custom-call | flops 1048576 | bytes 1048576 | tf_op jit(solution)/shard_map/own_hidden_grads/pallas_call | solution.py:276
  100.6 5.4 %collective-permute-done.23 = f16[256,512]{1,0:T(8,128)(2,1)S(1)} collective-permute-done((f16[256,512]{1,0:T(8,128)(2,1)S(1)}, f16[256,512]{1,0:T(8,128)(2,1)S(1)}, u32[]{:S(2)}, u32[]{:S(2)}) %collective-permute-start.23) | collective-permute-done | bytes 262176 | tf_op jit(solution)/shard_map/ppermute | solution.py:20
  106.0 1.2 collective-permute-done.24
  107.2 1.1 multiply_convert_fusion.2
  108.3 0.8 collective-permute-start.28
  109.1 0.5 slice.147
  109.6 5.6 %collective-permute-done.28 = f16[256,512]{1,0:T(8,128)(2,1)S(1)} collective-permute-done((f16[256,512]{1,0:T(8,128)(2,1)}, f16[256,512]{1,0:T(8,128)(2,1)S(1)}, u32[]{:S(2)}, u32[]{:S(2)}) %collective-permute-start.28) | collective-permute-done | bytes 262176 | tf_op jit(solution)/shard_map/ppermute | solution.py:20
  115.2 3.7 %add_bitcast_fusion = f32[1,1024,512]{2,1,0:T(8,128)} fusion(f32[1024,512]{1,0:T(8,128)S(1)} %own_hidden_grads.1, f32[1024,512]{1,0:T(8,128)} %copy-done.2, f16[1024,256]{1,0:T(8,128)(2,1)} %copy-done.5, f16[1024,256]{1,0:T(8,128)(2,1)} %collective-permute-done.21), kind=kLoop, calls=%fused_computation | loop fusion | flops 2621440 | bytes 7340032 | tf_op jit(solution)/shard_map/broadcast_in_dim | solution.py:413
  118.9 0.2 broadcast_in_dim.35
  119.2 1.1 constant_dynamic-update-slice_fusion.3
  120.3 1.1 constant_dynamic-update-slice_fusion.2
  121.6 1.3 %copy-done.3 = f32[4,4,64,512]{3,2,1,0:T(8,128)} copy-done((f32[4,4,64,512]{3,2,1,0:T(8,128)}, f32[4,4,64,512]{3,2,1,0:T(8,128)S(1)}, u32[]{:S(2)}) %copy-start.3) | copy-done | bytes 2097176
  (87 shorter events, 2.5 us)
Async XLA Ops:
  0.6 1.2 %copy-start = (bf16[1024,512]{1,0:T(8,128)(2,1)S(1)}, bf16[1024,512]{1,0:T(8,128)(2,1)}, u32[]{:S(2)}) copy-start(bf16[1024,512]{1,0:T(8,128)(2,1)} %param.9) | copy-start | bytes 3145732
  1.9 11.2 %copy-start.7 = (s32[1,1024]{1,0:T(1,128)S(1)}, s32[1,1024]{1,0:T(1,128)}, u32[]{:S(2)}) copy-start(s32[1,1024]{1,0:T(1,128)} %param.11) | copy-start | bytes 12292
  2.1 12.8 %copy-start.4 = (bf16[272,512]{1,0:T(8,128)(2,1)}, bf16[272,512]{1,0:T(8,128)(2,1)S(1)}, u32[]{:S(2)}) copy-start(bf16[272,512]{1,0:T(8,128)(2,1)S(1)} %maximum_maximum_fusion.refs_6_) | copy-start | bytes 835588
  2.1 14.5 %collective-permute-start = (bf16[272,512]{1,0:T(8,128)(2,1)S(1)}, bf16[272,512]{1,0:T(8,128)(2,1)}, u32[]{:S(2)}, u32[]{:S(2)}) collective-permute-start(bf16[272,512]{1,0:T(8,128)(2,1)S(1)} %maximum_maximum_fusion.refs_6_), channel_id=1, source_target_pairs={{0,1},{1,0},{2,3},{3,2},{4,5},{5,4},{6,7},{7,6},{8,9},{9,8},{10,11... | collective-permute-start | bytes 835592 | tf_op jit(solution)/shard_map/ppermute | solution.py:20
  5.1 14.1 %collective-permute-start.1 = (bf16[272,512]{1,0:T(8,128)(2,1)S(1)}, bf16[272,512]{1,0:T(8,128)(2,1)}, u32[]{:S(2)}, u32[]{:S(2)}) collective-permute-start(bf16[272,512]{1,0:T(8,128)(2,1)S(1)} %maximum_maximum_fusion.refs_6_), channel_id=1, source_target_pairs={{0,2},{1,3},{2,0},{3,1},{4,6},{5,7},{6,4},{7,5},{8,10},{9,11},{10,... | collective-permute-start | bytes 835592 | tf_op jit(solution)/shard_map/ppermute | solution.py:20
  6.7 14.9 %collective-permute-start.2 = (bf16[272,512]{1,0:T(8,128)(2,1)S(1)}, bf16[272,512]{1,0:T(8,128)(2,1)}, u32[]{:S(2)}, u32[]{:S(2)}) collective-permute-start(bf16[272,512]{1,0:T(8,128)(2,1)S(1)} %maximum_maximum_fusion.refs_6_), channel_id=1, source_target_pairs={{0,4},{1,5},{2,6},{3,7},{4,0},{5,1},{6,2},{7,3},{8,12},{9,13},{10,... | collective-permute-start | bytes 835592 | tf_op jit(solution)/shard_map/ppermute | solution.py:20
  10.1 6.4 %copy-start.8 = (s32[1,5]{1,0:T(1,128)S(1)}, s32[1,5]{1,0:T(1,128)}, u32[]{:S(2)}) copy-start(s32[1,5]{1,0:T(1,128)} %param.13) | copy-start | bytes 64
  14.9 24.5 %collective-permute-start.6 = (bf16[1040,512]{1,0:T(8,128)(2,1)S(1)}, bf16[1040,512]{1,0:T(8,128)(2,1)S(1)}, u32[]{:S(2)}, u32[]{:S(2)}) collective-permute-start(bf16[1040,512]{1,0:T(8,128)(2,1)S(1)} %concatenate.70.refs_1_.refs_2_), channel_id=1, source_target_pairs={{0,16},{8,24},{16,0},{24,8},{1,17},{9,25},{17,1},{25,9},{2,18},{10... | collective-permute-start | bytes 3194888 | tf_op jit(solution)/shard_map/ppermute | solution.py:20
  21.6 6.8 %collective-permute-start.3 = (bf16[272,512]{1,0:T(8,128)(2,1)}, bf16[272,512]{1,0:T(8,128)(2,1)S(1)}, u32[]{:S(2)}, u32[]{:S(2)}) collective-permute-start(bf16[272,512]{1,0:T(8,128)(2,1)} %collective-permute-done.2.refs_10_), channel_id=1, source_target_pairs={{0,1},{1,0},{2,3},{3,2},{4,5},{5,4},{6,7},{7,6},{8,9},{9,8},{10,11... | collective-permute-start | bytes 835592 | tf_op jit(solution)/shard_map/ppermute | solution.py:20
  22.1 6.9 %collective-permute-start.4 = (bf16[272,512]{1,0:T(8,128)(2,1)}, bf16[272,512]{1,0:T(8,128)(2,1)}, u32[]{:S(2)}, u32[]{:S(2)}) collective-permute-start(bf16[272,512]{1,0:T(8,128)(2,1)} %collective-permute-done.2.refs_10_), channel_id=1, source_target_pairs={{0,2},{1,3},{2,0},{3,1},{4,6},{5,7},{6,4},{7,5},{8,10},{9,11},{10,... | collective-permute-start | bytes 835592 | tf_op jit(solution)/shard_map/ppermute | solution.py:20
  28.3 15.6 %copy-start.6 = (bf16[272,512]{1,0:T(8,128)(2,1)}, bf16[272,512]{1,0:T(8,128)(2,1)S(1)}, u32[]{:S(2)}) copy-start(bf16[272,512]{1,0:T(8,128)(2,1)S(1)} %collective-permute-done.3.refs_11_) | copy-start | bytes 835588
  29.0 10.5 %collective-permute-start.5 = (bf16[1040,512]{1,0:T(8,128)(2,1)S(1)}, bf16[1040,512]{1,0:T(8,128)(2,1)}, u32[]{:S(2)}, u32[]{:S(2)}) collective-permute-start(bf16[1040,512]{1,0:T(8,128)(2,1)S(1)} %concatenate.70.refs_1_.refs_2_), channel_id=1, source_target_pairs={{0,8},{8,0},{16,24},{24,16},{1,9},{9,1},{17,25},{25,17},{2,10},{10... | collective-permute-start | bytes 3194888 | tf_op jit(solution)/shard_map/ppermute | solution.py:20
  29.0 15.0 %collective-permute-start.9 = (bf16[272,512]{1,0:T(8,128)(2,1)}, bf16[272,512]{1,0:T(8,128)(2,1)}, u32[]{:S(2)}, u32[]{:S(2)}) collective-permute-start(bf16[272,512]{1,0:T(8,128)(2,1)} %collective-permute-done.4.refs_12_), channel_id=1, source_target_pairs={{0,1},{1,0},{2,3},{3,2},{4,5},{5,4},{6,7},{7,6},{8,9},{9,8},{10,11... | collective-permute-start | bytes 835592 | tf_op jit(solution)/shard_map/ppermute | solution.py:20
  30.5 13.4 %collective-permute-start.8 = (bf16[272,512]{1,0:T(8,128)(2,1)}, bf16[272,512]{1,0:T(8,128)(2,1)}, u32[]{:S(2)}, u32[]{:S(2)}) collective-permute-start(bf16[272,512]{1,0:T(8,128)(2,1)} %collective-permute-done.refs_7_), channel_id=1, source_target_pairs={{0,2},{1,3},{2,0},{3,1},{4,6},{5,7},{6,4},{7,5},{8,10},{9,11},{10,... | collective-permute-start | bytes 835592 | tf_op jit(solution)/shard_map/ppermute | solution.py:20
  39.4 2.9 %collective-permute-start.7 = (bf16[1040,512]{1,0:T(8,128)(2,1)S(1)}, bf16[1040,512]{1,0:T(8,128)(2,1)}, u32[]{:S(2)}, u32[]{:S(2)}) collective-permute-start(bf16[1040,512]{1,0:T(8,128)(2,1)S(1)} %collective-permute-done.6.refs_3_.refs_4_), channel_id=1, source_target_pairs={{0,8},{8,0},{16,24},{24,16},{1,9},{9,1},{17,25},{25,17},{2,10},{10... | collective-permute-start | bytes 3194888 | tf_op jit(solution)/shard_map/ppermute | solution.py:20
  54.8 1.9 %collective-permute-start.10 = (f32[80,128]{1,0:T(8,128)S(1)}, f32[80,128]{1,0:T(8,128)S(1)}, u32[]{:S(2)}, u32[]{:S(2)}) collective-permute-start(f32[80,128]{1,0:T(8,128)S(1)} %get-tuple-element.65.refs_3_), channel_id=1, source_target_pairs={{0,8},{8,0},{16,24},{24,16},{1,9},{9,1},{17,25},{25,17},{2,10},{10... | collective-permute-start | bytes 122888 | tf_op jit(solution)/shard_map/ppermute | solution.py:20
  55.0 4.0 %collective-permute-start.11 = (f32[80,128]{1,0:T(8,128)S(1)}, f32[80,128]{1,0:T(8,128)S(1)}, u32[]{:S(2)}, u32[]{:S(2)}) collective-permute-start(f32[80,128]{1,0:T(8,128)S(1)} %get-tuple-element.65.refs_3_), channel_id=1, source_target_pairs={{0,16},{8,24},{16,0},{24,8},{1,17},{9,25},{17,1},{25,9},{2,18},{10... | collective-permute-start | bytes 122888 | tf_op jit(solution)/shard_map/ppermute | solution.py:20
  56.5 3.6 %collective-permute-start.12 = (f32[80,128]{1,0:T(8,128)S(1)}, f32[80,128]{1,0:T(8,128)S(1)}, u32[]{:S(2)}, u32[]{:S(2)}) collective-permute-start(f32[80,128]{1,0:T(8,128)S(1)} %get-tuple-element.65.refs_3_), channel_id=1, source_target_pairs={{0,24},{8,16},{16,8},{24,0},{1,25},{9,17},{17,9},{25,1},{2,26},{10... | collective-permute-start | bytes 122888 | tf_op jit(solution)/shard_map/ppermute | solution.py:20
  64.7 8.3 %collective-permute-start.13 = (f32[1024,512]{1,0:T(8,128)S(1)}, f32[1024,512]{1,0:T(8,128)S(1)}, u32[]{:S(2)}, u32[]{:S(2)}) collective-permute-start(f32[1024,512]{1,0:T(8,128)S(1)} %get-tuple-element.69), channel_id=1, source_target_pairs={{0,8},{8,0},{16,24},{24,16},{1,9},{9,1},{17,25},{25,17},{2,10},{10... | collective-permute-start | bytes 6291464 | tf_op jit(solution)/shard_map/ppermute | solution.py:20
  64.9 8.1 %collective-permute-start.14 = (f32[8,128]{1,0:T(8,128)S(1)}, f32[8,128]{1,0:T(8,128)S(1)}, u32[]{:S(2)}, u32[]{:S(2)}) collective-permute-start(f32[8,128]{1,0:T(8,128)S(1)} %get-tuple-element.66), channel_id=1, source_target_pairs={{0,1},{1,0},{2,3},{3,2},{4,5},{5,4},{6,7},{7,6},{8,9},{9,8},{10,11... | collective-permute-start | bytes 12296 | tf_op jit(solution)/shard_map/ppermute | solution.py:20
  65.4 19.8 %collective-permute-start.22 = (f32[1024,512]{1,0:T(8,128)S(1)}, f32[1024,512]{1,0:T(8,128)S(1)}, u32[]{:S(2)}, u32[]{:S(2)}) collective-permute-start(f32[1024,512]{1,0:T(8,128)S(1)} %get-tuple-element.79), channel_id=1, source_target_pairs={{0,8},{8,0},{16,24},{24,16},{1,9},{9,1},{17,25},{25,17},{2,10},{10... | collective-permute-start | bytes 6291464 | tf_op jit(solution)/shard_map/ppermute | solution.py:20
  73.6 10.0 %collective-permute-start.15 = (f16[256,512]{1,0:T(8,128)(2,1)S(1)}, f16[256,512]{1,0:T(8,128)(2,1)S(1)}, u32[]{:S(2)}, u32[]{:S(2)}) collective-permute-start(f16[256,512]{1,0:T(8,128)(2,1)S(1)} %get-tuple-element.74), channel_id=1, source_target_pairs={{0,1},{1,0},{2,3},{3,2},{4,5},{5,4},{6,7},{7,6},{8,9},{9,8},{10,11... | collective-permute-start | bytes 786440 | tf_op jit(solution)/shard_map/ppermute | solution.py:20
  75.2 8.4 %collective-permute-start.16 = (f16[256,512]{1,0:T(8,128)(2,1)S(1)}, f16[256,512]{1,0:T(8,128)(2,1)S(1)}, u32[]{:S(2)}, u32[]{:S(2)}) collective-permute-start(f16[256,512]{1,0:T(8,128)(2,1)S(1)} %get-tuple-element.75), channel_id=1, source_target_pairs={{0,2},{1,3},{2,0},{3,1},{4,6},{5,7},{6,4},{7,5},{8,10},{9,11},{10,... | collective-permute-start | bytes 786440 | tf_op jit(solution)/shard_map/ppermute | solution.py:20
  75.6 7.9 %collective-permute-start.17 = (f32[8,128]{1,0:T(8,128)S(1)}, f32[8,128]{1,0:T(8,128)S(1)}, u32[]{:S(2)}, u32[]{:S(2)}) collective-permute-start(f32[8,128]{1,0:T(8,128)S(1)} %maximum_select_fusion.2), channel_id=1, source_target_pairs={{0,2},{1,3},{2,0},{3,1},{4,6},{5,7},{6,4},{7,5},{8,10},{9,11},{10,... | collective-permute-start | bytes 12296 | tf_op jit(solution)/shard_map/ppermute | solution.py:20
  77.2 13.4 %collective-permute-start.21 = (f16[1024,256]{1,0:T(8,128)(2,1)S(1)}, f16[1024,256]{1,0:T(8,128)(2,1)}, u32[]{:S(2)}, u32[]{:S(2)}) collective-permute-start(f16[1024,256]{1,0:T(8,128)(2,1)S(1)} %get-tuple-element.78), channel_id=1, source_target_pairs={{0,16},{8,24},{16,0},{24,8},{1,17},{9,25},{17,1},{25,9},{2,18},{10... | collective-permute-start | bytes 1572872 | tf_op jit(solution)/shard_map/ppermute | solution.py:20
  83.6 4.6 %collective-permute-start.20 = (f32[8,128]{1,0:T(8,128)S(1)}, f32[8,128]{1,0:T(8,128)S(1)}, u32[]{:S(2)}, u32[]{:S(2)}) collective-permute-start(f32[8,128]{1,0:T(8,128)S(1)} %maximum_select_fusion.1), channel_id=1, source_target_pairs={{0,4},{1,5},{2,6},{3,7},{4,0},{5,1},{6,2},{7,3},{8,12},{9,13},{10,... | collective-permute-start | bytes 12296 | tf_op jit(solution)/shard_map/ppermute | solution.py:20
  84.0 13.9 %copy-start.1 = (bf16[1,1024,512]{2,1,0:T(8,128)(2,1)S(1)}, bf16[1,1024,512]{2,1,0:T(8,128)(2,1)}, u32[]{:S(2)}) copy-start(bf16[1,1024,512]{2,1,0:T(8,128)(2,1)} %param.8) | copy-start | bytes 3145732
  84.2 7.4 %collective-permute-start.18 = (f16[256,512]{1,0:T(8,128)(2,1)S(1)}, f16[256,512]{1,0:T(8,128)(2,1)S(1)}, u32[]{:S(2)}, u32[]{:S(2)}) collective-permute-start(f16[256,512]{1,0:T(8,128)(2,1)S(1)} %get-tuple-element.106), channel_id=1, source_target_pairs={{0,1},{1,0},{2,3},{3,2},{4,5},{5,4},{6,7},{7,6},{8,9},{9,8},{10,11... | collective-permute-start | bytes 786440 | tf_op jit(solution)/shard_map/ppermute | solution.py:20
  84.8 7.2 %collective-permute-start.19 = (f16[256,512]{1,0:T(8,128)(2,1)S(1)}, f16[256,512]{1,0:T(8,128)(2,1)S(1)}, u32[]{:S(2)}, u32[]{:S(2)}) collective-permute-start(f16[256,512]{1,0:T(8,128)(2,1)S(1)} %get-tuple-element.105), channel_id=1, source_target_pairs={{0,2},{1,3},{2,0},{3,1},{4,6},{5,7},{6,4},{7,5},{8,10},{9,11},{10,... | collective-permute-start | bytes 786440 | tf_op jit(solution)/shard_map/ppermute | solution.py:20
  85.2 15.3 %copy-start.2 = (f32[1024,512]{1,0:T(8,128)}, f32[1024,512]{1,0:T(8,128)S(1)}, u32[]{:S(2)}) copy-start(f32[1024,512]{1,0:T(8,128)S(1)} %collective-permute-done.22) | copy-start | bytes 6291460
  92.0 15.2 %collective-permute-start.26 = (f16[1024,256]{1,0:T(8,128)(2,1)S(1)}, f16[1024,256]{1,0:T(8,128)(2,1)S(1)}, u32[]{:S(2)}, u32[]{:S(2)}) collective-permute-start(f16[1024,256]{1,0:T(8,128)(2,1)S(1)} %get-tuple-element.87), channel_id=1, source_target_pairs={{0,16},{8,24},{16,0},{24,8},{1,17},{9,25},{17,1},{25,9},{2,18},{10... | collective-permute-start | bytes 1572872 | tf_op jit(solution)/shard_map/ppermute | solution.py:20
  93.4 12.6 %collective-permute-start.23 = (f16[256,512]{1,0:T(8,128)(2,1)S(1)}, f16[256,512]{1,0:T(8,128)(2,1)S(1)}, u32[]{:S(2)}, u32[]{:S(2)}) collective-permute-start(f16[256,512]{1,0:T(8,128)(2,1)S(1)} %get-tuple-element.104), channel_id=1, source_target_pairs={{0,4},{1,5},{2,6},{3,7},{4,0},{5,1},{6,2},{7,3},{8,12},{9,13},{10,... | collective-permute-start | bytes 786440 | tf_op jit(solution)/shard_map/ppermute | solution.py:20
  95.9 11.3 %collective-permute-start.24 = (f16[256,512]{1,0:T(8,128)(2,1)S(1)}, f16[256,512]{1,0:T(8,128)(2,1)S(1)}, u32[]{:S(2)}, u32[]{:S(2)}) collective-permute-start(f16[256,512]{1,0:T(8,128)(2,1)S(1)} %get-tuple-element.103), channel_id=1, source_target_pairs={{0,2},{1,3},{2,0},{3,1},{4,6},{5,7},{6,4},{7,5},{8,10},{9,11},{10,... | collective-permute-start | bytes 786440 | tf_op jit(solution)/shard_map/ppermute | solution.py:20
  96.4 10.8 %collective-permute-start.25 = (f16[256,512]{1,0:T(8,128)(2,1)S(1)}, f16[256,512]{1,0:T(8,128)(2,1)S(1)}, u32[]{:S(2)}, u32[]{:S(2)}) collective-permute-start(f16[256,512]{1,0:T(8,128)(2,1)S(1)} %get-tuple-element.102), channel_id=1, source_target_pairs={{0,1},{1,0},{2,3},{3,2},{4,5},{5,4},{6,7},{7,6},{8,9},{9,8},{10,11... | collective-permute-start | bytes 786440 | tf_op jit(solution)/shard_map/ppermute | solution.py:20
  107.2 1.1 copy-start.5
  108.3 6.9 %collective-permute-start.28 = (f16[256,512]{1,0:T(8,128)(2,1)}, f16[256,512]{1,0:T(8,128)(2,1)S(1)}, u32[]{:S(2)}, u32[]{:S(2)}) collective-permute-start(f16[256,512]{1,0:T(8,128)(2,1)} %get-tuple-element.95), channel_id=1, source_target_pairs={{0,16},{8,24},{16,0},{24,8},{1,17},{9,25},{17,1},{25,9},{2,18},{10... | collective-permute-start | bytes 786440 | tf_op jit(solution)/shard_map/ppermute | solution.py:20
  109.1 11.2 %collective-permute-start.27 = (f32[256,512]{1,0:T(8,128)}, f32[256,512]{1,0:T(8,128)}, u32[]{:S(2)}, u32[]{:S(2)}) collective-permute-start(f32[256,512]{1,0:T(8,128)} %get-tuple-element.96), channel_id=1, source_target_pairs={{0,8},{8,0},{16,24},{24,16},{1,9},{9,1},{17,25},{25,17},{2,10},{10... | collective-permute-start | bytes 1572872 | tf_op jit(solution)/shard_map/ppermute | solution.py:20
  115.2 6.2 %collective-permute-start.29 = (f16[256,512]{1,0:T(8,128)(2,1)S(1)}, f16[256,512]{1,0:T(8,128)(2,1)S(1)}, u32[]{:S(2)}, u32[]{:S(2)}) collective-permute-start(f16[256,512]{1,0:T(8,128)(2,1)S(1)} %collective-permute-done.28), channel_id=1, source_target_pairs={{0,8},{8,0},{16,24},{24,16},{1,9},{9,1},{17,25},{25,17},{2,10},{10... | collective-permute-start | bytes 786440 | tf_op jit(solution)/shard_map/ppermute | solution.py:20
  121.6 1.3 %copy-start.3 = (f32[4,4,64,512]{3,2,1,0:T(8,128)}, f32[4,4,64,512]{3,2,1,0:T(8,128)S(1)}, u32[]{:S(2)}) copy-start(f32[4,4,64,512]{3,2,1,0:T(8,128)S(1)} %constant_dynamic-update-slice_fusion) | copy-start | bytes 6291460

commit v4 on v3

--- a/solution.py
+++ b/solution.py
@@ -28,10 +28,14 @@
     return jnp.sum(jnp.where(inside, 1.0 / lengths, 0.0), axis=-1)
 
 
-def gather_slabs(table, index, first, count, per_piece, stride, slab):
+def note_places(length, features, blocks):
+    lines = length // features
+    return lines, 2 * lines, -(-(2 * lines + blocks + 1) // HEAD) * HEAD
+
+
+def gather_slabs(table, bases, per_piece, stride, slab):
     rows = []
-    for k in range(count):
-        base = index[first + k]
+    for base in bases:
         row = (base // per_piece) * stride + (base % per_piece) * slab
         rows.append(table[pl.ds(pl.multiple_of(row, 16), slab), :])
     return jnp.concatenate(rows, axis=0)
@@ -48,14 +52,55 @@
     return jnp.sum(folded.T, axis=0, keepdims=True)
 
 
-def score_kernel(dims, index, *refs):
+def pack_kernel(labels_from, chosen_from, hidden_from, packed, labels, chosen, hidden, lots, sems, note_sems):
+    note_copies = [
+        pltpu.make_async_copy(labels_from, labels, note_sems.at[0]),
+        pltpu.make_async_copy(chosen_from, chosen, note_sems.at[1]),
+    ]
+    for copy in note_copies:
+        copy.start()
+    length, features = hidden.shape
+    blocks, picks = chosen.shape
+    lines, first, count = note_places(length, features, blocks)
+    part = length // sems.shape[0]
+    copies = [
+        pltpu.make_async_copy(hidden_from.at[pl.ds(k * part, part)], hidden.at[pl.ds(k * part, part)], sems.at[k])
+        for k in range(sems.shape[0])
+    ]
+    for copy in copies:
+        copy.start()
+    lots[...] = jnp.zeros_like(lots)
+    for copy in note_copies:
+        copy.wait()
+    lots[:, :picks] = chosen[...].astype(jnp.float32)
+    row = lax.broadcasted_iota(jnp.int32, (count, features), 0)
+    notes = jnp.zeros((count, features), jnp.float32)
+    for k in range(lines):
+        line = labels[:, k * features:(k + 1) * features]
+        notes = jnp.where(row == k, (line // ID_BASE).astype(jnp.float32), notes)
+        notes = jnp.where(row == lines + k, (line % ID_BASE).astype(jnp.float32), notes)
+    for k in range(blocks):
+        notes = jnp.where(row == first + k, lots[k:k + 1, :], notes)
+    top = jnp.zeros((8, features), jnp.float32)
+    for k, copy in enumerate(copies):
+        copy.wait()
+        narrow = hidden[k * part:(k + 1) * part, :].astype(jnp.bfloat16)
+        packed[k * part:(k + 1) * part, :] = narrow
+        sizes = jnp.abs(narrow.astype(jnp.float32))
+        top = jnp.maximum(top, jnp.max(sizes.reshape(part // 8, 8, features), axis=0))
+    notes = jnp.where(row == count - 1, jnp.max(top, keepdims=True), notes)
+    packed[length:, :] = notes.astype(jnp.bfloat16)
+
+
+def score_kernel(dims, user, *refs):
     peers, blocks, picks, users, per_piece, slab = dims
-    labels, narrows = refs[0], refs[1:1 + peers]
-    target_from, pieces = refs[1 + peers], refs[2 + peers:-7]
-    scores, stats, table, items, target, sems, target_sem = refs[-7:]
+    narrows, target_from, pieces = refs[:peers], refs[peers], refs[1 + peers:-11]
+    scores, stats, table, index, items, target, labels, lots, sems, target_sem, index_sem = refs[-11:]
     rows = per_piece * slab
     stride = rows + HEAD
     kept = 2 * peers * blocks
+    length, features = target.shape
+    lines, first_lot, _ = note_places(length, features, blocks)
 
     target_copy = pltpu.make_async_copy(target_from, target, target_sem)
     target_copy.start()
@@ -65,11 +110,23 @@
     ]
     for copy in copies:
         copy.start()
+    tops = []
+    for r in range(peers):
+        notes = narrows[r][length:, :].astype(jnp.float32)
+        lot = notes[first_lot:first_lot + blocks, :PB].astype(jnp.int32)
+        lots[r * blocks:(r + 1) * blocks, :] = ((lot // per_piece) ^ user[0]) * per_piece + lot % per_piece
+        for k in range(blocks):
+            line, lane = divmod(k * PB, features)
+            high, low = notes[line:line + 1, lane:lane + PB], notes[lines + line:lines + line + 1, lane:lane + PB]
+            labels[r * blocks + k:r * blocks + k + 1, :] = high * ID_BASE + low
+        tops.append(notes[-1:, :PB])
+    index_copy = pltpu.make_async_copy(lots, index, index_sem)
+    index_copy.start()
+    stats[pl.ds(kept + blocks, 8), :] = jnp.broadcast_to(functools.reduce(jnp.maximum, tops), (8, PB))
     place = lax.broadcasted_iota(jnp.int32, (HEAD, PB), 0)
     units = jnp.where(place == 0, float(ID_BASE), jnp.where(place == 1, 1.0, 0.0)).astype(jnp.bfloat16)
-    top = [narrow[narrow.shape[0] - HEAD:, :PB].astype(jnp.float32)[HEAD - 1:] for narrow in narrows]
-    stats[pl.ds(kept + blocks, 8), :] = jnp.broadcast_to(functools.reduce(jnp.maximum, top), (8, PB))
     target_copy.wait()
+    index_copy.wait()
     for copy in copies:
         copy.wait()
     for k in range(users):
@@ -79,10 +136,10 @@
 
     def advance(step, _):
         for r in range(peers):
-            first = (r * blocks + step) * picks
+            bases = [index[r * blocks + step, k] for k in range(picks)]
             narrow = block_of(narrows[r], step)
-            candidates = gather_slabs(table, index, first, picks, per_piece, stride, slab)
-            ids = gather_slabs(items, index, first, picks, per_piece, stride, slab)
+            candidates = gather_slabs(table, bases, per_piece, stride, slab)
+            ids = gather_slabs(items, bases, per_piece, stride, slab)
             score = lax.dot_general(candidates, narrow, NT, preferred_element_type=jnp.float32)
             masked = jnp.where(ids == labels[pl.ds(r * blocks + step, 1), :], -1e30, score)
             scores[step, r] = masked
@@ -98,7 +155,7 @@
             stats[pl.ds((peers + r) * blocks + step, 1), :] = total
         return 0
 
-    lax.fori_loop(0, blocks, advance, 0)
+    lax.fori_loop(0, blocks, advance, 0, unroll=2)
 
 
 def tree_sum(terms):
@@ -144,12 +201,12 @@
                 near[step] = grad
             else:
                 far[step, r - 1] = grad
-                first = (r * blocks + step) * picks
-                candidates = gather_slabs(table, index, first, picks, per_piece, stride, slab)
+                bases = [index[r * blocks + step, k] for k in range(picks)]
+                candidates = gather_slabs(table, bases, per_piece, stride, slab)
                 hiddens[r - 1][span, :] = lax.dot_general(grad, candidates, TN, preferred_element_type=jnp.float32)
         return 0
 
-    lax.fori_loop(0, blocks, advance, 0)
+    lax.fori_loop(0, blocks, advance, 0, unroll=2)
 
 
 def table_kernel(dims, index, *refs):
@@ -163,30 +220,45 @@
         for r in range(peers):
             grad = near[step] if r == 0 else far[step, r - 1]
             rows = jnp.dot(grad, block_of(narrows[r], step), preferred_element_type=jnp.float32)
-            first = (r * blocks + step) * picks
             for k in range(picks):
-                place = pl.ds(pl.multiple_of(index[first + k] * slab, 16), slab)
+                place = pl.ds(pl.multiple_of(index[r * blocks + step, k] * slab, 16), slab)
                 partial[place, :] += rows[k * slab:(k + 1) * slab]
         return 0
 
-    lax.fori_loop(0, blocks, advance, 0)
-
-
-def hidden_kernel(dims, index, near, table, pos_grad, target, out):
+    lax.fori_loop(0, blocks, advance, 0, unroll=2)
+
+
+def hidden_kernel(dims, index, near, table, pos_grad, target, from_core, out):
     peers, blocks, picks, users, per_piece, slab = dims
     stride = per_piece * slab + HEAD
 
     def advance(step, _):
         span = pl.ds(pl.multiple_of(step * PB, PB), PB)
-        candidates = gather_slabs(table, index, step * picks, picks, per_piece, stride, slab)
+        candidates = gather_slabs(table, [index[step, k] for k in range(picks)], per_piece, stride, slab)
         result = lax.dot_general(near[step], candidates, TN, preferred_element_type=jnp.float32)
         row = jnp.broadcast_to(pos_grad[pl.ds(step, 1), :], (PB, PB)).T
         wide = block_of(target, step).astype(jnp.float32)
         for k in range(0, wide.shape[1], PB):
-            out[span, k:k + PB] = result[:, k:k + PB] + row * wide[:, k:k + PB]
+            out[span, k:k + PB] = result[:, k:k + PB] + row * wide[:, k:k + PB] + from_core[span, k:k + PB]
         return 0
 
-    lax.fori_loop(0, blocks, advance, 0)
+    lax.fori_loop(0, blocks, advance, 0, unroll=2)
+
+
+def order_kernel(dims, rank, *refs):
+    peers, blocks, picks, users, per_piece, slab = dims
+    quarters, out, sems = refs[:peers], refs[peers], refs[peers + 1]
+    copies = []
+    for q, quarter in enumerate(quarters):
+        for k in range(per_piece):
+            place = pl.multiple_of(k * NB + (rank[0] ^ q) * slab, slab)
+            copies.append(pltpu.make_async_copy(
+                quarter.at[pl.ds(k * slab, slab)], out.at[pl.ds(place, slab)], sems.at[q * per_piece + k]
+            ))
+    for copy in copies:
+        copy.start()
+    for copy in copies:
+        copy.wait()
 
 
 def per_device(hidden, target, pool_table, pool_items, labels, chosen, offsets):
@@ -202,28 +274,35 @@
     factor = 1.0 / (users * (offsets.shape[1] - 1))
     f32, bf16 = jnp.float32, jnp.bfloat16
 
-    narrow = hidden[0].astype(bf16)
-    largest = jnp.max(jnp.abs(narrow))
-
     def halves(whole_numbers):
         numbers = whole_numbers.reshape(-1)
         numbers = jnp.pad(numbers, (0, -numbers.shape[0] % features)).reshape(-1, features)
         return [(numbers // ID_BASE).astype(bf16), (numbers % ID_BASE).astype(bf16)]
 
-    def whole_again(array, row, count):
-        lines = -(-count // features)
-        high, low = array[row:row + lines], array[row + lines:row + 2 * lines]
-        return (high.astype(f32) * ID_BASE + low.astype(f32)).reshape(-1)[:count], row + 2 * lines
-
     own_rows = lax.dynamic_slice_in_dim(pool_table.reshape(per_piece, NB, features), peer * slab, slab, axis=1)
     own_ids = lax.dynamic_slice_in_dim(pool_items.reshape(per_piece, NB), peer * slab, slab, axis=1)
     spare = jnp.zeros((HEAD - 2, features), bf16)
     piece = jnp.concatenate([own_rows.reshape(rows, features)] + halves(own_ids) + [spare])
 
-    notes = halves(labels) + halves(chosen)
-    spare = -(sum(note.shape[0] for note in notes) + 1) % HEAD
-    notes += [jnp.zeros((spare, features), bf16), jnp.broadcast_to(largest, (1, features))]
-    packed = jnp.concatenate([narrow] + notes)
+    in_vmem, in_smem = pl.BlockSpec(memory_space=pltpu.VMEM), pl.BlockSpec(memory_space=pltpu.SMEM)
+    in_hbm = pl.BlockSpec(memory_space=pltpu.HBM)
+    params = pltpu.CompilerParams(vmem_limit_bytes=VMEM)
+    _, first_lot, note_rows = note_places(length, features, blocks)
+    packed = pl.pallas_call(
+        pack_kernel,
+        in_specs=[in_hbm] * 3,
+        out_specs=in_vmem,
+        out_shape=jax.ShapeDtypeStruct((length + note_rows, features), bf16),
+        scratch_shapes=[
+            pltpu.VMEM(labels.shape, jnp.int32),
+            pltpu.VMEM(chosen.shape[1:], jnp.int32),
+            pltpu.VMEM((length, features), f32),
+            pltpu.VMEM((blocks, features), f32),
+            pltpu.SemaphoreType.DMA((4,)),
+            pltpu.SemaphoreType.DMA((2,)),
+        ],
+        compiler_params=params, name="states",
+    )(*[pltpu.with_memory_space_constraint(x, pltpu.HBM) for x in (labels, chosen[0], hidden[0])])
 
     pieces = {0: piece, 1: swap(piece, "users", 1)}
     states = {0: packed}
@@ -248,50 +327,43 @@
     narrows = [states[q] for q in range(peers)]
     pieces = [pieces[q] for q in range(users)]
 
-    label_rows, picked = [], []
-    for state in narrows:
-        line, row = whole_again(state, length, length)
-        label_rows.append(line.reshape(blocks, PB))
-        line, row = whole_again(state, row, blocks * picks)
-        picked.append(line.astype(jnp.int32))
-    label_rows, picked = jnp.concatenate(label_rows), jnp.concatenate(picked)
-    owner = picked // per_piece
-    index = (owner ^ user) * per_piece + picked % per_piece
-
     owners = peer ^ jnp.arange(peers, dtype=jnp.int32)
     positions = owners[:, None] * length + jnp.arange(length, dtype=jnp.int32)[None, :]
     weights = history_weights(offsets[0], positions).reshape(peers * blocks, PB)
-    weights, label_rows, index = lax.optimization_barrier((weights, label_rows, index))
+    weights, narrows = lax.optimization_barrier((weights, narrows))
 
     dims = (peers, blocks, picks, users, per_piece, slab)
     half = features // 2
     stat_rows = (2 * peers + 1) * blocks + 8
-    in_vmem, in_smem = pl.BlockSpec(memory_space=pltpu.VMEM), pl.BlockSpec(memory_space=pltpu.SMEM)
-    in_hbm = pl.BlockSpec(memory_space=pltpu.HBM)
     cost = pl.CostEstimate(flops=1 << 20, bytes_accessed=1 << 20, transcendentals=0)
-    params = pltpu.CompilerParams(vmem_limit_bytes=VMEM)
 
     def call(kernel, name, outs, scratch, rows_of, *operands, unplaced=0):
         placed = len(operands) - unplaced
         return pl.pallas_call(
             kernel,
             in_specs=[in_smem] + [in_vmem] * placed + [in_hbm] * unplaced,
-            out_specs=[in_vmem] * len(outs),
+            out_specs=[in_smem if dtype == jnp.int32 else in_vmem for _, dtype in outs],
             out_shape=[jax.ShapeDtypeStruct(shape, dtype) for shape, dtype in outs],
             scratch_shapes=scratch,
             compiler_params=params, cost_estimate=cost, name=name,
         )(rows_of, *operands[:placed], *[pltpu.with_memory_space_constraint(x, pltpu.HBM) for x in operands[placed:]])
 
-    scores, stats, table = call(
+    scores, stats, table, index = call(
         functools.partial(score_kernel, dims), "scores",
-        [((blocks, peers, wide, PB), f32), ((stat_rows, PB), f32), ((users * stride, features), bf16)],
+        [
+            ((blocks, peers, wide, PB), f32), ((stat_rows, PB), f32), ((users * stride, features), bf16),
+            ((peers * blocks, PB), jnp.int32),
+        ],
         [
             pltpu.VMEM((users * stride, PB), f32),
             pltpu.VMEM((length, features), bf16),
+            pltpu.VMEM((peers * blocks, PB), f32),
+            pltpu.VMEM((peers * blocks, PB), jnp.int32),
             pltpu.SemaphoreType.DMA((users,)),
             pltpu.SemaphoreType.DMA,
+            pltpu.SemaphoreType.DMA,
         ],
-        index, label_rows, *narrows, target[0], *pieces, unplaced=1 + users,
+        user.reshape(1), *narrows, target[0], *pieces, unplaced=1 + users,
     )
     all_stats = [stats] + [swap(stats, "seq", q) for q in range(1, peers)]
 
@@ -376,7 +448,7 @@
         hidden_arrived.append(with_far(hidden_coded))
         (own_hidden,) = call(
             functools.partial(hidden_kernel, dims), "own_hidden_grads", [state_out], [],
-            index, near, table, pos_grad, target[0],
+            index, near, table, pos_grad, target[0], own_core,
         )
         arrived, own_hidden, hidden_arrived = lax.optimization_barrier((arrived, own_hidden, hidden_arrived))
         owned = added(parts[0], *[(part, top) for part in arrived])
@@ -394,23 +466,29 @@
         own_core = swap(hiddens[0], "seq", 1)
         (own_hidden,) = call(
             functools.partial(hidden_kernel, dims), "own_hidden_grads", [state_out], [],
-            index, near, table, pos_grad, target[0],
+            index, near, table, pos_grad, target[0], own_core,
         )
 
-    quarters = {0: owned, 1: swap(owned, "seq", 1)}
-    for q in range(2, peers, 2):
-        coded_owned = swap(coded(owned, top), "seq", q)
-        quarters[q] = added(0.0, (coded_owned, top))
-        quarters[q + 1] = added(0.0, (swap(coded_owned, "seq", 1), top))
-    grad_hidden = own_hidden + own_core
+    grad_hidden = own_hidden
     for k in range(peers // 2 - 1):
         part = jnp.concatenate([lanes[k] for lanes in hidden_arrived], axis=1)
         grad_hidden = grad_hidden + part.astype(f32) * (1.0 / hidden_scale)
-    grad_table = jnp.zeros((per_piece, peers, slab, features), f32)
-    for q in range(peers):
-        quarter = quarters[q].reshape(per_piece, 1, slab, features)
-        grad_table = lax.dynamic_update_slice_in_dim(grad_table, quarter, peer ^ q, axis=1)
-    return word[0, 0], grad_hidden[None], grad_table.reshape(pool_table.shape)
+    quarters = {0: owned, 1: swap(owned, "seq", 1)}
+    for q in range(2, peers, 2):
+        quarters[q] = swap(coded(owned, top), "seq", q)
+    quarters, grad_hidden = lax.optimization_barrier((quarters, grad_hidden))
+    for q in range(2, peers, 2):
+        far = quarters[q]
+        quarters[q], quarters[q + 1] = added(0.0, (far, top)), added(0.0, (swap(far, "seq", 1), top))
+    grad_table = pl.pallas_call(
+        functools.partial(order_kernel, dims),
+        in_specs=[in_smem] + [in_vmem] * peers,
+        out_specs=in_hbm,
+        out_shape=jax.ShapeDtypeStruct(pool_table.shape, f32),
+        scratch_shapes=[pltpu.SemaphoreType.DMA((peers * per_piece,))],
+        compiler_params=params, name="ordered_table_grads",
+    )(peer.reshape(1), *[quarters[q] for q in range(peers)])
+    return word[0, 0], grad_hidden[None], grad_table
 
 
 def solution(mesh):

time: 124 us -> 114 us (0.919)
  local copies, waits for them, and re-layouts: 9.76 us -> 1.06 us
  other arithmetic: 11.5 us -> 3.7 us
  waiting for transfers between devices: 48.3 us -> 53.1 us
  starting transfers between devices: 27 us -> 29.1 us
    ppermute x30, waiting for transfers between devices: 48.3 us -> 53.1 us  [swap(): return lax.ppermute(array, axis, [(i, i ^ mask) for i in range(count)])]
    broadcast_in_dim x1 -> x0, other arithmetic: 3.73 us -> none  [per_device(): return (word[0, 0], grad_hidden[None], grad_table.reshape(pool_table.shape))]
    pallas_call x0 -> x2, Pallas kernels: none -> 3.29 us  [the longest x1 1.85 us: per_device(): pl.pallas_call(pack_kernel, in_specs=[in_hbm] * 3, out_specs=in_vmem, out...]
    reduce_max x1 -> x0, other arithmetic: 2.42 us -> none  [per_device(): largest = jnp.max(jnp.abs(narrow))]
    pallas_call x4, Pallas kernels: 25.4 us -> 23.1 us  [call(): pl.pallas_call(kernel, in_specs=[in_smem] + [in_vmem] * placed + [in_hbm]...]
    dynamic_update_slice x4 -> x0, local copies, waits for them, and re-layouts: 2.26 us -> none  [per_device(): lax.dynamic_update_slice_in_dim(grad_table, quarter, peer ^ q, axis=1)]
    ppermute x30, starting transfers between devices: 27 us -> 29.1 us  [swap(): return lax.ppermute(array, axis, [(i, i ^ mask) for i in range(count)])]
    unnamed x19 -> x16, local copies, waits for them, and re-layouts: 2.11 us -> 0.19 us
  transfers between devices with their start and end apart: 30 -> 30, of which waited for: 16 -> 16; matrix products, arithmetic and copies ran while one was open for 14% -> 4% of each run, Pallas kernels for 8% -> 8%
where the time goes in v4:
time: 114 us
  waiting for transfers between devices  53.1 us (47%)
  starting transfers between devices  29.1 us (26%)
  Pallas kernels  26.4 us (23%)
  other arithmetic  3.7 us (3%)
    ppermute x30, waiting for transfers between devices, swap(): return lax.ppermute(array, axis, [(i, i ^ mask) for i in range(count)])  53.1 us
    ppermute x30, starting transfers between devices, swap(): return lax.ppermute(array, axis, [(i, i ^ mask) for i in range(count)])  29.1 us
    pallas_call x4, Pallas kernels, call(): pl.pallas_call(kernel, in_specs=[in_smem] + [in_vmem] * placed + [in_hbm]...  23.1 us
  transfers between devices with their start and end apart: 30, of which 16 were waited for; matrix products, arithmetic and copies ran while one was open for 4% of the time, Pallas kernels for 8%

profile of v4, /device:TPU:0, one launch (start us, length us, event | category | flops | bytes accessed | tf_op | source)
XLA Modules:
  0.0 114.2 jit_solution(16498701884429233403)
XLA Ops:
  0.7 1.8 %states.1.refs_0_.refs_2_ = bf16[1040,512]{1,0:T(8,128)(2,1)S(1)} custom-call(s32[1,1024]{1,0:T(1,128)} %labels_from.1, s32[8,8]{1,0:T(8,128)} %bitcast.31, f32[1024,512]{1,0:T(8,128)} %bitcast.28), custom_call_target="tpu_custom_call" | custom-call | tf_op jit(solution)/shard_map/states/pallas_call | solution.py:291
  2.5 3.0 %collective-permute-start.6 = (bf16[1040,512]{1,0:T(8,128)(2,1)S(1)}, bf16[1040,512]{1,0:T(8,128)(2,1)S(1)}, u32[]{:S(2)}, u32[]{:S(2)}) collective-permute-start(bf16[1040,512]{1,0:T(8,128)(2,1)S(1)} %states.1.refs_0_.refs_2_), channel_id=1, source_target_pairs={{0,16},{8,24},{16,0},{24,8},{1,17},{9,25},{17,1},{25,9},{2,18},{10... | collective-permute-start | bytes 3194888 | tf_op jit(solution)/shard_map/ppermute | solution.py:20
  5.6 0.1 constant_dynamic-slice_fusion
  5.6 0.1 reshape.346
  5.8 0.1 pad.26.clone
  5.9 0.1 maximum_maximum_fusion.refs_5_
  6.0 1.6 %collective-permute-start = (bf16[272,512]{1,0:T(8,128)(2,1)S(1)}, bf16[272,512]{1,0:T(8,128)(2,1)}, u32[]{:S(2)}, u32[]{:S(2)}) collective-permute-start(bf16[272,512]{1,0:T(8,128)(2,1)S(1)} %maximum_maximum_fusion.refs_5_), channel_id=1, source_target_pairs={{0,1},{1,0},{2,3},{3,2},{4,5},{5,4},{6,7},{7,6},{8,9},{9,8},{10,11... | collective-permute-start | bytes 835592 | tf_op jit(solution)/shard_map/ppermute | solution.py:20
  7.6 1.6 %collective-permute-start.1 = (bf16[272,512]{1,0:T(8,128)(2,1)S(1)}, bf16[272,512]{1,0:T(8,128)(2,1)S(1)}, u32[]{:S(2)}, u32[]{:S(2)}) collective-permute-start(bf16[272,512]{1,0:T(8,128)(2,1)S(1)} %maximum_maximum_fusion.refs_5_), channel_id=1, source_target_pairs={{0,2},{1,3},{2,0},{3,1},{4,6},{5,7},{6,4},{7,5},{8,10},{9,11},{10,... | collective-permute-start | bytes 835592 | tf_op jit(solution)/shard_map/ppermute | solution.py:20
  9.1 2.6 %collective-permute-start.2 = (bf16[272,512]{1,0:T(8,128)(2,1)S(1)}, bf16[272,512]{1,0:T(8,128)(2,1)S(1)}, u32[]{:S(2)}, u32[]{:S(2)}) collective-permute-start(bf16[272,512]{1,0:T(8,128)(2,1)S(1)} %maximum_maximum_fusion.refs_5_), channel_id=1, source_target_pairs={{0,4},{1,5},{2,6},{3,7},{4,0},{5,1},{6,2},{7,3},{8,12},{9,13},{10,... | collective-permute-start | bytes 835592 | tf_op jit(solution)/shard_map/ppermute | solution.py:20
  11.7 2.6 %collective-permute-done.refs_6_ = bf16[272,512]{1,0:T(8,128)(2,1)} collective-permute-done((bf16[272,512]{1,0:T(8,128)(2,1)S(1)}, bf16[272,512]{1,0:T(8,128)(2,1)}, u32[]{:S(2)}, u32[]{:S(2)}) %collective-permute-start) | collective-permute-done | bytes 278560 | tf_op jit(solution)/shard_map/ppermute | solution.py:20
  14.3 7.0 %collective-permute-done.1.refs_7_ = bf16[272,512]{1,0:T(8,128)(2,1)S(1)} collective-permute-done((bf16[272,512]{1,0:T(8,128)(2,1)S(1)}, bf16[272,512]{1,0:T(8,128)(2,1)S(1)}, u32[]{:S(2)}, u32[]{:S(2)}) %collective-permute-start.1) | collective-permute-done | bytes 278560 | tf_op jit(solution)/shard_map/ppermute | solution.py:20
  21.3 2.5 %collective-permute-done.2.refs_9_ = bf16[272,512]{1,0:T(8,128)(2,1)S(1)} collective-permute-done((bf16[272,512]{1,0:T(8,128)(2,1)S(1)}, bf16[272,512]{1,0:T(8,128)(2,1)S(1)}, u32[]{:S(2)}, u32[]{:S(2)}) %collective-permute-start.2) | collective-permute-done | bytes 278560 | tf_op jit(solution)/shard_map/ppermute | solution.py:20
  23.7 0.4 collective-permute-start.3
  24.2 0.4 collective-permute-start.4
  24.6 5.7 %collective-permute-done.3.refs_10_ = bf16[272,512]{1,0:T(8,128)(2,1)S(1)} collective-permute-done((bf16[272,512]{1,0:T(8,128)(2,1)S(1)}, bf16[272,512]{1,0:T(8,128)(2,1)S(1)}, u32[]{:S(2)}, u32[]{:S(2)}) %collective-permute-start.3) | collective-permute-done | bytes 278560 | tf_op jit(solution)/shard_map/ppermute | solution.py:20
  30.3 0.5 collective-permute-done.4.refs_11_
  30.8 0.1 copy-done.5
  31.0 0.4 collective-permute-start.7
  31.5 0.1 iota_add_fusion
  31.6 1.6 %collective-permute-start.9 = (bf16[272,512]{1,0:T(8,128)(2,1)}, bf16[272,512]{1,0:T(8,128)(2,1)}, u32[]{:S(2)}, u32[]{:S(2)}) collective-permute-start(bf16[272,512]{1,0:T(8,128)(2,1)} %collective-permute-done.4.refs_11_), channel_id=1, source_target_pairs={{0,1},{1,0},{2,3},{3,2},{4,5},{5,4},{6,7},{7,6},{8,9},{9,8},{10,11... | collective-permute-start | bytes 835592 | tf_op jit(solution)/shard_map/ppermute | solution.py:20
  33.2 0.4 collective-permute-start.8
  33.5 0.1 convert_divide_fusion
  33.6 0.1 select_reduce_fusion
  33.8 1.4 %collective-permute-done.7.refs_3_.refs_5_ = bf16[1040,512]{1,0:T(8,128)(2,1)} collective-permute-done((bf16[1040,512]{1,0:T(8,128)(2,1)S(1)}, bf16[1040,512]{1,0:T(8,128)(2,1)}, u32[]{:S(2)}, u32[]{:S(2)}) %collective-permute-start.7) | collective-permute-done | bytes 1064992 | tf_op jit(solution)/shard_map/ppermute | solution.py:20
  35.1 6.6 %collective-permute-done.8.refs_8_ = bf16[272,512]{1,0:T(8,128)(2,1)} collective-permute-done((bf16[272,512]{1,0:T(8,128)(2,1)}, bf16[272,512]{1,0:T(8,128)(2,1)}, u32[]{:S(2)}, u32[]{:S(2)}) %collective-permute-start.8) | collective-permute-done | bytes 278560 | tf_op jit(solution)/shard_map/ppermute | solution.py:20
  41.8 10.3 %scores.1 = (f32[8,4,512,128]{3,2,1,0:T(8,128)S(1)}, f32[80,128]{1,0:T(8,128)S(1)}, bf16[2176,512]{1,0:T(8,128)(2,1)S(1)}, s32[32,128]{1,0:T(8,128)S(1)}) custom-call(s32[1]{0:T(128)} %bitcast.user, bf16[1040,512]{1,0:T(8,128)(2,1)S(1)} %states.1.refs_0_.refs_2_, bf16[1040,512]{1,0:T(8,128)(2,1)} %collective-permute-done.5.refs_1_.refs_3_, ...), custom_call_target="tpu_custom_call" | custom-call | flops 1048576 | bytes 1048576 | tf_op jit(solution)/shard_map/scores/pallas_call | solution.py:342
  52.2 0.6 collective-permute-start.11
  52.7 1.3 %collective-permute-start.12 = (f32[80,128]{1,0:T(8,128)S(1)}, f32[80,128]{1,0:T(8,128)S(1)}, u32[]{:S(2)}, u32[]{:S(2)}) collective-permute-start(f32[80,128]{1,0:T(8,128)S(1)} %get-tuple-element.75.refs_3_), channel_id=1, source_target_pairs={{0,24},{8,16},{16,8},{24,0},{1,25},{9,17},{17,9},{25,1},{2,26},{10... | collective-permute-start | bytes 122888 | tf_op jit(solution)/shard_map/ppermute | solution.py:20
  54.0 2.6 %collective-permute-done.11.refs_5_ = f32[80,128]{1,0:T(8,128)S(1)} collective-permute-done((f32[80,128]{1,0:T(8,128)S(1)}, f32[80,128]{1,0:T(8,128)S(1)}, u32[]{:S(2)}, u32[]{:S(2)}) %collective-permute-start.11) | collective-permute-done | bytes 40992 | tf_op jit(solution)/shard_map/ppermute | solution.py:20
  56.6 3.8 %grads.1 = (bf16[8,512,128]{2,1,0:T(8,128)(2,1)S(1)}, bf16[8,3,512,128]{3,2,1,0:T(8,128)(2,1)S(1)}, f32[8,128]{1,0:T(8,128)S(1)}, f32[8,128]{1,0:T(8,128)S(1)}, ...) custom-call(s32[32,128]{1,0:T(8,128)S(1)} %get-tuple-element.71.index, ...), custom_call_target="tpu_custom_call" | custom-call | flops 1048576 | bytes 1048576 | tf_op jit(solution)/shard_map/grads/pallas_call | solution.py:342
  60.4 0.3 collective-permute-start.13
  60.7 0.5 collective-permute-start.14
  61.3 6.8 %table_grads.1 = f32[2048,512]{1,0:T(8,128)S(1)} custom-call(s32[32,128]{1,0:T(8,128)S(1)} %get-tuple-element.71.index, bf16[8,512,128]{2,1,0:T(8,128)(2,1)S(1)} %get-tuple-element.94.refs_0_.near, bf16[8,3,512,128]{3,2,1,0:T(8,128)(2,1)S(1)} %get-tuple-element.78.refs_1_, bf16[1040,512]{1,0:T(8,128)(2,1)S(1)} %states.1.refs_0_.refs_2_, ...), custom_call_target="tpu_custom_call" | custom-call | flops 1048576 | bytes 1048576 | tf_op jit(solution)/shard_map/table_grads/pallas_call | solution.py:342
  68.1 0.1 maximum_select_fusion.2
  68.2 0.1 multiply_convert_fusion.8
  68.3 0.4 multiply_convert_fusion
  68.7 1.6 %collective-permute-start.15 = (f16[256,512]{1,0:T(8,128)(2,1)S(1)}, f16[256,512]{1,0:T(8,128)(2,1)S(1)}, u32[]{:S(2)}, u32[]{:S(2)}) collective-permute-start(f16[256,512]{1,0:T(8,128)(2,1)S(1)} %get-tuple-element.84), channel_id=1, source_target_pairs={{0,1},{1,0},{2,3},{3,2},{4,5},{5,4},{6,7},{7,6},{8,9},{9,8},{10,11... | collective-permute-start | bytes 786440 | tf_op jit(solution)/shard_map/ppermute | solution.py:20
  70.3 0.5 collective-permute-start.16
  70.8 1.5 %collective-permute-start.17 = (f32[8,128]{1,0:T(8,128)S(1)}, f32[8,128]{1,0:T(8,128)S(1)}, u32[]{:S(2)}, u32[]{:S(2)}) collective-permute-start(f32[8,128]{1,0:T(8,128)S(1)} %maximum_select_fusion.2), channel_id=1, source_target_pairs={{0,2},{1,3},{2,0},{3,1},{4,6},{5,7},{6,4},{7,5},{8,10},{9,11},{10,... | collective-permute-start | bytes 12296 | tf_op jit(solution)/shard_map/ppermute | solution.py:20
  72.3 1.1 %collective-permute-start.21 = (f16[1024,256]{1,0:T(8,128)(2,1)S(1)}, f16[1024,256]{1,0:T(8,128)(2,1)S(1)}, u32[]{:S(2)}, u32[]{:S(2)}) collective-permute-start(f16[1024,256]{1,0:T(8,128)(2,1)S(1)} %get-tuple-element.88), channel_id=1, source_target_pairs={{0,16},{8,24},{16,0},{24,8},{1,17},{9,25},{17,1},{25,9},{2,18},{10... | collective-permute-start | bytes 1572872 | tf_op jit(solution)/shard_map/ppermute | solution.py:20
  73.5 5.4 %collective-permute-done.17 = f32[8,128]{1,0:T(8,128)S(1)} collective-permute-done((f32[8,128]{1,0:T(8,128)S(1)}, f32[8,128]{1,0:T(8,128)S(1)}, u32[]{:S(2)}, u32[]{:S(2)}) %collective-permute-start.17) | collective-permute-done | bytes 4128 | tf_op jit(solution)/shard_map/ppermute | solution.py:20
  78.9 1.5 %collective-permute-start.20 = (f32[8,128]{1,0:T(8,128)S(1)}, f32[8,128]{1,0:T(8,128)S(1)}, u32[]{:S(2)}, u32[]{:S(2)}) collective-permute-start(f32[8,128]{1,0:T(8,128)S(1)} %maximum_select_fusion.1), channel_id=1, source_target_pairs={{0,4},{1,5},{2,6},{3,7},{4,0},{5,1},{6,2},{7,3},{8,12},{9,13},{10,... | collective-permute-start | bytes 12296 | tf_op jit(solution)/shard_map/ppermute | solution.py:20
  80.4 0.2 multiply_convert_fusion.6
  80.6 0.6 collective-permute-start.18
  81.2 1.6 %collective-permute-start.19 = (f16[256,512]{1,0:T(8,128)(2,1)S(1)}, f16[256,512]{1,0:T(8,128)(2,1)S(1)}, u32[]{:S(2)}, u32[]{:S(2)}) collective-permute-start(f16[256,512]{1,0:T(8,128)(2,1)S(1)} %get-tuple-element.114), channel_id=1, source_target_pairs={{0,2},{1,3},{2,0},{3,1},{4,6},{5,7},{6,4},{7,5},{8,10},{9,11},{10,... | collective-permute-start | bytes 786440 | tf_op jit(solution)/shard_map/ppermute | solution.py:20
  82.8 0.7 collective-permute-done.20
  83.5 2.3 %collective-permute-done.21 = f16[1024,256]{1,0:T(8,128)(2,1)S(1)} collective-permute-done((f16[1024,256]{1,0:T(8,128)(2,1)S(1)}, f16[1024,256]{1,0:T(8,128)(2,1)S(1)}, u32[]{:S(2)}, u32[]{:S(2)}) %collective-permute-start.21) | collective-permute-done | bytes 524320 | tf_op jit(solution)/shard_map/ppermute | solution.py:20
  85.8 2.1 %collective-permute-done.18 = f16[256,512]{1,0:T(8,128)(2,1)S(1)} collective-permute-done((f16[256,512]{1,0:T(8,128)(2,1)S(1)}, f16[256,512]{1,0:T(8,128)(2,1)S(1)}, u32[]{:S(2)}, u32[]{:S(2)}) %collective-permute-start.18) | collective-permute-done | bytes 262176 | tf_op jit(solution)/shard_map/ppermute | solution.py:20
  88.0 0.3 collective-permute-done.19
  88.3 1.0 collective-permute-start.26
  89.4 0.3 multiply_convert_fusion.3
  89.7 1.5 %collective-permute-start.23 = (f16[256,512]{1,0:T(8,128)(2,1)S(1)}, f16[256,512]{1,0:T(8,128)(2,1)S(1)}, u32[]{:S(2)}, u32[]{:S(2)}) collective-permute-start(f16[256,512]{1,0:T(8,128)(2,1)S(1)} %get-tuple-element.113), channel_id=1, source_target_pairs={{0,4},{1,5},{2,6},{3,7},{4,0},{5,1},{6,2},{7,3},{8,12},{9,13},{10,... | collective-permute-start | bytes 786440 | tf_op jit(solution)/shard_map/ppermute | solution.py:20
  91.3 0.7 collective-permute-start.24
  92.0 1.3 %collective-permute-start.25 = (f16[256,512]{1,0:T(8,128)(2,1)S(1)}, f16[256,512]{1,0:T(8,128)(2,1)S(1)}, u32[]{:S(2)}, u32[]{:S(2)}) collective-permute-start(f16[256,512]{1,0:T(8,128)(2,1)S(1)} %get-tuple-element.111), channel_id=1, source_target_pairs={{0,1},{1,0},{2,3},{3,2},{4,5},{5,4},{6,7},{7,6},{8,9},{9,8},{10,11... | collective-permute-start | bytes 786440 | tf_op jit(solution)/shard_map/ppermute | solution.py:20
  93.3 2.1 %own_hidden_grads.1 = f32[1024,512]{1,0:T(8,128)S(1)} custom-call(s32[32,128]{1,0:T(8,128)S(1)} %get-tuple-element.71.index, bf16[8,512,128]{2,1,0:T(8,128)(2,1)S(1)} %get-tuple-element.94.refs_0_.near, bf16[2176,512]{1,0:T(8,128)(2,1)S(1)} %get-tuple-element.74.refs_2_.table, f32[8,128]{1,0:T(8,128)S(1)} %get-tuple-element.95.pos_grad, ...), custom_call_target="tpu_custom_call" | custom-call | flops 1048576 | bytes 1048576 | tf_op jit(solution)/shard_map/own_hidden_grads/pallas_call | solution.py:342
  95.4 6.6 %collective-permute-done.23 = f16[256,512]{1,0:T(8,128)(2,1)S(1)} collective-permute-done((f16[256,512]{1,0:T(8,128)(2,1)S(1)}, f16[256,512]{1,0:T(8,128)(2,1)S(1)}, u32[]{:S(2)}, u32[]{:S(2)}) %collective-permute-start.23) | collective-permute-done | bytes 262176 | tf_op jit(solution)/shard_map/ppermute | solution.py:20
  102.0 0.2 multiply_convert_fusion.2
  102.3 1.2 %collective-permute-start.28 = (f16[256,512]{1,0:T(8,128)(2,1)S(1)}, f16[256,512]{1,0:T(8,128)(2,1)S(1)}, u32[]{:S(2)}, u32[]{:S(2)}) collective-permute-start(f16[256,512]{1,0:T(8,128)(2,1)S(1)} %get-tuple-element.109), channel_id=1, source_target_pairs={{0,16},{8,24},{16,0},{24,8},{1,17},{9,25},{17,1},{25,9},{2,18},{10... | collective-permute-start | bytes 786440 | tf_op jit(solution)/shard_map/ppermute | solution.py:20
  103.5 1.6 %multiply_add_fusion = f32[1024,512]{1,0:T(8,128)} fusion(f32[1024,512]{1,0:T(8,128)S(1)} %own_hidden_grads.1, f16[1024,256]{1,0:T(8,128)(2,1)S(1)} %collective-permute-done.26, f16[1024,256]{1,0:T(8,128)(2,1)S(1)} %collective-permute-done.21), kind=kLoop, calls=%fused_computation | loop fusion | flops 2097152 | bytes 5242880 | tf_op jit(solution)/shard_map/add | solution.py:475
  105.2 5.9 %collective-permute-done.28 = f16[256,512]{1,0:T(8,128)(2,1)S(1)} collective-permute-done((f16[256,512]{1,0:T(8,128)(2,1)S(1)}, f16[256,512]{1,0:T(8,128)(2,1)S(1)}, u32[]{:S(2)}, u32[]{:S(2)}) %collective-permute-start.28) | collective-permute-done | bytes 262176 | tf_op jit(solution)/shard_map/ppermute | solution.py:20
  111.1 0.5 slice.79
  111.6 1.0 collective-permute-done.29
  112.6 0.1 convert_multiply_fusion
  112.7 1.4 %ordered_table_grads.1 = f32[1024,512]{1,0:T(8,128)} custom-call(s32[1]{0:T(128)} %bitcast.14.rank, f32[256,512]{1,0:T(8,128)S(1)} %get-tuple-element.106.refs_0_, f32[256,512]{1,0:T(8,128)S(1)} %collective-permute-done.27.refs_1_, f32[256,512]{1,0:T(8,128)S(1)} %get-tuple-element.121.refs_2_, f32[256,512]{1,0:T(8,128)S(1)} %get-tuple-element.120.refs_3_), custom_call_target="tpu_custom_call" | custom-call | tf_op jit(solution)/shard_map/ordered_table_grads/pallas_call | solution.py:483
  (54 shorter events, 0.6 us)
Async XLA Ops:
  0.6 5.2 %copy-start = (bf16[1024,512]{1,0:T(8,128)(2,1)S(1)}, bf16[1024,512]{1,0:T(8,128)(2,1)}, u32[]{:S(2)}) copy-start(bf16[1024,512]{1,0:T(8,128)(2,1)} %param.9) | copy-start | bytes 3145732
  0.6 4.9 %copy-start.6 = (s32[1024]{0:T(1024)S(1)}, s32[1024]{0:T(1024)}, u32[]{:S(2)}) copy-start(s32[1024]{0:T(1024)} %param.10) | copy-start | bytes 12292
  0.7 30.8 %copy-start.7 = (s32[1,5]{1,0:T(1,128)S(1)}, s32[1,5]{1,0:T(1,128)}, u32[]{:S(2)}) copy-start(s32[1,5]{1,0:T(1,128)} %param.13) | copy-start | bytes 64
  2.5 28.3 %collective-permute-start.6 = (bf16[1040,512]{1,0:T(8,128)(2,1)S(1)}, bf16[1040,512]{1,0:T(8,128)(2,1)S(1)}, u32[]{:S(2)}, u32[]{:S(2)}) collective-permute-start(bf16[1040,512]{1,0:T(8,128)(2,1)S(1)} %states.1.refs_0_.refs_2_), channel_id=1, source_target_pairs={{0,16},{8,24},{16,0},{24,8},{1,17},{9,25},{17,1},{25,9},{2,18},{10... | collective-permute-start | bytes 3194888 | tf_op jit(solution)/shard_map/ppermute | solution.py:20
  6.0 35.8 %copy-start.2 = (bf16[272,512]{1,0:T(8,128)(2,1)}, bf16[272,512]{1,0:T(8,128)(2,1)S(1)}, u32[]{:S(2)}) copy-start(bf16[272,512]{1,0:T(8,128)(2,1)S(1)} %maximum_maximum_fusion.refs_5_) | copy-start | bytes 835588
  6.0 8.3 %collective-permute-start = (bf16[272,512]{1,0:T(8,128)(2,1)S(1)}, bf16[272,512]{1,0:T(8,128)(2,1)}, u32[]{:S(2)}, u32[]{:S(2)}) collective-permute-start(bf16[272,512]{1,0:T(8,128)(2,1)S(1)} %maximum_maximum_fusion.refs_5_), channel_id=1, source_target_pairs={{0,1},{1,0},{2,3},{3,2},{4,5},{5,4},{6,7},{7,6},{8,9},{9,8},{10,11... | collective-permute-start | bytes 835592 | tf_op jit(solution)/shard_map/ppermute | solution.py:20
  7.6 13.7 %collective-permute-start.1 = (bf16[272,512]{1,0:T(8,128)(2,1)S(1)}, bf16[272,512]{1,0:T(8,128)(2,1)S(1)}, u32[]{:S(2)}, u32[]{:S(2)}) collective-permute-start(bf16[272,512]{1,0:T(8,128)(2,1)S(1)} %maximum_maximum_fusion.refs_5_), channel_id=1, source_target_pairs={{0,2},{1,3},{2,0},{3,1},{4,6},{5,7},{6,4},{7,5},{8,10},{9,11},{10,... | collective-permute-start | bytes 835592 | tf_op jit(solution)/shard_map/ppermute | solution.py:20
  9.1 14.6 %collective-permute-start.2 = (bf16[272,512]{1,0:T(8,128)(2,1)S(1)}, bf16[272,512]{1,0:T(8,128)(2,1)S(1)}, u32[]{:S(2)}, u32[]{:S(2)}) collective-permute-start(bf16[272,512]{1,0:T(8,128)(2,1)S(1)} %maximum_maximum_fusion.refs_5_), channel_id=1, source_target_pairs={{0,4},{1,5},{2,6},{3,7},{4,0},{5,1},{6,2},{7,3},{8,12},{9,13},{10,... | collective-permute-start | bytes 835592 | tf_op jit(solution)/shard_map/ppermute | solution.py:20
  21.3 9.6 %copy-start.3 = (bf16[272,512]{1,0:T(8,128)(2,1)}, bf16[272,512]{1,0:T(8,128)(2,1)S(1)}, u32[]{:S(2)}) copy-start(bf16[272,512]{1,0:T(8,128)(2,1)S(1)} %collective-permute-done.1.refs_7_) | copy-start | bytes 835588
  23.7 7.1 %copy-start.4 = (bf16[272,512]{1,0:T(8,128)(2,1)}, bf16[272,512]{1,0:T(8,128)(2,1)S(1)}, u32[]{:S(2)}) copy-start(bf16[272,512]{1,0:T(8,128)(2,1)S(1)} %collective-permute-done.2.refs_9_) | copy-start | bytes 835588
  23.7 6.5 %collective-permute-start.3 = (bf16[272,512]{1,0:T(8,128)(2,1)S(1)}, bf16[272,512]{1,0:T(8,128)(2,1)S(1)}, u32[]{:S(2)}, u32[]{:S(2)}) collective-permute-start(bf16[272,512]{1,0:T(8,128)(2,1)S(1)} %collective-permute-done.2.refs_9_), channel_id=1, source_target_pairs={{0,1},{1,0},{2,3},{3,2},{4,5},{5,4},{6,7},{7,6},{8,9},{9,8},{10,11... | collective-permute-start | bytes 835592 | tf_op jit(solution)/shard_map/ppermute | solution.py:20
  24.2 6.7 %collective-permute-start.4 = (bf16[272,512]{1,0:T(8,128)(2,1)S(1)}, bf16[272,512]{1,0:T(8,128)(2,1)}, u32[]{:S(2)}, u32[]{:S(2)}) collective-permute-start(bf16[272,512]{1,0:T(8,128)(2,1)S(1)} %collective-permute-done.2.refs_9_), channel_id=1, source_target_pairs={{0,2},{1,3},{2,0},{3,1},{4,6},{5,7},{6,4},{7,5},{8,10},{9,11},{10,... | collective-permute-start | bytes 835592 | tf_op jit(solution)/shard_map/ppermute | solution.py:20
  30.3 0.7 copy-start.5
  30.8 3.0 %collective-permute-start.5 = (bf16[1040,512]{1,0:T(8,128)(2,1)S(1)}, bf16[1040,512]{1,0:T(8,128)(2,1)}, u32[]{:S(2)}, u32[]{:S(2)}) collective-permute-start(bf16[1040,512]{1,0:T(8,128)(2,1)S(1)} %states.1.refs_0_.refs_2_), channel_id=1, source_target_pairs={{0,8},{8,0},{16,24},{24,16},{1,9},{9,1},{17,25},{25,17},{2,10},{10... | collective-permute-start | bytes 3194888 | tf_op jit(solution)/shard_map/ppermute | solution.py:20
  31.0 4.2 %collective-permute-start.7 = (bf16[1040,512]{1,0:T(8,128)(2,1)S(1)}, bf16[1040,512]{1,0:T(8,128)(2,1)}, u32[]{:S(2)}, u32[]{:S(2)}) collective-permute-start(bf16[1040,512]{1,0:T(8,128)(2,1)S(1)} %collective-permute-done.6.refs_2_.refs_4_), channel_id=1, source_target_pairs={{0,8},{8,0},{16,24},{24,16},{1,9},{9,1},{17,25},{25,17},{2,10},{10... | collective-permute-start | bytes 3194888 | tf_op jit(solution)/shard_map/ppermute | solution.py:20
  31.6 10.2 %collective-permute-start.9 = (bf16[272,512]{1,0:T(8,128)(2,1)}, bf16[272,512]{1,0:T(8,128)(2,1)}, u32[]{:S(2)}, u32[]{:S(2)}) collective-permute-start(bf16[272,512]{1,0:T(8,128)(2,1)} %collective-permute-done.4.refs_11_), channel_id=1, source_target_pairs={{0,1},{1,0},{2,3},{3,2},{4,5},{5,4},{6,7},{7,6},{8,9},{9,8},{10,11... | collective-permute-start | bytes 835592 | tf_op jit(solution)/shard_map/ppermute | solution.py:20
  33.2 8.6 %collective-permute-start.8 = (bf16[272,512]{1,0:T(8,128)(2,1)}, bf16[272,512]{1,0:T(8,128)(2,1)}, u32[]{:S(2)}, u32[]{:S(2)}) collective-permute-start(bf16[272,512]{1,0:T(8,128)(2,1)} %collective-permute-done.refs_6_), channel_id=1, source_target_pairs={{0,2},{1,3},{2,0},{3,1},{4,6},{5,7},{6,4},{7,5},{8,10},{9,11},{10,... | collective-permute-start | bytes 835592 | tf_op jit(solution)/shard_map/ppermute | solution.py:20
  52.1 1.9 %collective-permute-start.10 = (f32[80,128]{1,0:T(8,128)S(1)}, f32[80,128]{1,0:T(8,128)S(1)}, u32[]{:S(2)}, u32[]{:S(2)}) collective-permute-start(f32[80,128]{1,0:T(8,128)S(1)} %get-tuple-element.75.refs_3_), channel_id=1, source_target_pairs={{0,8},{8,0},{16,24},{24,16},{1,9},{9,1},{17,25},{25,17},{2,10},{10... | collective-permute-start | bytes 122888 | tf_op jit(solution)/shard_map/ppermute | solution.py:20
  52.2 4.4 %collective-permute-start.11 = (f32[80,128]{1,0:T(8,128)S(1)}, f32[80,128]{1,0:T(8,128)S(1)}, u32[]{:S(2)}, u32[]{:S(2)}) collective-permute-start(f32[80,128]{1,0:T(8,128)S(1)} %get-tuple-element.75.refs_3_), channel_id=1, source_target_pairs={{0,16},{8,24},{16,0},{24,8},{1,17},{9,25},{17,1},{25,9},{2,18},{10... | collective-permute-start | bytes 122888 | tf_op jit(solution)/shard_map/ppermute | solution.py:20
  52.7 3.9 %collective-permute-start.12 = (f32[80,128]{1,0:T(8,128)S(1)}, f32[80,128]{1,0:T(8,128)S(1)}, u32[]{:S(2)}, u32[]{:S(2)}) collective-permute-start(f32[80,128]{1,0:T(8,128)S(1)} %get-tuple-element.75.refs_3_), channel_id=1, source_target_pairs={{0,24},{8,16},{16,8},{24,0},{1,25},{9,17},{17,9},{25,1},{2,26},{10... | collective-permute-start | bytes 122888 | tf_op jit(solution)/shard_map/ppermute | solution.py:20
  60.4 7.7 %collective-permute-start.13 = (f32[1024,512]{1,0:T(8,128)S(1)}, f32[1024,512]{1,0:T(8,128)S(1)}, u32[]{:S(2)}, u32[]{:S(2)}) collective-permute-start(f32[1024,512]{1,0:T(8,128)S(1)} %get-tuple-element.79), channel_id=1, source_target_pairs={{0,8},{8,0},{16,24},{24,16},{1,9},{9,1},{17,25},{25,17},{2,10},{10... | collective-permute-start | bytes 6291464 | tf_op jit(solution)/shard_map/ppermute | solution.py:20
  60.7 7.3 %collective-permute-start.14 = (f32[8,128]{1,0:T(8,128)S(1)}, f32[8,128]{1,0:T(8,128)S(1)}, u32[]{:S(2)}, u32[]{:S(2)}) collective-permute-start(f32[8,128]{1,0:T(8,128)S(1)} %get-tuple-element.76), channel_id=1, source_target_pairs={{0,1},{1,0},{2,3},{3,2},{4,5},{5,4},{6,7},{7,6},{8,9},{9,8},{10,11... | collective-permute-start | bytes 12296 | tf_op jit(solution)/shard_map/ppermute | solution.py:20
  61.3 21.6 %collective-permute-start.22 = (f32[1024,512]{1,0:T(8,128)S(1)}, f32[1024,512]{1,0:T(8,128)S(1)}, u32[]{:S(2)}, u32[]{:S(2)}) collective-permute-start(f32[1024,512]{1,0:T(8,128)S(1)} %get-tuple-element.89), channel_id=1, source_target_pairs={{0,8},{8,0},{16,24},{24,16},{1,9},{9,1},{17,25},{25,17},{2,10},{10... | collective-permute-start | bytes 6291464 | tf_op jit(solution)/shard_map/ppermute | solution.py:20
  68.7 10.1 %collective-permute-start.15 = (f16[256,512]{1,0:T(8,128)(2,1)S(1)}, f16[256,512]{1,0:T(8,128)(2,1)S(1)}, u32[]{:S(2)}, u32[]{:S(2)}) collective-permute-start(f16[256,512]{1,0:T(8,128)(2,1)S(1)} %get-tuple-element.84), channel_id=1, source_target_pairs={{0,1},{1,0},{2,3},{3,2},{4,5},{5,4},{6,7},{7,6},{8,9},{9,8},{10,11... | collective-permute-start | bytes 786440 | tf_op jit(solution)/shard_map/ppermute | solution.py:20
  70.3 8.5 %collective-permute-start.16 = (f16[256,512]{1,0:T(8,128)(2,1)S(1)}, f16[256,512]{1,0:T(8,128)(2,1)S(1)}, u32[]{:S(2)}, u32[]{:S(2)}) collective-permute-start(f16[256,512]{1,0:T(8,128)(2,1)S(1)} %get-tuple-element.85), channel_id=1, source_target_pairs={{0,2},{1,3},{2,0},{3,1},{4,6},{5,7},{6,4},{7,5},{8,10},{9,11},{10,... | collective-permute-start | bytes 786440 | tf_op jit(solution)/shard_map/ppermute | solution.py:20
  70.8 8.0 %collective-permute-start.17 = (f32[8,128]{1,0:T(8,128)S(1)}, f32[8,128]{1,0:T(8,128)S(1)}, u32[]{:S(2)}, u32[]{:S(2)}) collective-permute-start(f32[8,128]{1,0:T(8,128)S(1)} %maximum_select_fusion.2), channel_id=1, source_target_pairs={{0,2},{1,3},{2,0},{3,1},{4,6},{5,7},{6,4},{7,5},{8,10},{9,11},{10,... | collective-permute-start | bytes 12296 | tf_op jit(solution)/shard_map/ppermute | solution.py:20
  72.3 13.5 %collective-permute-start.21 = (f16[1024,256]{1,0:T(8,128)(2,1)S(1)}, f16[1024,256]{1,0:T(8,128)(2,1)S(1)}, u32[]{:S(2)}, u32[]{:S(2)}) collective-permute-start(f16[1024,256]{1,0:T(8,128)(2,1)S(1)} %get-tuple-element.88), channel_id=1, source_target_pairs={{0,16},{8,24},{16,0},{24,8},{1,17},{9,25},{17,1},{25,9},{2,18},{10... | collective-permute-start | bytes 1572872 | tf_op jit(solution)/shard_map/ppermute | solution.py:20
  78.9 4.6 %collective-permute-start.20 = (f32[8,128]{1,0:T(8,128)S(1)}, f32[8,128]{1,0:T(8,128)S(1)}, u32[]{:S(2)}, u32[]{:S(2)}) collective-permute-start(f32[8,128]{1,0:T(8,128)S(1)} %maximum_select_fusion.1), channel_id=1, source_target_pairs={{0,4},{1,5},{2,6},{3,7},{4,0},{5,1},{6,2},{7,3},{8,12},{9,13},{10,... | collective-permute-start | bytes 12296 | tf_op jit(solution)/shard_map/ppermute | solution.py:20
  80.4 12.8 %copy-start.1 = (bf16[1,1024,512]{2,1,0:T(8,128)(2,1)S(1)}, bf16[1,1024,512]{2,1,0:T(8,128)(2,1)}, u32[]{:S(2)}) copy-start(bf16[1,1024,512]{2,1,0:T(8,128)(2,1)} %param.8) | copy-start | bytes 3145732
  80.6 7.3 %collective-permute-start.18 = (f16[256,512]{1,0:T(8,128)(2,1)S(1)}, f16[256,512]{1,0:T(8,128)(2,1)S(1)}, u32[]{:S(2)}, u32[]{:S(2)}) collective-permute-start(f16[256,512]{1,0:T(8,128)(2,1)S(1)} %get-tuple-element.115), channel_id=1, source_target_pairs={{0,1},{1,0},{2,3},{3,2},{4,5},{5,4},{6,7},{7,6},{8,9},{9,8},{10,11... | collective-permute-start | bytes 786440 | tf_op jit(solution)/shard_map/ppermute | solution.py:20
  81.2 7.0 %collective-permute-start.19 = (f16[256,512]{1,0:T(8,128)(2,1)S(1)}, f16[256,512]{1,0:T(8,128)(2,1)S(1)}, u32[]{:S(2)}, u32[]{:S(2)}) collective-permute-start(f16[256,512]{1,0:T(8,128)(2,1)S(1)} %get-tuple-element.114), channel_id=1, source_target_pairs={{0,2},{1,3},{2,0},{3,1},{4,6},{5,7},{6,4},{7,5},{8,10},{9,11},{10,... | collective-permute-start | bytes 786440 | tf_op jit(solution)/shard_map/ppermute | solution.py:20
  88.3 13.7 %collective-permute-start.26 = (f16[1024,256]{1,0:T(8,128)(2,1)S(1)}, f16[1024,256]{1,0:T(8,128)(2,1)S(1)}, u32[]{:S(2)}, u32[]{:S(2)}) collective-permute-start(f16[1024,256]{1,0:T(8,128)(2,1)S(1)} %get-tuple-element.98), channel_id=1, source_target_pairs={{0,16},{8,24},{16,0},{24,8},{1,17},{9,25},{17,1},{25,9},{2,18},{10... | collective-permute-start | bytes 1572872 | tf_op jit(solution)/shard_map/ppermute | solution.py:20
  89.7 12.3 %collective-permute-start.23 = (f16[256,512]{1,0:T(8,128)(2,1)S(1)}, f16[256,512]{1,0:T(8,128)(2,1)S(1)}, u32[]{:S(2)}, u32[]{:S(2)}) collective-permute-start(f16[256,512]{1,0:T(8,128)(2,1)S(1)} %get-tuple-element.113), channel_id=1, source_target_pairs={{0,4},{1,5},{2,6},{3,7},{4,0},{5,1},{6,2},{7,3},{8,12},{9,13},{10,... | collective-permute-start | bytes 786440 | tf_op jit(solution)/shard_map/ppermute | solution.py:20
  91.3 10.8 %collective-permute-start.24 = (f16[256,512]{1,0:T(8,128)(2,1)S(1)}, f16[256,512]{1,0:T(8,128)(2,1)S(1)}, u32[]{:S(2)}, u32[]{:S(2)}) collective-permute-start(f16[256,512]{1,0:T(8,128)(2,1)S(1)} %get-tuple-element.112), channel_id=1, source_target_pairs={{0,2},{1,3},{2,0},{3,1},{4,6},{5,7},{6,4},{7,5},{8,10},{9,11},{10,... | collective-permute-start | bytes 786440 | tf_op jit(solution)/shard_map/ppermute | solution.py:20
  92.0 10.1 %collective-permute-start.25 = (f16[256,512]{1,0:T(8,128)(2,1)S(1)}, f16[256,512]{1,0:T(8,128)(2,1)S(1)}, u32[]{:S(2)}, u32[]{:S(2)}) collective-permute-start(f16[256,512]{1,0:T(8,128)(2,1)S(1)} %get-tuple-element.111), channel_id=1, source_target_pairs={{0,1},{1,0},{2,3},{3,2},{4,5},{5,4},{6,7},{7,6},{8,9},{9,8},{10,11... | collective-permute-start | bytes 786440 | tf_op jit(solution)/shard_map/ppermute | solution.py:20
  102.3 8.8 %collective-permute-start.27 = (f32[256,512]{1,0:T(8,128)S(1)}, f32[256,512]{1,0:T(8,128)S(1)}, u32[]{:S(2)}, u32[]{:S(2)}) collective-permute-start(f32[256,512]{1,0:T(8,128)S(1)} %get-tuple-element.106.refs_0_), channel_id=1, source_target_pairs={{0,8},{8,0},{16,24},{24,16},{1,9},{9,1},{17,25},{25,17},{2,10},{10... | collective-permute-start | bytes 1572872 | tf_op jit(solution)/shard_map/ppermute | solution.py:20
  102.3 8.7 %collective-permute-start.28 = (f16[256,512]{1,0:T(8,128)(2,1)S(1)}, f16[256,512]{1,0:T(8,128)(2,1)S(1)}, u32[]{:S(2)}, u32[]{:S(2)}) collective-permute-start(f16[256,512]{1,0:T(8,128)(2,1)S(1)} %get-tuple-element.109), channel_id=1, source_target_pairs={{0,16},{8,24},{16,0},{24,8},{1,17},{9,25},{17,1},{25,9},{2,18},{10... | collective-permute-start | bytes 786440 | tf_op jit(solution)/shard_map/ppermute | solution.py:20
  111.1 1.5 %collective-permute-start.29 = (f16[256,512]{1,0:T(8,128)(2,1)S(1)}, f16[256,512]{1,0:T(8,128)(2,1)S(1)}, u32[]{:S(2)}, u32[]{:S(2)}) collective-permute-start(f16[256,512]{1,0:T(8,128)(2,1)S(1)} %collective-permute-done.28), channel_id=1, source_target_pairs={{0,8},{8,0},{16,24},{24,16},{1,9},{9,1},{17,25},{25,17},{2,10},{10... | collective-permute-start | bytes 786440 | tf_op jit(solution)/shard_map/ppermute | solution.py:20

commit v5 on v4

--- a/solution.py
+++ b/solution.py
@@ -33,6 +33,14 @@
     return lines, 2 * lines, -(-(2 * lines + blocks + 1) // HEAD) * HEAD
 
 
+def is_late(users, slot):
+    return (slot & 3) == 3 if users == 8 else slot < 0
+
+
+def place_of(users, slot):
+    return jnp.where(is_late(users, slot), 6 + (slot >> 2), slot - (slot >> 2)) if users == 8 else slot
+
+
 def gather_slabs(table, bases, per_piece, stride, slab):
     rows = []
     for base in bases:
@@ -52,7 +60,7 @@
     return jnp.sum(folded.T, axis=0, keepdims=True)
 
 
-def pack_kernel(labels_from, chosen_from, hidden_from, packed, labels, chosen, hidden, lots, sems, note_sems):
+def pack_kernel(users, per_piece, user, labels_from, chosen_from, hidden_from, packed, labels, chosen, hidden, lots, sems, note_sems):
     note_copies = [
         pltpu.make_async_copy(labels_from, labels, note_sems.at[0]),
         pltpu.make_async_copy(chosen_from, chosen, note_sems.at[1]),
@@ -72,7 +80,15 @@
     lots[...] = jnp.zeros_like(lots)
     for copy in note_copies:
         copy.wait()
-    lots[:, :picks] = chosen[...].astype(jnp.float32)
+    columns = [chosen[:, k:k + 1] for k in range(picks)]
+    late = [is_late(users, (column // per_piece) ^ user[0]).astype(jnp.int32) for column in columns]
+    ranks = [
+        sum(((late[j] < late[k]) | ((late[j] == late[k]) & (j < k))).astype(jnp.int32) for j in range(picks))
+        for k in range(picks)
+    ]
+    for place in range(picks):
+        column = sum(jnp.where(rank == place, column, 0) for rank, column in zip(ranks, columns))
+        lots[:, place:place + 1] = column.astype(jnp.float32)
     row = lax.broadcasted_iota(jnp.int32, (count, features), 0)
     notes = jnp.zeros((count, features), jnp.float32)
     for k in range(lines):
@@ -92,13 +108,28 @@
     packed[length:, :] = notes.astype(jnp.bfloat16)
 
 
-def score_kernel(dims, user, *refs):
+def load_items(items, table, first, count, rows, stride):
+    place = lax.broadcasted_iota(jnp.int32, (HEAD, PB), 0)
+    units = jnp.where(place == 0, float(ID_BASE), jnp.where(place == 1, 1.0, 0.0)).astype(jnp.bfloat16)
+    for k in range(first, first + count):
+        items[k * stride:k * stride + rows, :] = lax.dot_general(
+            table[k * stride + rows:(k + 1) * stride, :rows], units, TN, preferred_element_type=jnp.float32
+        )
+
+
+def masked_scores(table, items, bases, narrow, label, per_piece, stride, slab):
+    candidates = gather_slabs(table, bases, per_piece, stride, slab)
+    ids = gather_slabs(items, bases, per_piece, stride, slab)
+    score = lax.dot_general(candidates, narrow, NT, preferred_element_type=jnp.float32)
+    return jnp.where(ids == label, -1e30, score)
+
+
+def early_kernel(dims, user, *refs):
     peers, blocks, picks, users, per_piece, slab = dims
-    narrows, target_from, pieces = refs[:peers], refs[peers], refs[1 + peers:-11]
-    scores, stats, table, index, items, target, labels, lots, sems, target_sem, index_sem = refs[-11:]
+    narrows, target_from, pieces = refs[:peers], refs[peers], refs[1 + peers:-12]
+    scores, table, items, index, labels, positives, tops, target, lots, sems, target_sem, index_sem = refs[-12:]
     rows = per_piece * slab
     stride = rows + HEAD
-    kept = 2 * peers * blocks
     length, features = target.shape
     lines, first_lot, _ = note_places(length, features, blocks)
 
@@ -110,52 +141,114 @@
     ]
     for copy in copies:
         copy.start()
-    tops = []
+    largest = []
     for r in range(peers):
         notes = narrows[r][length:, :].astype(jnp.float32)
         lot = notes[first_lot:first_lot + blocks, :PB].astype(jnp.int32)
-        lots[r * blocks:(r + 1) * blocks, :] = ((lot // per_piece) ^ user[0]) * per_piece + lot % per_piece
+        slot = place_of(users, (lot // per_piece) ^ user[0])
+        lots[r * blocks:(r + 1) * blocks, :] = slot * per_piece + lot % per_piece
         for k in range(blocks):
             line, lane = divmod(k * PB, features)
             high, low = notes[line:line + 1, lane:lane + PB], notes[lines + line:lines + line + 1, lane:lane + PB]
             labels[r * blocks + k:r * blocks + k + 1, :] = high * ID_BASE + low
-        tops.append(notes[-1:, :PB])
+        largest.append(notes[-1:, :PB])
     index_copy = pltpu.make_async_copy(lots, index, index_sem)
     index_copy.start()
-    stats[pl.ds(kept + blocks, 8), :] = jnp.broadcast_to(functools.reduce(jnp.maximum, tops), (8, PB))
-    place = lax.broadcasted_iota(jnp.int32, (HEAD, PB), 0)
-    units = jnp.where(place == 0, float(ID_BASE), jnp.where(place == 1, 1.0, 0.0)).astype(jnp.bfloat16)
+    tops[...] = jnp.broadcast_to(functools.reduce(jnp.maximum, largest), (8, PB))
     target_copy.wait()
     index_copy.wait()
     for copy in copies:
         copy.wait()
-    for k in range(users):
-        items[k * stride:k * stride + rows, :] = lax.dot_general(
-            table[k * stride + rows:(k + 1) * stride, :rows], units, TN, preferred_element_type=jnp.float32
-        )
+    load_items(items, table, 0, len(pieces), rows, stride)
+    last = len(pieces) * per_piece - 1
 
     def advance(step, _):
         for r in range(peers):
-            bases = [index[r * blocks + step, k] for k in range(picks)]
+            row = r * blocks + step
+            bases = [jnp.minimum(index[row, k], last) for k in range(picks // 2)]
             narrow = block_of(narrows[r], step)
-            candidates = gather_slabs(table, bases, per_piece, stride, slab)
-            ids = gather_slabs(items, bases, per_piece, stride, slab)
-            score = lax.dot_general(candidates, narrow, NT, preferred_element_type=jnp.float32)
-            masked = jnp.where(ids == labels[pl.ds(r * blocks + step, 1), :], -1e30, score)
-            scores[step, r] = masked
-            peak = jnp.max(masked, axis=0, keepdims=True)
-            total = jnp.sum(jnp.exp(masked - peak), axis=0, keepdims=True)
+            label = labels[pl.ds(row, 1), :]
+            scores[step, r] = masked_scores(table, items, bases, narrow, label, per_piece, stride, slab)
             if r == 0:
-                positive = lane_row(narrow.astype(jnp.float32) * block_of(target, step).astype(jnp.float32))
-                stats[pl.ds(kept + step, 1), :] = positive
-                higher = jnp.maximum(peak, positive)
-                total = total * jnp.exp(peak - higher) + jnp.exp(positive - higher)
-                peak = higher
-            stats[pl.ds(r * blocks + step, 1), :] = peak
-            stats[pl.ds((peers + r) * blocks + step, 1), :] = total
+                product = narrow.astype(jnp.float32) * block_of(target, step).astype(jnp.float32)
+                positives[pl.ds(step, 1), :] = lane_row(product)
         return 0
 
-    lax.fori_loop(0, blocks, advance, 0, unroll=2)
+    lax.fori_loop(0, blocks, advance, 0, unroll=4)
+
+
+def late_kernel(dims, index, *refs):
+    peers, blocks, picks, users, per_piece, slab = dims
+    narrows = refs[:peers]
+    first_scores, first_table, first_items, labels, positives = refs[peers:peers + 5]
+    pieces = refs[peers + 5:-5]
+    scores, stats, table, items, sems = refs[-5:]
+    rows = per_piece * slab
+    stride = rows + HEAD
+    kept = 2 * peers * blocks
+    half = picks // 2
+    middle = half * slab
+    early = first_table.shape[0] // stride
+
+    copies = [
+        pltpu.make_async_copy(piece, table.at[pl.ds((early + k) * stride, stride)], sems.at[k])
+        for k, piece in enumerate(pieces)
+    ]
+    for copy in copies:
+        copy.start()
+    table[:early * stride, :] = first_table[...]
+    items[:early * stride, :] = first_items[...]
+    stats[pl.ds(kept, blocks), :] = positives[...]
+
+    for copy in copies:
+        copy.wait()
+    load_items(items, table, early, len(pieces), rows, stride)
+
+    def summarise(row, first, second, positive):
+        peak = jnp.maximum(jnp.max(first, axis=0, keepdims=True), jnp.max(second, axis=0, keepdims=True))
+        total = jnp.sum(jnp.exp(first - peak) + jnp.exp(second - peak), axis=0, keepdims=True)
+        if positive is not None:
+            higher = jnp.maximum(peak, positive)
+            total = total * jnp.exp(peak - higher) + jnp.exp(positive - higher)
+            peak = higher
+        stats[pl.ds(row, 1), :] = peak
+        stats[pl.ds(peers * blocks + row, 1), :] = total
+
+    def advance(step, _):
+        for r in range(peers):
+            row = r * blocks + step
+            bases = [index[row, k] for k in range(half, picks)]
+            label = labels[pl.ds(row, 1), :]
+            second = masked_scores(
+                table, items, bases, block_of(narrows[r], step), label, per_piece, stride, slab
+            )
+            first = first_scores[step, r]
+            scores[step, r, :middle, :] = first
+            scores[step, r, middle:, :] = second
+            summarise(row, first, second, positives[pl.ds(step, 1), :] if r == 0 else None)
+        return 0
+
+    lax.fori_loop(0, blocks, advance, 0, unroll=4)
+
+    if pieces:
+        def repair(row, _):
+            @pl.when(index[row, half - 1] >= early * per_piece)
+            def _():
+                step = row % blocks
+                bases = [index[row, k] for k in range(half)]
+                label = labels[pl.ds(row, 1), :]
+                for r in range(peers):
+                    @pl.when(row // blocks == r)
+                    def _(r=r):
+                        first = masked_scores(
+                            table, items, bases, block_of(narrows[r], step), label, per_piece, stride, slab
+                        )
+                        scores[step, r, :middle, :] = first
+                        second = scores[step, r, middle:, :]
+                        summarise(row, first, second, positives[pl.ds(step, 1), :] if r == 0 else None)
+            return 0
+
+        lax.fori_loop(0, peers * blocks, repair, 0)
 
 
 def tree_sum(terms):
@@ -168,7 +261,8 @@
     peers, blocks, picks, users, per_piece, slab, factor = dims
     scores, weights, table = refs[:3]
     stats = refs[3:3 + peers]
-    outs = refs[3 + peers:]
+    largest, partner_largest = refs[3 + peers:5 + peers]
+    outs = refs[5 + peers:]
     near, far, pos_grad, word = outs[:4]
     hiddens, (peaks, ratios) = outs[4:3 + peers], outs[3 + peers:]
     kept = 2 * peers * blocks
@@ -188,8 +282,7 @@
         if r == 0:
             pos_grad[...] = weight * factor * (jnp.exp(positive - peak) / total - 1.0)
     word[:4, :] = jnp.broadcast_to(jnp.sum(tree_sum(terms), keepdims=True) * factor, (4, word.shape[1]))
-    top = jnp.maximum(stats[0][pl.ds(kept + blocks, 4), :], 1e-30)
-    word[4:, :] = top
+    word[4:, :] = jnp.maximum(jnp.maximum(largest[4:, :], partner_largest[4:, :]), 1e-30)
 
     def advance(step, _):
         span = pl.ds(pl.multiple_of(step * PB, PB), PB)
@@ -206,7 +299,7 @@
                 hiddens[r - 1][span, :] = lax.dot_general(grad, candidates, TN, preferred_element_type=jnp.float32)
         return 0
 
-    lax.fori_loop(0, blocks, advance, 0, unroll=2)
+    lax.fori_loop(0, blocks, advance, 0, unroll=8)
 
 
 def table_kernel(dims, index, *refs):
@@ -225,7 +318,7 @@
                 partial[place, :] += rows[k * slab:(k + 1) * slab]
         return 0
 
-    lax.fori_loop(0, blocks, advance, 0, unroll=2)
+    lax.fori_loop(0, blocks, advance, 0, unroll=4)
 
 
 def hidden_kernel(dims, index, near, table, pos_grad, target, from_core, out):
@@ -242,7 +335,7 @@
             out[span, k:k + PB] = result[:, k:k + PB] + row * wide[:, k:k + PB] + from_core[span, k:k + PB]
         return 0
 
-    lax.fori_loop(0, blocks, advance, 0, unroll=2)
+    lax.fori_loop(0, blocks, advance, 0, unroll=8)
 
 
 def order_kernel(dims, rank, *refs):
@@ -289,8 +382,8 @@
     params = pltpu.CompilerParams(vmem_limit_bytes=VMEM)
     _, first_lot, note_rows = note_places(length, features, blocks)
     packed = pl.pallas_call(
-        pack_kernel,
-        in_specs=[in_hbm] * 3,
+        functools.partial(pack_kernel, users, per_piece),
+        in_specs=[in_smem] + [in_hbm] * 3,
         out_specs=in_vmem,
         out_shape=jax.ShapeDtypeStruct((length + note_rows, features), bf16),
         scratch_shapes=[
@@ -302,19 +395,18 @@
             pltpu.SemaphoreType.DMA((2,)),
         ],
         compiler_params=params, name="states",
-    )(*[pltpu.with_memory_space_constraint(x, pltpu.HBM) for x in (labels, chosen[0], hidden[0])])
-
-    pieces = {0: piece, 1: swap(piece, "users", 1)}
-    states = {0: packed}
+    )(user.reshape(1), *[pltpu.with_memory_space_constraint(x, pltpu.HBM) for x in (labels, chosen[0], hidden[0])])
+
+    pairs = users // 2
+    pieces, states = {0: piece}, {0: packed}
+    for q in (4, 2, 1) if pairs == 4 else (1,):
+        pieces[q] = swap(piece, "users", q)
     for q in range(2, peers, 2):
         states[q] = swap(packed, "seq", q)
-    pairs = users // 2
     if pairs == 4:
-        pieces[4], pieces[2] = swap(piece, "users", 4), swap(piece, "users", 2)
-        pieces = lax.optimization_barrier(pieces)
+        pieces[4], pieces[2], pieces[1] = lax.optimization_barrier((pieces[4], pieces[2], pieces[1]))
         pieces[6], pieces[5] = swap(pieces[4], "users", 2), swap(pieces[4], "users", 1)
-        pieces = lax.optimization_barrier(pieces)
-        own, came = lax.optimization_barrier((packed, pieces[6]))
+        pieces[6], pieces[5], pieces[1], own = lax.optimization_barrier((pieces[6], pieces[5], pieces[1], packed))
         pieces[7], pieces[3] = swap(pieces[6], "users", 1), swap(pieces[1], "users", 2)
     else:
         for q in range(2, users, 2):
@@ -334,7 +426,7 @@
 
     dims = (peers, blocks, picks, users, per_piece, slab)
     half = features // 2
-    stat_rows = (2 * peers + 1) * blocks + 8
+    stat_rows = (2 * peers + 1) * blocks
     cost = pl.CostEstimate(flops=1 << 20, bytes_accessed=1 << 20, transcendentals=0)
 
     def call(kernel, name, outs, scratch, rows_of, *operands, unplaced=0):
@@ -348,23 +440,38 @@
             compiler_params=params, cost_estimate=cost, name=name,
         )(rows_of, *operands[:placed], *[pltpu.with_memory_space_constraint(x, pltpu.HBM) for x in operands[placed:]])
 
-    scores, stats, table, index = call(
-        functools.partial(score_kernel, dims), "scores",
+    early = [q for q in range(users) if not is_late(users, q)]
+    late = [q for q in range(users) if is_late(users, q)]
+    first_scores, first_table, first_items, index, label_rows, positives, tops = call(
+        functools.partial(early_kernel, dims), "early_scores",
         [
-            ((blocks, peers, wide, PB), f32), ((stat_rows, PB), f32), ((users * stride, features), bf16),
+            ((blocks, peers, wide // 2, PB), f32),
+            ((len(early) * stride, features), bf16),
+            ((len(early) * stride, PB), f32),
             ((peers * blocks, PB), jnp.int32),
+            ((peers * blocks, PB), f32),
+            ((blocks, PB), f32),
+            ((8, PB), f32),
         ],
         [
-            pltpu.VMEM((users * stride, PB), f32),
             pltpu.VMEM((length, features), bf16),
-            pltpu.VMEM((peers * blocks, PB), f32),
             pltpu.VMEM((peers * blocks, PB), jnp.int32),
-            pltpu.SemaphoreType.DMA((users,)),
+            pltpu.SemaphoreType.DMA((len(early),)),
             pltpu.SemaphoreType.DMA,
             pltpu.SemaphoreType.DMA,
         ],
-        user.reshape(1), *narrows, target[0], *pieces, unplaced=1 + users,
+        user.reshape(1), *narrows, target[0], *[pieces[q] for q in early], unplaced=1 + len(early),
     )
+    scores, stats, table = call(
+        functools.partial(late_kernel, dims), "late_scores",
+        [
+            ((blocks, peers, wide, PB), f32), ((stat_rows, PB), f32), ((users * stride, features), bf16),
+        ],
+        [pltpu.VMEM((users * stride, PB), f32), pltpu.SemaphoreType.DMA((max(len(late), 1),))],
+        index, *narrows, first_scores, first_table, first_items, label_rows, positives,
+        *[pieces[q] for q in late], unplaced=len(late),
+    )
+    partner_tops = swap(tops, "users", 1)
     all_stats = [stats] + [swap(stats, "seq", q) for q in range(1, peers)]
 
     state_out = ((length, features), f32)
@@ -377,7 +484,7 @@
             ((8, PB), f32),
         ] + [state_out] * (peers - 1),
         [pltpu.VMEM((peers * blocks, PB), f32)] * 2,
-        index, scores, weights, table, *all_stats,
+        index, scores, weights, table, *all_stats, tops, partner_tops,
     )
 
     def meet(ours, theirs):
@@ -385,16 +492,16 @@
         return jnp.where(row < 4, ours + theirs, jnp.maximum(ours, theirs))
 
     from_core = [swap(hiddens[q], "seq", 1) for q in range(2, peers, 2)]
-    partner_word = swap(word, "users", 1)
     (partial,) = call(
         functools.partial(table_kernel, dims), "table_grads", [((users * rows, features), f32)], [],
         index, near, far, *narrows,
     )
-    partial, from_core, partner_word = lax.optimization_barrier((partial, from_core, partner_word))
+    partial, from_core = lax.optimization_barrier((partial, from_core))
 
     hidden_scale = 16384.0 / factor
 
     parts = partial.reshape(users, rows, features)
+    parts = {q: parts[k] for k, q in enumerate(early + late)}
     halved = [slice(0, half), slice(half, features)]
 
     def coded(sums, bound):
@@ -418,7 +525,6 @@
     def with_far(coded):
         return [swap(part, "seq", 2 * k + 2) for k, part in enumerate(coded)]
 
-    word = meet(word, partner_word)
     if pairs == 4:
         pair_bound = bound_of(word)
         sent, hidden_coded = lax.optimization_barrier(
@@ -433,6 +539,7 @@
         four_bound = bound_of(word)
         pair_sum = added(parts[1], (from_line, line_bound))
         sent = [coded(added(parts[6], (from_pair, pair_bound)), four_bound), coded(parts[5], four_bound)]
+        sent, word = lax.optimization_barrier((sent, word))
 
         from_line, from_pair = swap(sent[0], "users", 2), swap(sent[1], "users", 1)
         far_word = swap(word, "users", 4)
@@ -446,14 +553,18 @@
 
         arrived = [swap(sent[0], "users", 4), swap(sent[1], "users", 2), swap(sent[2], "users", 1)]
         hidden_arrived.append(with_far(hidden_coded))
+        last_word = swap(word, "users", 1)
         (own_hidden,) = call(
             functools.partial(hidden_kernel, dims), "own_hidden_grads", [state_out], [],
             index, near, table, pos_grad, target[0], own_core,
         )
-        arrived, own_hidden, hidden_arrived = lax.optimization_barrier((arrived, own_hidden, hidden_arrived))
+        arrived, own_hidden, hidden_arrived, last_word = lax.optimization_barrier(
+            (arrived, own_hidden, hidden_arrived, last_word)
+        )
+        word = meet(word, last_word)
         owned = added(parts[0], *[(part, top) for part in arrived])
     else:
-        mask = 2
+        mask = 1
         while mask < users:
             word = meet(word, swap(word, "users", mask))
             mask *= 2

time: 114 us -> 109 us (0.956)
  waiting for transfers between devices: 53.1 us -> 36.8 us
  starting transfers between devices: 29.1 us -> 36.8 us
  Pallas kernels: 26.4 us -> 28.4 us
    ppermute x30 -> x31, waiting for transfers between devices: 53.1 us -> 36.8 us  [swap(): return lax.ppermute(array, axis, [(i, i ^ mask) for i in range(count)])]
    ppermute x30 -> x31, starting transfers between devices: 29.1 us -> 36.8 us  [swap(): return lax.ppermute(array, axis, [(i, i ^ mask) for i in range(count)])]
    pallas_call x4 -> x5, Pallas kernels: 23.1 us -> 25 us  [call(): pl.pallas_call(kernel, in_specs=[in_smem] + [in_vmem] * placed + [in_hbm]...]
  transfers between devices with their start and end apart: 30 -> 31, of which waited for: 16 -> 14; matrix products, arithmetic and copies ran while one was open for 4% -> 4% of each run, Pallas kernels for 8% -> 14%
where the time goes in v5:
time: 109 us; the launch traced here: 108 us
  starting transfers between devices  36.8 us (34%)
  waiting for transfers between devices  36.8 us (34%)
  Pallas kernels  28.4 us (26%)
  other arithmetic  3.77 us (3%)
  local copies, waits for them, and re-layouts  1.57 us (1%)
    ppermute x31, waiting for transfers between devices, swap(): return lax.ppermute(array, axis, [(i, i ^ mask) for i in range(count)])  36.8 us
    ppermute x31, starting transfers between devices, swap(): return lax.ppermute(array, axis, [(i, i ^ mask) for i in range(count)])  36.8 us
    pallas_call x5, Pallas kernels, call(): pl.pallas_call(kernel, in_specs=[in_smem] + [in_vmem] * placed + [in_hbm]...  25 us
  transfers between devices with their start and end apart: 31, of which 14 were waited for; matrix products, arithmetic and copies ran while one was open for 4% of the time, Pallas kernels for 14%

profile of v5, /device:TPU:0, one launch (start us, length us, event | category | flops | bytes accessed | tf_op | source)
XLA Modules:
  0.0 108.4 jit_solution(12584655202281258314)
XLA Ops:
  0.7 2.0 %states.1.refs_0_.refs_2_ = bf16[1040,512]{1,0:T(8,128)(2,1)S(1)} custom-call(s32[1]{0:T(128)} %bitcast.user, s32[1,1024]{1,0:T(1,128)} %labels_from.1, s32[8,8]{1,0:T(8,128)} %bitcast.31, f32[1024,512]{1,0:T(8,128)} %bitcast.28), custom_call_target="tpu_custom_call" | custom-call | tf_op jit(solution)/shard_map/states/pallas_call | solution.py:384
  2.7 3.0 %collective-permute-start.6 = (bf16[1040,512]{1,0:T(8,128)(2,1)S(1)}, bf16[1040,512]{1,0:T(8,128)(2,1)S(1)}, u32[]{:S(2)}, u32[]{:S(2)}) collective-permute-start(bf16[1040,512]{1,0:T(8,128)(2,1)S(1)} %states.1.refs_0_.refs_2_), channel_id=1, source_target_pairs={{0,16},{8,24},{16,0},{24,8},{1,17},{9,25},{17,1},{25,9},{2,18},{10... | collective-permute-start | bytes 3194888 | tf_op jit(solution)/shard_map/ppermute | solution.py:20
  5.7 0.1 constant_dynamic-slice_fusion
  5.8 0.1 reshape.347
  5.9 0.1 pad.26.clone
  6.0 0.1 maximum_maximum_fusion.refs_5_
  6.2 2.7 %collective-permute-start = (bf16[272,512]{1,0:T(8,128)(2,1)S(1)}, bf16[272,512]{1,0:T(8,128)(2,1)S(1)}, u32[]{:S(2)}, u32[]{:S(2)}) collective-permute-start(bf16[272,512]{1,0:T(8,128)(2,1)S(1)} %maximum_maximum_fusion.refs_5_), channel_id=1, source_target_pairs={{0,4},{1,5},{2,6},{3,7},{4,0},{5,1},{6,2},{7,3},{8,12},{9,13},{10,... | collective-permute-start | bytes 835592 | tf_op jit(solution)/shard_map/ppermute | solution.py:20
  8.8 1.6 %collective-permute-start.1 = (bf16[272,512]{1,0:T(8,128)(2,1)S(1)}, bf16[272,512]{1,0:T(8,128)(2,1)S(1)}, u32[]{:S(2)}, u32[]{:S(2)}) collective-permute-start(bf16[272,512]{1,0:T(8,128)(2,1)S(1)} %maximum_maximum_fusion.refs_5_), channel_id=1, source_target_pairs={{0,2},{1,3},{2,0},{3,1},{4,6},{5,7},{6,4},{7,5},{8,10},{9,11},{10,... | collective-permute-start | bytes 835592 | tf_op jit(solution)/shard_map/ppermute | solution.py:20
  10.4 1.5 %collective-permute-start.2 = (bf16[272,512]{1,0:T(8,128)(2,1)S(1)}, bf16[272,512]{1,0:T(8,128)(2,1)}, u32[]{:S(2)}, u32[]{:S(2)}) collective-permute-start(bf16[272,512]{1,0:T(8,128)(2,1)S(1)} %maximum_maximum_fusion.refs_5_), channel_id=1, source_target_pairs={{0,1},{1,0},{2,3},{3,2},{4,5},{5,4},{6,7},{7,6},{8,9},{9,8},{10,11... | collective-permute-start | bytes 835592 | tf_op jit(solution)/shard_map/ppermute | solution.py:20
  11.9 9.4 %collective-permute-done.refs_8_ = bf16[272,512]{1,0:T(8,128)(2,1)S(1)} collective-permute-done((bf16[272,512]{1,0:T(8,128)(2,1)S(1)}, bf16[272,512]{1,0:T(8,128)(2,1)S(1)}, u32[]{:S(2)}, u32[]{:S(2)}) %collective-permute-start) | collective-permute-done | bytes 278560 | tf_op jit(solution)/shard_map/ppermute | solution.py:20
  21.3 0.2 collective-permute-done.1.refs_7_
  21.5 1.4 %collective-permute-start.3 = (bf16[272,512]{1,0:T(8,128)(2,1)S(1)}, bf16[272,512]{1,0:T(8,128)(2,1)}, u32[]{:S(2)}, u32[]{:S(2)}) collective-permute-start(bf16[272,512]{1,0:T(8,128)(2,1)S(1)} %collective-permute-done.refs_8_), channel_id=1, source_target_pairs={{0,2},{1,3},{2,0},{3,1},{4,6},{5,7},{6,4},{7,5},{8,10},{9,11},{10,... | collective-permute-start | bytes 835592 | tf_op jit(solution)/shard_map/ppermute | solution.py:20
  23.0 1.5 %collective-permute-start.4 = (bf16[272,512]{1,0:T(8,128)(2,1)S(1)}, bf16[272,512]{1,0:T(8,128)(2,1)S(1)}, u32[]{:S(2)}, u32[]{:S(2)}) collective-permute-start(bf16[272,512]{1,0:T(8,128)(2,1)S(1)} %collective-permute-done.refs_8_), channel_id=1, source_target_pairs={{0,1},{1,0},{2,3},{3,2},{4,5},{5,4},{6,7},{7,6},{8,9},{9,8},{10,11... | collective-permute-start | bytes 835592 | tf_op jit(solution)/shard_map/ppermute | solution.py:20
  24.4 4.5 %collective-permute-done.3.refs_10_ = bf16[272,512]{1,0:T(8,128)(2,1)} collective-permute-done((bf16[272,512]{1,0:T(8,128)(2,1)S(1)}, bf16[272,512]{1,0:T(8,128)(2,1)}, u32[]{:S(2)}, u32[]{:S(2)}) %collective-permute-start.3) | collective-permute-done | bytes 278560 | tf_op jit(solution)/shard_map/ppermute | solution.py:20
  29.0 1.3 %collective-permute-done.4.refs_9_ = bf16[272,512]{1,0:T(8,128)(2,1)S(1)} collective-permute-done((bf16[272,512]{1,0:T(8,128)(2,1)S(1)}, bf16[272,512]{1,0:T(8,128)(2,1)S(1)}, u32[]{:S(2)}, u32[]{:S(2)}) %collective-permute-start.4) | collective-permute-done | bytes 278560 | tf_op jit(solution)/shard_map/ppermute | solution.py:20
  30.3 0.7 copy-done.5
  31.0 0.1 slice_bitcast_fusion.1
  31.0 0.1 iota_add_fusion
  31.1 0.4 collective-permute-start.8
  31.5 1.5 %collective-permute-start.9 = (bf16[272,512]{1,0:T(8,128)(2,1)}, bf16[272,512]{1,0:T(8,128)(2,1)}, u32[]{:S(2)}, u32[]{:S(2)}) collective-permute-start(bf16[272,512]{1,0:T(8,128)(2,1)} %collective-permute-done.3.refs_10_), channel_id=1, source_target_pairs={{0,1},{1,0},{2,3},{3,2},{4,5},{5,4},{6,7},{7,6},{8,9},{9,8},{10,11... | collective-permute-start | bytes 835592 | tf_op jit(solution)/shard_map/ppermute | solution.py:20
  33.0 0.1 convert_divide_fusion
  33.1 0.1 select_reduce_fusion
  33.2 1.4 %collective-permute-done.7.refs_3_.refs_5_ = bf16[1040,512]{1,0:T(8,128)(2,1)} collective-permute-done((bf16[1040,512]{1,0:T(8,128)(2,1)S(1)}, bf16[1040,512]{1,0:T(8,128)(2,1)}, u32[]{:S(2)}, u32[]{:S(2)}) %collective-permute-start.7) | collective-permute-done | bytes 1064992 | tf_op jit(solution)/shard_map/ppermute | solution.py:20
  34.6 7.1 %early_scores.1 = (f32[8,4,256,128]{3,2,1,0:T(8,128)S(1)}, bf16[1632,512]{1,0:T(8,128)(2,1)S(1)}, f32[1632,128]{1,0:T(8,128)S(1)}, s32[32,128]{1,0:T(8,128)S(1)}...) custom-call(s32[1]{0:T(128)} %bitcast.user, bf16[1040,512]{1,0:T(8,128)(2,1)S(1)} %states.1.refs_0_.refs_2_, ...), custom_call_target="tpu_custom_call" | custom-call | flops 1048576 | bytes 1048576 | tf_op jit(solution)/shard_map/early_scores/pallas_call | solution.py:434
  41.7 6.5 %late_scores.1 = (f32[8,4,512,128]{3,2,1,0:T(8,128)S(1)}, f32[72,128]{1,0:T(8,128)S(1)}, bf16[2176,512]{1,0:T(8,128)(2,1)S(1)}) custom-call(s32[32,128]{1,0:T(8,128)S(1)} %get-tuple-element.72.index, bf16[1040,512]{1,0:T(8,128)(2,1)S(1)} %states.1.refs_0_.refs_2_, bf16[1040,512]{1,0:T(8,128)(2,1)} %collective-permute-done.5.refs_1_.refs_3_, ...), custom_call_target="tpu_custom_call" | custom-call | flops 1048576 | bytes 1048576 | tf_op jit(solution)/shard_map/late_scores/pallas_call | solution.py:434
  48.2 0.2 collective-permute-start.10
  48.4 0.5 collective-permute-start.11
  48.9 1.2 %collective-permute-start.12 = (f32[72,128]{1,0:T(8,128)S(1)}, f32[72,128]{1,0:T(8,128)S(1)}, u32[]{:S(2)}, u32[]{:S(2)}) collective-permute-start(f32[72,128]{1,0:T(8,128)S(1)} %get-tuple-element.81.refs_3_), channel_id=1, source_target_pairs={{0,24},{8,16},{16,8},{24,0},{1,25},{9,17},{17,9},{25,1},{2,26},{10... | collective-permute-start | bytes 110600 | tf_op jit(solution)/shard_map/ppermute | solution.py:20
  50.1 1.8 %collective-permute-start.13 = (f32[8,128]{1,0:T(8,128)S(1)}, f32[8,128]{1,0:T(8,128)S(1)}, u32[]{:S(2)}, u32[]{:S(2)}) collective-permute-start(f32[8,128]{1,0:T(8,128)S(1)} %get-tuple-element.82.refs_7_), channel_id=1, source_target_pairs={{0,1},{1,0},{2,3},{3,2},{4,5},{5,4},{6,7},{7,6},{8,9},{9,8},{10,11... | collective-permute-start | bytes 12296 | tf_op jit(solution)/shard_map/ppermute | solution.py:20
  51.9 1.8 %collective-permute-done.13.refs_8_ = f32[8,128]{1,0:T(8,128)S(1)} collective-permute-done((f32[8,128]{1,0:T(8,128)S(1)}, f32[8,128]{1,0:T(8,128)S(1)}, u32[]{:S(2)}, u32[]{:S(2)}) %collective-permute-start.13) | collective-permute-done | bytes 4128 | tf_op jit(solution)/shard_map/ppermute | solution.py:20
  53.8 3.0 %grads.1 = (bf16[8,512,128]{2,1,0:T(8,128)(2,1)S(1)}, bf16[8,3,512,128]{3,2,1,0:T(8,128)(2,1)S(1)}, f32[8,128]{1,0:T(8,128)S(1)}, f32[8,128]{1,0:T(8,128)S(1)}, ...) custom-call(s32[32,128]{1,0:T(8,128)S(1)} %get-tuple-element.72.index, ...), custom_call_target="tpu_custom_call" | custom-call | flops 1048576 | bytes 1048576 | tf_op jit(solution)/shard_map/grads/pallas_call | solution.py:434
  56.9 0.5 collective-permute-start.22
  57.4 6.7 %table_grads.1 = f32[2048,512]{1,0:T(8,128)S(1)} custom-call(s32[32,128]{1,0:T(8,128)S(1)} %get-tuple-element.72.index, bf16[8,512,128]{2,1,0:T(8,128)(2,1)S(1)} %get-tuple-element.103.refs_0_.near, bf16[8,3,512,128]{3,2,1,0:T(8,128)(2,1)S(1)} %get-tuple-element.84.refs_1_, bf16[1040,512]{1,0:T(8,128)(2,1)S(1)} %states.1.refs_0_.refs_2_, ...), custom_call_target="tpu_custom_call" | custom-call | flops 1048576 | bytes 1048576 | tf_op jit(solution)/shard_map/table_grads/pallas_call | solution.py:434
  64.1 0.1 multiply_convert_fusion.8
  64.3 0.4 multiply_convert_fusion
  64.6 1.9 %collective-permute-start.15 = (f16[256,512]{1,0:T(8,128)(2,1)S(1)}, f16[256,512]{1,0:T(8,128)(2,1)S(1)}, u32[]{:S(2)}, u32[]{:S(2)}) collective-permute-start(f16[256,512]{1,0:T(8,128)(2,1)S(1)} %get-tuple-element.90), channel_id=1, source_target_pairs={{0,1},{1,0},{2,3},{3,2},{4,5},{5,4},{6,7},{7,6},{8,9},{9,8},{10,11... | collective-permute-start | bytes 786440 | tf_op jit(solution)/shard_map/ppermute | solution.py:20
  66.5 0.2 collective-permute-start.16
  66.7 1.8 %collective-permute-start.17 = (f32[8,128]{1,0:T(8,128)S(1)}, f32[8,128]{1,0:T(8,128)S(1)}, u32[]{:S(2)}, u32[]{:S(2)}) collective-permute-start(f32[8,128]{1,0:T(8,128)S(1)} %get-tuple-element.87), channel_id=1, source_target_pairs={{0,2},{1,3},{2,0},{3,1},{4,6},{5,7},{6,4},{7,5},{8,10},{9,11},{10,... | collective-permute-start | bytes 12296 | tf_op jit(solution)/shard_map/ppermute | solution.py:20
  68.5 0.5 collective-permute-start.21
  69.0 5.6 %collective-permute-done.17 = f32[8,128]{1,0:T(8,128)S(1)} collective-permute-done((f32[8,128]{1,0:T(8,128)S(1)}, f32[8,128]{1,0:T(8,128)S(1)}, u32[]{:S(2)}, u32[]{:S(2)}) %collective-permute-start.17) | collective-permute-done | bytes 4128 | tf_op jit(solution)/shard_map/ppermute | solution.py:20
  74.7 0.2 multiply_convert_fusion.6
  74.9 0.4 collective-permute-start.18
  75.3 0.4 collective-permute-start.19
  75.7 4.6 %collective-permute-start.20 = (f32[8,128]{1,0:T(8,128)S(1)}, f32[8,128]{1,0:T(8,128)S(1)}, u32[]{:S(2)}, u32[]{:S(2)}) collective-permute-start(f32[8,128]{1,0:T(8,128)S(1)} %maximum_select_fusion.2), channel_id=1, source_target_pairs={{0,4},{1,5},{2,6},{3,7},{4,0},{5,1},{6,2},{7,3},{8,12},{9,13},{10,... | collective-permute-start | bytes 12296 | tf_op jit(solution)/shard_map/ppermute | solution.py:20
  80.3 1.7 %collective-permute-done.20 = f32[8,128]{1,0:T(8,128)S(1)} collective-permute-done((f32[8,128]{1,0:T(8,128)S(1)}, f32[8,128]{1,0:T(8,128)S(1)}, u32[]{:S(2)}, u32[]{:S(2)}) %collective-permute-start.20) | collective-permute-done | bytes 4128 | tf_op jit(solution)/shard_map/ppermute | solution.py:20
  82.0 0.1 collective-permute-done.18
  82.1 0.3 collective-permute-done.19
  82.5 0.6 collective-permute-start.26
  83.1 0.3 multiply_convert_fusion.3
  83.4 3.2 %collective-permute-start.23 = (f16[256,512]{1,0:T(8,128)(2,1)S(1)}, f16[256,512]{1,0:T(8,128)(2,1)S(1)}, u32[]{:S(2)}, u32[]{:S(2)}) collective-permute-start(f16[256,512]{1,0:T(8,128)(2,1)S(1)} %get-tuple-element.123), channel_id=1, source_target_pairs={{0,4},{1,5},{2,6},{3,7},{4,0},{5,1},{6,2},{7,3},{8,12},{9,13},{10,... | collective-permute-start | bytes 786440 | tf_op jit(solution)/shard_map/ppermute | solution.py:20
  86.6 1.8 %collective-permute-start.24 = (f16[256,512]{1,0:T(8,128)(2,1)S(1)}, f16[256,512]{1,0:T(8,128)(2,1)S(1)}, u32[]{:S(2)}, u32[]{:S(2)}) collective-permute-start(f16[256,512]{1,0:T(8,128)(2,1)S(1)} %get-tuple-element.122), channel_id=1, source_target_pairs={{0,2},{1,3},{2,0},{3,1},{4,6},{5,7},{6,4},{7,5},{8,10},{9,11},{10,... | collective-permute-start | bytes 786440 | tf_op jit(solution)/shard_map/ppermute | solution.py:20
  88.3 0.5 collective-permute-start.25
  88.8 1.5 %collective-permute-start.27 = (f32[8,128]{1,0:T(8,128)S(1)}, f32[8,128]{1,0:T(8,128)S(1)}, u32[]{:S(2)}, u32[]{:S(2)}) collective-permute-start(f32[8,128]{1,0:T(8,128)S(1)} %maximum_select_fusion.1), channel_id=1, source_target_pairs={{0,1},{1,0},{2,3},{3,2},{4,5},{5,4},{6,7},{7,6},{8,9},{9,8},{10,11... | collective-permute-start | bytes 12296 | tf_op jit(solution)/shard_map/ppermute | solution.py:20
  90.4 1.7 %own_hidden_grads.1 = f32[1024,512]{1,0:T(8,128)S(1)} custom-call(s32[32,128]{1,0:T(8,128)S(1)} %get-tuple-element.72.index, bf16[8,512,128]{2,1,0:T(8,128)(2,1)S(1)} %get-tuple-element.103.refs_0_.near, bf16[2176,512]{1,0:T(8,128)(2,1)S(1)} %get-tuple-element.80.refs_2_.table, f32[8,128]{1,0:T(8,128)S(1)} %get-tuple-element.104.pos_grad, ...), custom_call_target="tpu_custom_call" | custom-call | flops 1048576 | bytes 1048576 | tf_op jit(solution)/shard_map/own_hidden_grads/pallas_call | solution.py:434
  92.0 2.7 %collective-permute-done.27 = f32[8,128]{1,0:T(8,128)S(1)} collective-permute-done((f32[8,128]{1,0:T(8,128)S(1)}, f32[8,128]{1,0:T(8,128)S(1)}, u32[]{:S(2)}, u32[]{:S(2)}) %collective-permute-start.27) | collective-permute-done | bytes 4128 | tf_op jit(solution)/shard_map/ppermute | solution.py:20
  94.7 1.4 %collective-permute-done.23 = f16[256,512]{1,0:T(8,128)(2,1)S(1)} collective-permute-done((f16[256,512]{1,0:T(8,128)(2,1)S(1)}, f16[256,512]{1,0:T(8,128)(2,1)S(1)}, u32[]{:S(2)}, u32[]{:S(2)}) %collective-permute-start.23) | collective-permute-done | bytes 262176 | tf_op jit(solution)/shard_map/ppermute | solution.py:20
  96.1 0.2 multiply_convert_fusion.2
  96.4 1.5 %collective-permute-start.29 = (f16[256,512]{1,0:T(8,128)(2,1)S(1)}, f16[256,512]{1,0:T(8,128)(2,1)S(1)}, u32[]{:S(2)}, u32[]{:S(2)}) collective-permute-start(f16[256,512]{1,0:T(8,128)(2,1)S(1)} %get-tuple-element.119), channel_id=1, source_target_pairs={{0,16},{8,24},{16,0},{24,8},{1,17},{9,25},{17,1},{25,9},{2,18},{10... | collective-permute-start | bytes 786440 | tf_op jit(solution)/shard_map/ppermute | solution.py:20
  98.0 1.7 %multiply_add_fusion = f32[1024,512]{1,0:T(8,128)} fusion(f32[1024,512]{1,0:T(8,128)S(1)} %own_hidden_grads.1, f16[1024,256]{1,0:T(8,128)(2,1)S(1)} %collective-permute-done.26, f16[1024,256]{1,0:T(8,128)(2,1)S(1)} %collective-permute-done.21), kind=kLoop, calls=%fused_computation | loop fusion | flops 2097152 | bytes 5242880 | tf_op jit(solution)/shard_map/add | solution.py:586
  99.7 5.5 %collective-permute-done.29 = f16[256,512]{1,0:T(8,128)(2,1)S(1)} collective-permute-done((f16[256,512]{1,0:T(8,128)(2,1)S(1)}, f16[256,512]{1,0:T(8,128)(2,1)S(1)}, u32[]{:S(2)}, u32[]{:S(2)}) %collective-permute-start.29) | collective-permute-done | bytes 262176 | tf_op jit(solution)/shard_map/ppermute | solution.py:20
  105.2 0.5 slice.84
  105.8 0.9 collective-permute-done.30
  106.7 0.1 convert_multiply_fusion
  106.8 1.4 %ordered_table_grads.1 = f32[1024,512]{1,0:T(8,128)} custom-call(s32[1]{0:T(128)} %bitcast.14.rank, f32[256,512]{1,0:T(8,128)S(1)} %get-tuple-element.116.refs_0_, f32[256,512]{1,0:T(8,128)S(1)} %collective-permute-done.28.refs_1_, f32[256,512]{1,0:T(8,128)S(1)} %get-tuple-element.131.refs_2_, f32[256,512]{1,0:T(8,128)S(1)} %get-tuple-element.130.refs_3_), custom_call_target="tpu_custom_call" | custom-call | tf_op jit(solution)/shard_map/ordered_table_grads/pallas_call | solution.py:594
  (57 shorter events, 0.6 us)
Async XLA Ops:
  0.6 5.4 %copy-start = (bf16[1024,512]{1,0:T(8,128)(2,1)S(1)}, bf16[1024,512]{1,0:T(8,128)(2,1)}, u32[]{:S(2)}) copy-start(bf16[1024,512]{1,0:T(8,128)(2,1)} %param.9) | copy-start | bytes 3145732
  0.6 5.1 %copy-start.6 = (s32[1024]{0:T(1024)S(1)}, s32[1024]{0:T(1024)}, u32[]{:S(2)}) copy-start(s32[1024]{0:T(1024)} %param.10) | copy-start | bytes 12292
  0.7 30.3 %copy-start.7 = (s32[1,5]{1,0:T(1,128)S(1)}, s32[1,5]{1,0:T(1,128)}, u32[]{:S(2)}) copy-start(s32[1,5]{1,0:T(1,128)} %param.13) | copy-start | bytes 64
  2.7 27.6 %collective-permute-start.6 = (bf16[1040,512]{1,0:T(8,128)(2,1)S(1)}, bf16[1040,512]{1,0:T(8,128)(2,1)S(1)}, u32[]{:S(2)}, u32[]{:S(2)}) collective-permute-start(bf16[1040,512]{1,0:T(8,128)(2,1)S(1)} %states.1.refs_0_.refs_2_), channel_id=1, source_target_pairs={{0,16},{8,24},{16,0},{24,8},{1,17},{9,25},{17,1},{25,9},{2,18},{10... | collective-permute-start | bytes 3194888 | tf_op jit(solution)/shard_map/ppermute | solution.py:20
  6.2 28.5 %copy-start.2 = (bf16[272,512]{1,0:T(8,128)(2,1)}, bf16[272,512]{1,0:T(8,128)(2,1)S(1)}, u32[]{:S(2)}) copy-start(bf16[272,512]{1,0:T(8,128)(2,1)S(1)} %maximum_maximum_fusion.refs_5_) | copy-start | bytes 835588
  6.2 15.2 %collective-permute-start = (bf16[272,512]{1,0:T(8,128)(2,1)S(1)}, bf16[272,512]{1,0:T(8,128)(2,1)S(1)}, u32[]{:S(2)}, u32[]{:S(2)}) collective-permute-start(bf16[272,512]{1,0:T(8,128)(2,1)S(1)} %maximum_maximum_fusion.refs_5_), channel_id=1, source_target_pairs={{0,4},{1,5},{2,6},{3,7},{4,0},{5,1},{6,2},{7,3},{8,12},{9,13},{10,... | collective-permute-start | bytes 835592 | tf_op jit(solution)/shard_map/ppermute | solution.py:20
  8.8 12.7 %collective-permute-start.1 = (bf16[272,512]{1,0:T(8,128)(2,1)S(1)}, bf16[272,512]{1,0:T(8,128)(2,1)S(1)}, u32[]{:S(2)}, u32[]{:S(2)}) collective-permute-start(bf16[272,512]{1,0:T(8,128)(2,1)S(1)} %maximum_maximum_fusion.refs_5_), channel_id=1, source_target_pairs={{0,2},{1,3},{2,0},{3,1},{4,6},{5,7},{6,4},{7,5},{8,10},{9,11},{10,... | collective-permute-start | bytes 835592 | tf_op jit(solution)/shard_map/ppermute | solution.py:20
  10.4 11.1 %collective-permute-start.2 = (bf16[272,512]{1,0:T(8,128)(2,1)S(1)}, bf16[272,512]{1,0:T(8,128)(2,1)}, u32[]{:S(2)}, u32[]{:S(2)}) collective-permute-start(bf16[272,512]{1,0:T(8,128)(2,1)S(1)} %maximum_maximum_fusion.refs_5_), channel_id=1, source_target_pairs={{0,1},{1,0},{2,3},{3,2},{4,5},{5,4},{6,7},{7,6},{8,9},{9,8},{10,11... | collective-permute-start | bytes 835592 | tf_op jit(solution)/shard_map/ppermute | solution.py:20
  21.3 9.0 %copy-start.3 = (bf16[272,512]{1,0:T(8,128)(2,1)}, bf16[272,512]{1,0:T(8,128)(2,1)S(1)}, u32[]{:S(2)}) copy-start(bf16[272,512]{1,0:T(8,128)(2,1)S(1)} %collective-permute-done.refs_8_) | copy-start | bytes 835588
  21.5 8.8 %copy-start.4 = (bf16[272,512]{1,0:T(8,128)(2,1)}, bf16[272,512]{1,0:T(8,128)(2,1)S(1)}, u32[]{:S(2)}) copy-start(bf16[272,512]{1,0:T(8,128)(2,1)S(1)} %collective-permute-done.1.refs_7_) | copy-start | bytes 835588
  21.5 7.4 %collective-permute-start.3 = (bf16[272,512]{1,0:T(8,128)(2,1)S(1)}, bf16[272,512]{1,0:T(8,128)(2,1)}, u32[]{:S(2)}, u32[]{:S(2)}) collective-permute-start(bf16[272,512]{1,0:T(8,128)(2,1)S(1)} %collective-permute-done.refs_8_), channel_id=1, source_target_pairs={{0,2},{1,3},{2,0},{3,1},{4,6},{5,7},{6,4},{7,5},{8,10},{9,11},{10,... | collective-permute-start | bytes 835592 | tf_op jit(solution)/shard_map/ppermute | solution.py:20
  23.0 7.3 %collective-permute-start.4 = (bf16[272,512]{1,0:T(8,128)(2,1)S(1)}, bf16[272,512]{1,0:T(8,128)(2,1)S(1)}, u32[]{:S(2)}, u32[]{:S(2)}) collective-permute-start(bf16[272,512]{1,0:T(8,128)(2,1)S(1)} %collective-permute-done.refs_8_), channel_id=1, source_target_pairs={{0,1},{1,0},{2,3},{3,2},{4,5},{5,4},{6,7},{7,6},{8,9},{9,8},{10,11... | collective-permute-start | bytes 835592 | tf_op jit(solution)/shard_map/ppermute | solution.py:20
  30.3 0.7 copy-start.5
  30.3 3.0 %collective-permute-start.5 = (bf16[1040,512]{1,0:T(8,128)(2,1)S(1)}, bf16[1040,512]{1,0:T(8,128)(2,1)}, u32[]{:S(2)}, u32[]{:S(2)}) collective-permute-start(bf16[1040,512]{1,0:T(8,128)(2,1)S(1)} %states.1.refs_0_.refs_2_), channel_id=1, source_target_pairs={{0,8},{8,0},{16,24},{24,16},{1,9},{9,1},{17,25},{25,17},{2,10},{10... | collective-permute-start | bytes 3194888 | tf_op jit(solution)/shard_map/ppermute | solution.py:20
  31.0 3.6 %collective-permute-start.7 = (bf16[1040,512]{1,0:T(8,128)(2,1)S(1)}, bf16[1040,512]{1,0:T(8,128)(2,1)}, u32[]{:S(2)}, u32[]{:S(2)}) collective-permute-start(bf16[1040,512]{1,0:T(8,128)(2,1)S(1)} %collective-permute-done.6.refs_2_.refs_4_), channel_id=1, source_target_pairs={{0,8},{8,0},{16,24},{24,16},{1,9},{9,1},{17,25},{25,17},{2,10},{10... | collective-permute-start | bytes 3194888 | tf_op jit(solution)/shard_map/ppermute | solution.py:20
  31.1 10.6 %collective-permute-start.8 = (bf16[272,512]{1,0:T(8,128)(2,1)}, bf16[272,512]{1,0:T(8,128)(2,1)}, u32[]{:S(2)}, u32[]{:S(2)}) collective-permute-start(bf16[272,512]{1,0:T(8,128)(2,1)} %collective-permute-done.2.refs_6_), channel_id=1, source_target_pairs={{0,2},{1,3},{2,0},{3,1},{4,6},{5,7},{6,4},{7,5},{8,10},{9,11},{10,... | collective-permute-start | bytes 835592 | tf_op jit(solution)/shard_map/ppermute | solution.py:20
  31.5 10.2 %collective-permute-start.9 = (bf16[272,512]{1,0:T(8,128)(2,1)}, bf16[272,512]{1,0:T(8,128)(2,1)}, u32[]{:S(2)}, u32[]{:S(2)}) collective-permute-start(bf16[272,512]{1,0:T(8,128)(2,1)} %collective-permute-done.3.refs_10_), channel_id=1, source_target_pairs={{0,1},{1,0},{2,3},{3,2},{4,5},{5,4},{6,7},{7,6},{8,9},{9,8},{10,11... | collective-permute-start | bytes 835592 | tf_op jit(solution)/shard_map/ppermute | solution.py:20
  48.2 5.5 %collective-permute-start.10 = (f32[72,128]{1,0:T(8,128)S(1)}, f32[72,128]{1,0:T(8,128)S(1)}, u32[]{:S(2)}, u32[]{:S(2)}) collective-permute-start(f32[72,128]{1,0:T(8,128)S(1)} %get-tuple-element.81.refs_3_), channel_id=1, source_target_pairs={{0,8},{8,0},{16,24},{24,16},{1,9},{9,1},{17,25},{25,17},{2,10},{10... | collective-permute-start | bytes 110600 | tf_op jit(solution)/shard_map/ppermute | solution.py:20
  48.4 5.4 %collective-permute-start.11 = (f32[72,128]{1,0:T(8,128)S(1)}, f32[72,128]{1,0:T(8,128)S(1)}, u32[]{:S(2)}, u32[]{:S(2)}) collective-permute-start(f32[72,128]{1,0:T(8,128)S(1)} %get-tuple-element.81.refs_3_), channel_id=1, source_target_pairs={{0,16},{8,24},{16,0},{24,8},{1,17},{9,25},{17,1},{25,9},{2,18},{10... | collective-permute-start | bytes 110600 | tf_op jit(solution)/shard_map/ppermute | solution.py:20
  48.9 4.8 %collective-permute-start.12 = (f32[72,128]{1,0:T(8,128)S(1)}, f32[72,128]{1,0:T(8,128)S(1)}, u32[]{:S(2)}, u32[]{:S(2)}) collective-permute-start(f32[72,128]{1,0:T(8,128)S(1)} %get-tuple-element.81.refs_3_), channel_id=1, source_target_pairs={{0,24},{8,16},{16,8},{24,0},{1,25},{9,17},{17,9},{25,1},{2,26},{10... | collective-permute-start | bytes 110600 | tf_op jit(solution)/shard_map/ppermute | solution.py:20
  50.1 3.6 %collective-permute-start.13 = (f32[8,128]{1,0:T(8,128)S(1)}, f32[8,128]{1,0:T(8,128)S(1)}, u32[]{:S(2)}, u32[]{:S(2)}) collective-permute-start(f32[8,128]{1,0:T(8,128)S(1)} %get-tuple-element.82.refs_7_), channel_id=1, source_target_pairs={{0,1},{1,0},{2,3},{3,2},{4,5},{5,4},{6,7},{7,6},{8,9},{9,8},{10,11... | collective-permute-start | bytes 12296 | tf_op jit(solution)/shard_map/ppermute | solution.py:20
  56.8 7.3 %collective-permute-start.14 = (f32[1024,512]{1,0:T(8,128)S(1)}, f32[1024,512]{1,0:T(8,128)S(1)}, u32[]{:S(2)}, u32[]{:S(2)}) collective-permute-start(f32[1024,512]{1,0:T(8,128)S(1)} %get-tuple-element.85), channel_id=1, source_target_pairs={{0,8},{8,0},{16,24},{24,16},{1,9},{9,1},{17,25},{25,17},{2,10},{10... | collective-permute-start | bytes 6291464 | tf_op jit(solution)/shard_map/ppermute | solution.py:20
  56.9 23.4 %collective-permute-start.22 = (f32[1024,512]{1,0:T(8,128)S(1)}, f32[1024,512]{1,0:T(8,128)S(1)}, u32[]{:S(2)}, u32[]{:S(2)}) collective-permute-start(f32[1024,512]{1,0:T(8,128)S(1)} %get-tuple-element.98), channel_id=1, source_target_pairs={{0,8},{8,0},{16,24},{24,16},{1,9},{9,1},{17,25},{25,17},{2,10},{10... | collective-permute-start | bytes 6291464 | tf_op jit(solution)/shard_map/ppermute | solution.py:20
  64.6 10.0 %collective-permute-start.15 = (f16[256,512]{1,0:T(8,128)(2,1)S(1)}, f16[256,512]{1,0:T(8,128)(2,1)S(1)}, u32[]{:S(2)}, u32[]{:S(2)}) collective-permute-start(f16[256,512]{1,0:T(8,128)(2,1)S(1)} %get-tuple-element.90), channel_id=1, source_target_pairs={{0,1},{1,0},{2,3},{3,2},{4,5},{5,4},{6,7},{7,6},{8,9},{9,8},{10,11... | collective-permute-start | bytes 786440 | tf_op jit(solution)/shard_map/ppermute | solution.py:20
  66.5 8.1 %collective-permute-start.16 = (f16[256,512]{1,0:T(8,128)(2,1)S(1)}, f16[256,512]{1,0:T(8,128)(2,1)S(1)}, u32[]{:S(2)}, u32[]{:S(2)}) collective-permute-start(f16[256,512]{1,0:T(8,128)(2,1)S(1)} %get-tuple-element.91), channel_id=1, source_target_pairs={{0,2},{1,3},{2,0},{3,1},{4,6},{5,7},{6,4},{7,5},{8,10},{9,11},{10,... | collective-permute-start | bytes 786440 | tf_op jit(solution)/shard_map/ppermute | solution.py:20
  66.7 7.9 %collective-permute-start.17 = (f32[8,128]{1,0:T(8,128)S(1)}, f32[8,128]{1,0:T(8,128)S(1)}, u32[]{:S(2)}, u32[]{:S(2)}) collective-permute-start(f32[8,128]{1,0:T(8,128)S(1)} %get-tuple-element.87), channel_id=1, source_target_pairs={{0,2},{1,3},{2,0},{3,1},{4,6},{5,7},{6,4},{7,5},{8,10},{9,11},{10,... | collective-permute-start | bytes 12296 | tf_op jit(solution)/shard_map/ppermute | solution.py:20
  68.5 13.4 %collective-permute-start.21 = (f16[1024,256]{1,0:T(8,128)(2,1)S(1)}, f16[1024,256]{1,0:T(8,128)(2,1)S(1)}, u32[]{:S(2)}, u32[]{:S(2)}) collective-permute-start(f16[1024,256]{1,0:T(8,128)(2,1)S(1)} %get-tuple-element.97), channel_id=1, source_target_pairs={{0,16},{8,24},{16,0},{24,8},{1,17},{9,25},{17,1},{25,9},{2,18},{10... | collective-permute-start | bytes 1572872 | tf_op jit(solution)/shard_map/ppermute | solution.py:20
  74.7 15.7 %copy-start.1 = (bf16[1,1024,512]{2,1,0:T(8,128)(2,1)S(1)}, bf16[1,1024,512]{2,1,0:T(8,128)(2,1)}, u32[]{:S(2)}) copy-start(bf16[1,1024,512]{2,1,0:T(8,128)(2,1)} %param.8) | copy-start | bytes 3145732
  74.9 7.2 %collective-permute-start.18 = (f16[256,512]{1,0:T(8,128)(2,1)S(1)}, f16[256,512]{1,0:T(8,128)(2,1)S(1)}, u32[]{:S(2)}, u32[]{:S(2)}) collective-permute-start(f16[256,512]{1,0:T(8,128)(2,1)S(1)} %get-tuple-element.95), channel_id=1, source_target_pairs={{0,1},{1,0},{2,3},{3,2},{4,5},{5,4},{6,7},{7,6},{8,9},{9,8},{10,11... | collective-permute-start | bytes 786440 | tf_op jit(solution)/shard_map/ppermute | solution.py:20
  75.3 7.1 %collective-permute-start.19 = (f16[256,512]{1,0:T(8,128)(2,1)S(1)}, f16[256,512]{1,0:T(8,128)(2,1)S(1)}, u32[]{:S(2)}, u32[]{:S(2)}) collective-permute-start(f16[256,512]{1,0:T(8,128)(2,1)S(1)} %get-tuple-element.96), channel_id=1, source_target_pairs={{0,2},{1,3},{2,0},{3,1},{4,6},{5,7},{6,4},{7,5},{8,10},{9,11},{10,... | collective-permute-start | bytes 786440 | tf_op jit(solution)/shard_map/ppermute | solution.py:20
  75.7 6.3 %collective-permute-start.20 = (f32[8,128]{1,0:T(8,128)S(1)}, f32[8,128]{1,0:T(8,128)S(1)}, u32[]{:S(2)}, u32[]{:S(2)}) collective-permute-start(f32[8,128]{1,0:T(8,128)S(1)} %maximum_select_fusion.2), channel_id=1, source_target_pairs={{0,4},{1,5},{2,6},{3,7},{4,0},{5,1},{6,2},{7,3},{8,12},{9,13},{10,... | collective-permute-start | bytes 12296 | tf_op jit(solution)/shard_map/ppermute | solution.py:20
  82.5 13.6 %collective-permute-start.26 = (f16[1024,256]{1,0:T(8,128)(2,1)S(1)}, f16[1024,256]{1,0:T(8,128)(2,1)S(1)}, u32[]{:S(2)}, u32[]{:S(2)}) collective-permute-start(f16[1024,256]{1,0:T(8,128)(2,1)S(1)} %get-tuple-element.107), channel_id=1, source_target_pairs={{0,16},{8,24},{16,0},{24,8},{1,17},{9,25},{17,1},{25,9},{2,18},{10... | collective-permute-start | bytes 1572872 | tf_op jit(solution)/shard_map/ppermute | solution.py:20
  83.4 12.7 %collective-permute-start.23 = (f16[256,512]{1,0:T(8,128)(2,1)S(1)}, f16[256,512]{1,0:T(8,128)(2,1)S(1)}, u32[]{:S(2)}, u32[]{:S(2)}) collective-permute-start(f16[256,512]{1,0:T(8,128)(2,1)S(1)} %get-tuple-element.123), channel_id=1, source_target_pairs={{0,4},{1,5},{2,6},{3,7},{4,0},{5,1},{6,2},{7,3},{8,12},{9,13},{10,... | collective-permute-start | bytes 786440 | tf_op jit(solution)/shard_map/ppermute | solution.py:20
  86.6 9.6 %collective-permute-start.24 = (f16[256,512]{1,0:T(8,128)(2,1)S(1)}, f16[256,512]{1,0:T(8,128)(2,1)S(1)}, u32[]{:S(2)}, u32[]{:S(2)}) collective-permute-start(f16[256,512]{1,0:T(8,128)(2,1)S(1)} %get-tuple-element.122), channel_id=1, source_target_pairs={{0,2},{1,3},{2,0},{3,1},{4,6},{5,7},{6,4},{7,5},{8,10},{9,11},{10,... | collective-permute-start | bytes 786440 | tf_op jit(solution)/shard_map/ppermute | solution.py:20
  88.3 7.8 %collective-permute-start.25 = (f16[256,512]{1,0:T(8,128)(2,1)S(1)}, f16[256,512]{1,0:T(8,128)(2,1)S(1)}, u32[]{:S(2)}, u32[]{:S(2)}) collective-permute-start(f16[256,512]{1,0:T(8,128)(2,1)S(1)} %get-tuple-element.121), channel_id=1, source_target_pairs={{0,1},{1,0},{2,3},{3,2},{4,5},{5,4},{6,7},{7,6},{8,9},{9,8},{10,11... | collective-permute-start | bytes 786440 | tf_op jit(solution)/shard_map/ppermute | solution.py:20
  88.8 5.9 %collective-permute-start.27 = (f32[8,128]{1,0:T(8,128)S(1)}, f32[8,128]{1,0:T(8,128)S(1)}, u32[]{:S(2)}, u32[]{:S(2)}) collective-permute-start(f32[8,128]{1,0:T(8,128)S(1)} %maximum_select_fusion.1), channel_id=1, source_target_pairs={{0,1},{1,0},{2,3},{3,2},{4,5},{5,4},{6,7},{7,6},{8,9},{9,8},{10,11... | collective-permute-start | bytes 12296 | tf_op jit(solution)/shard_map/ppermute | solution.py:20
  96.4 8.8 %collective-permute-start.28 = (f32[256,512]{1,0:T(8,128)S(1)}, f32[256,512]{1,0:T(8,128)S(1)}, u32[]{:S(2)}, u32[]{:S(2)}) collective-permute-start(f32[256,512]{1,0:T(8,128)S(1)} %get-tuple-element.116.refs_0_), channel_id=1, source_target_pairs={{0,8},{8,0},{16,24},{24,16},{1,9},{9,1},{17,25},{25,17},{2,10},{10... | collective-permute-start | bytes 1572872 | tf_op jit(solution)/shard_map/ppermute | solution.py:20
  96.4 8.7 %collective-permute-start.29 = (f16[256,512]{1,0:T(8,128)(2,1)S(1)}, f16[256,512]{1,0:T(8,128)(2,1)S(1)}, u32[]{:S(2)}, u32[]{:S(2)}) collective-permute-start(f16[256,512]{1,0:T(8,128)(2,1)S(1)} %get-tuple-element.119), channel_id=1, source_target_pairs={{0,16},{8,24},{16,0},{24,8},{1,17},{9,25},{17,1},{25,9},{2,18},{10... | collective-permute-start | bytes 786440 | tf_op jit(solution)/shard_map/ppermute | solution.py:20
  105.2 1.5 %collective-permute-start.30 = (f16[256,512]{1,0:T(8,128)(2,1)S(1)}, f16[256,512]{1,0:T(8,128)(2,1)S(1)}, u32[]{:S(2)}, u32[]{:S(2)}) collective-permute-start(f16[256,512]{1,0:T(8,128)(2,1)S(1)} %collective-permute-done.29), channel_id=1, source_target_pairs={{0,8},{8,0},{16,24},{24,16},{1,9},{9,1},{17,25},{25,17},{2,10},{10... | collective-permute-start | bytes 786440 | tf_op jit(solution)/shard_map/ppermute | solution.py:20
